TPU v7x, 32 devices: a whole 2x2x4 slice. The times are simulated.
32 devices in a mesh: row: 4 (over z), col: 8 (over y, x, core).
Axes of the slice: x: 2, y: 2, z: 4, core: 2. Of those that a mesh axis runs over, the one named last changes fastest.
Arguments:
- factor_tiles: bfloat16 [3, 48, 64, 512], P(None, 'row', None, 'col'), may hold values from -0.3125 to 0.3125
- tile_row: int32 [3, 48, 8], P(None, 'row', 'col'), may hold values from 0 to 15
- tile_col: int32 [3, 48, 8], P(None, 'row', 'col'), may hold values from 0 to 7
- right_sides: float32 [4, 64, 64, 128], P(None, ('col', 'row')), may hold values from -6 to 6
- diag_inverse: float32 [4, 64, 4096], P(None, None, ('col', 'row')), as said below
Outputs:
- preconditioned: float32 [4, 64, 64, 128], P(None, ('col', 'row'))
Inputs may be any that keep to these rules, and one draw needn't show every extreme that they name: `tile_row`: a block row within its row group. `tile_col`: a block column within its column group. `diag_inverse`: diagonal entries of every block between 0.5 and 2.
All inputs are finite; a program needn't handle non-finite values.
Results may differ from a plain program's by a relative error of at most 0.025.
Values may be sent and summed in bfloat16 or wider, within the bound.
No kernel may reach another device: no remote copies, remote signals or barrier semaphores. Data moves between devices by JAX's collectives and lax.ppermute only.
A program may use at most 64 MiB of HBM per device.

v0:
```python
import jax
import jax.numpy as jnp
from jax import lax
from jax.sharding import PartitionSpec as P


def apply_inverse(inverse, vector, transposed):
    matrix = inverse.reshape(inverse.shape[0], -1, inverse.shape[0])
    if transposed:
        return jnp.einsum("cir,irn->icn", matrix, vector, precision=lax.Precision.HIGHEST)
    return jnp.einsum("cir,icn->irn", matrix, vector, precision=lax.Precision.HIGHEST)


def solve_all(factor_tiles, tile_row, tile_col, right_sides, diag_inverse):
    levels = factor_tiles.shape[0]
    rows_dev = right_sides.shape[1]
    group_rows = rows_dev * lax.axis_size("row")
    row_ids = tile_row[:, :, 0]
    col_ids = tile_col[:, :, 0]
    current = apply_inverse(diag_inverse[0], right_sides[0], False)
    solved = [current]
    for section_no in range(1, levels + 1):
        gathered = lax.all_gather(current.astype(jnp.bfloat16), "row", axis=0, tiled=True)
        picked = gathered[col_ids[section_no - 1]]
        products = jnp.einsum(
            "tab,tbn->tan", factor_tiles[section_no - 1], picked, preferred_element_type=jnp.float32
        )
        targets = row_ids[section_no - 1]

        def term(offset, length, products=products, targets=targets):
            places = jnp.arange(length, dtype=jnp.int32)
            select = (targets[:, None] == places[None, :]).astype(jnp.float32)
            return jnp.einsum("tq,tan->qan", select, products, precision=lax.Precision.HIGHEST)

        row_sums = lax.psum_scatter(
            term(jnp.int32(0), lax.axis_size("col") * rows_dev).astype(jnp.bfloat16),
            "col",
            scatter_dimension=0,
            tiled=True,
        ).astype(jnp.float32)
        current = apply_inverse(diag_inverse[section_no], right_sides[section_no] - row_sums, False)
        solved.append(current)
    current = apply_inverse(diag_inverse[levels], solved[levels], True)
    result = [current]
    columns_here = jnp.arange(group_rows, dtype=jnp.int32)
    for section_no in range(levels - 1, -1, -1):
        everyone = lax.all_gather(current.astype(jnp.bfloat16), "col", axis=0, tiled=True)
        picked = everyone[row_ids[section_no]]
        spread = jnp.einsum(
            "tab,tan->tbn", factor_tiles[section_no], picked, preferred_element_type=jnp.float32
        )
        select = (col_ids[section_no][:, None] == columns_here[None, :]).astype(jnp.float32)
        column_sums = jnp.einsum("tj,tbn->jbn", select, spread, precision=lax.Precision.HIGHEST)
        received = lax.psum_scatter(
            column_sums.astype(jnp.bfloat16), "row", scatter_dimension=0, tiled=True
        ).astype(jnp.float32)
        current = apply_inverse(diag_inverse[section_no], solved[section_no] - received, True)
        result.insert(0, current)
    return jnp.stack(result)


def on_device(factor_tiles, tile_row, tile_col, right_sides, diag_inverse):
    return solve_all(factor_tiles, tile_row, tile_col, right_sides, diag_inverse)


def solution(mesh):
    return jax.shard_map(
        on_device,
        mesh=mesh,
        in_specs=(
            P(None, "row", None, "col"),
            P(None, "row", "col"),
            P(None, "row", "col"),
            P(None, ("col", "row"), None, None),
            P(None, None, ("col", "row")),
        ),
        out_specs=P(None, ("col", "row"), None, None),
        check_vma=False,
    )
```

profile of v0, /device:TPU:0, one launch (start us, length us, event | category | flops | bytes accessed | tf_op | source)
XLA Modules:
  0.0 260.9 jit_solution(13873485134685438498)
XLA Ops:
  6.5 0.9 fusion.66
  7.7 15.1 %all_gather.18 = bf16[8,64,128]{2,1,0:T(8,128)(2,1)S(1)} all-gather(bf16[2,64,128]{2,1,0:T(8,128)(2,1)S(1)} %get-tuple-element.21), channel_id=1, replica_groups=mesh['row'=4,'col'=8] {'row'}, dimensions={0}, use_global_device_ids=true | all-gather | bytes 163840 | tf_op jit(solution)/shard_map/all_gather | solution.py:23
  23.5 0.7 slice_bitcast_fusion
  25.6 0.8 copy.47
  26.5 35.0 %reduce-scatter.7.cloned.1.call-done = bf16[2,64,128]{2,1,0:T(8,128)(2,1)} async-done(((bf16[16,64,128]{2,1,0:T(8,128)(2,1)}), bf16[2,64,128]{2,1,0:T(8,128)(2,1)}) %reduce-scatter.7.cloned.1.call-update) | async-done | bytes 32784 | tf_op jit(solution)/shard_map/reduce_scatter | solution.py:35
  61.5 1.0 fusion.68
  62.5 13.5 %all_gather.19 = bf16[8,64,128]{2,1,0:T(8,128)(2,1)S(1)} all-gather(bf16[2,64,128]{2,1,0:T(8,128)(2,1)S(1)} %get-tuple-element.23), channel_id=1, replica_groups=mesh['row'=4,'col'=8] {'row'}, dimensions={0}, use_global_device_ids=true | all-gather | bytes 163840 | tf_op jit(solution)/shard_map/all_gather | solution.py:23
  77.3 0.8 copy.50
  78.3 33.5 %reduce-scatter.9.cloned.1.call-done = bf16[2,64,128]{2,1,0:T(8,128)(2,1)} async-done(((bf16[16,64,128]{2,1,0:T(8,128)(2,1)}), bf16[2,64,128]{2,1,0:T(8,128)(2,1)}) %reduce-scatter.9.cloned.1.call-update) | async-done | bytes 32784 | tf_op jit(solution)/shard_map/reduce_scatter | solution.py:35
  111.8 1.0 fusion.69
  112.8 13.5 %all_gather.20 = bf16[8,64,128]{2,1,0:T(8,128)(2,1)S(1)} all-gather(bf16[2,64,128]{2,1,0:T(8,128)(2,1)S(1)} %get-tuple-element.25), channel_id=1, replica_groups=mesh['row'=4,'col'=8] {'row'}, dimensions={0}, use_global_device_ids=true | all-gather | bytes 163840 | tf_op jit(solution)/shard_map/all_gather | solution.py:23
  127.7 0.8 copy.53
  129.9 32.3 %reduce-scatter.11.cloned.1.call-done = bf16[2,64,128]{2,1,0:T(8,128)(2,1)} async-done(((bf16[16,64,128]{2,1,0:T(8,128)(2,1)}), bf16[2,64,128]{2,1,0:T(8,128)(2,1)}) %reduce-scatter.11.cloned.1.call-update) | async-done | bytes 32784 | tf_op jit(solution)/shard_map/reduce_scatter | solution.py:35
  162.2 1.0 fusion.21
  163.5 9.3 %all_gather.21 = bf16[16,64,128]{2,1,0:T(8,128)(2,1)S(1)} all-gather(bf16[2,64,128]{2,1,0:T(8,128)(2,1)S(1)} %get-tuple-element.27), channel_id=1, replica_groups=mesh['row'=4,'col'=8] {'col'}, dimensions={0}, use_global_device_ids=true | all-gather | bytes 294912 | tf_op jit(solution)/shard_map/all_gather | solution.py:47
  174.9 19.3 %reduce-scatter.13.cloned.1.call-done = bf16[2,64,128]{2,1,0:T(8,128)(2,1)} async-done(((bf16[8,64,128]{2,1,0:T(8,128)(2,1)}), bf16[2,64,128]{2,1,0:T(8,128)(2,1)}) %reduce-scatter.13.cloned.1.call-update) | async-done | bytes 32784 | tf_op jit(solution)/shard_map/reduce_scatter | solution.py:54
  194.1 1.0 bitcast_convert_fusion.1
  195.2 9.3 %all_gather.22 = bf16[16,64,128]{2,1,0:T(8,128)(2,1)S(1)} all-gather(bf16[2,64,128]{2,1,0:T(8,128)(2,1)S(1)} %get-tuple-element.29), channel_id=1, replica_groups=mesh['row'=4,'col'=8] {'col'}, dimensions={0}, use_global_device_ids=true | all-gather | bytes 294912 | tf_op jit(solution)/shard_map/all_gather | solution.py:47
  206.6 16.6 %reduce-scatter.15.cloned.1.call-done = bf16[2,64,128]{2,1,0:T(8,128)(2,1)} async-done(((bf16[8,64,128]{2,1,0:T(8,128)(2,1)}), bf16[2,64,128]{2,1,0:T(8,128)(2,1)}) %reduce-scatter.15.cloned.1.call-update) | async-done | bytes 32784 | tf_op jit(solution)/shard_map/reduce_scatter | solution.py:54
  223.2 1.0 bitcast_convert_fusion
  224.2 9.3 %all_gather.23 = bf16[16,64,128]{2,1,0:T(8,128)(2,1)S(1)} all-gather(bf16[2,64,128]{2,1,0:T(8,128)(2,1)S(1)} %get-tuple-element.31), channel_id=1, replica_groups=mesh['row'=4,'col'=8] {'col'}, dimensions={0}, use_global_device_ids=true | all-gather | bytes 294912 | tf_op jit(solution)/shard_map/all_gather | solution.py:47
  235.6 16.7 %reduce-scatter.17.cloned.1.call-done = bf16[2,64,128]{2,1,0:T(8,128)(2,1)} async-done(((bf16[8,64,128]{2,1,0:T(8,128)(2,1)}), bf16[2,64,128]{2,1,0:T(8,128)(2,1)}) %reduce-scatter.17.cloned.1.call-update) | async-done | bytes 32784 | tf_op jit(solution)/shard_map/reduce_scatter | solution.py:54
  252.3 1.0 convolution_bitcast_fusion.6
  253.3 0.7 pad_maximum_fusion
  (56 shorter events, 13.3 us)
Async XLA Ops:
  6.5 1.0 copy-start.1
  6.5 18.3 %copy-start = (bf16[3,12,64,64]{3,2,1,0:T(8,128)(2,1)S(1)}, bf16[3,12,64,64]{3,2,1,0:T(8,128)(2,1)}, u32[]{:S(2)}) copy-start(bf16[3,12,64,64]{3,2,1,0:T(8,128)(2,1)} %param.5) | copy-start | bytes 884740
  6.5 55.0 %reduce-scatter.7.cloned.1.call-start = ((), (), s32[]{:S(2)}) async-start(), calls=%async_computation.6 | async-start | bytes 294912 | tf_op jit(solution)/shard_map/reduce_scatter | solution.py:35
  26.4 85.4 %reduce-scatter.9.cloned.1.call-start = ((), (), s32[]{:S(2)}) async-start(), calls=%async_computation.7 | async-start | bytes 294912 | tf_op jit(solution)/shard_map/reduce_scatter | solution.py:35
  78.1 84.1 %reduce-scatter.11.cloned.1.call-start = ((), (), s32[]{:S(2)}) async-start(), calls=%async_computation.8 | async-start | bytes 294912 | tf_op jit(solution)/shard_map/reduce_scatter | solution.py:35
  128.5 0.7 copy-start.2
  128.5 65.6 %reduce-scatter.13.cloned.1.call-start = ((), (), s32[]{:S(2)}) async-start(), calls=%async_computation.9 | async-start | bytes 163840 | tf_op jit(solution)/shard_map/reduce_scatter | solution.py:54
  129.3 0.7 copy-start.3
  174.8 48.4 %reduce-scatter.15.cloned.1.call-start = ((), (), s32[]{:S(2)}) async-start(), calls=%async_computation.10 | async-start | bytes 163840 | tf_op jit(solution)/shard_map/reduce_scatter | solution.py:54
  206.5 45.7 %reduce-scatter.17.cloned.1.call-start = ((), (), s32[]{:S(2)}) async-start(), calls=%async_computation.11 | async-start | bytes 163840 | tf_op jit(solution)/shard_map/reduce_scatter | solution.py:54
Sparse Core Ops, SparseCore 0:
  26.5 34.9 reduce-scatter.6
  78.3 33.5 reduce-scatter.8
  128.6 33.5 reduce-scatter.10
  174.9 19.1 reduce-scatter.12
  206.7 16.4 reduce-scatter.14
  235.7 16.5 reduce-scatter.16
where the time goes:
time: 262 us; the launch traced here: 261 us
  waiting for transfers between devices  153 us (58%)
  blocking collectives  69.9 us (27%)
  between operations  13.7 us (5%)
  local copies, waits for them, and re-layouts  11.1 us (4%)
  matrix products  11.1 us (4%)
    reduce_scatter x3, waiting for transfers between devices, solve_all(): lax.psum_scatter(term(jnp.int32(0), lax.axis_size('col') * rows_dev).asty...  101 us
    reduce_scatter x3, waiting for transfers between devices, solve_all(): lax.psum_scatter(column_sums.astype(jnp.bfloat16), 'row', scatter_dimensi...  52.5 us
    all_gather x3, blocking collectives, solve_all(): lax.all_gather(current.astype(jnp.bfloat16), 'row', axis=0, tiled=True)  42 us
    all_gather x3, blocking collectives, solve_all(): lax.all_gather(current.astype(jnp.bfloat16), 'col', axis=0, tiled=True)  27.8 us
  transfers between devices with their start and end apart: 6, of which 6 were waited for; matrix products, arithmetic and copies ran while one was open for 0% of the time, Pallas kernels for 0%

commit v1 on v0

v1 whole, which is shorter than its diff:
```python
import functools

import jax
import jax.numpy as jnp
from jax import lax
from jax.experimental import pallas as pl
from jax.experimental.pallas import tpu as pltpu
from jax.sharding import PartitionSpec as P

BF16 = jnp.bfloat16
F32 = jnp.float32
NT = (((1,), (1,)), ((), ()))
VMEM_BYTES = 24 << 20
SLICE_ROWS = 16


class Plan:
    def __init__(self, n_row, n_col, factor_tiles, right_sides):
        self.levels, self.tiles, self.block, _ = factor_tiles.shape
        self.rows_dev = right_sides.shape[1]
        self.vectors = right_sides.shape[3]
        self.n_row, self.n_col = n_row, n_col
        split = 1
        while n_col % (split * 2) == 0 and self.vectors // (n_row * split * 2) >= SLICE_ROWS:
            split *= 2
        self.split = split
        self.groups = n_col // split
        self.sources = n_row * split
        self.slice = self.vectors // self.sources
        self.lanes = self.rows_dev * self.block
        self.owned = self.sources * self.rows_dev
        self.blocks = self.groups * self.owned
        self.tile_rows = self.tiles // 2 * self.block
        self.levels_in = [[0]] + [[s] for s in range(1, self.levels - 1)] + [[self.levels - 1, self.levels]]
        self.index_at = self.tile_rows
        self.inverse_at = self.index_at + 16

    def vector_parts(self, coupling):
        return 1 if coupling == 0 else 2 * len(self.levels_in[coupling])

    def vectors_at(self, coupling):
        inverses = 0 if coupling == 0 else len(self.levels_in[coupling])
        return self.inverse_at + inverses * self.block

    def payload_rows(self, coupling):
        return self.vectors_at(coupling) + self.split * self.vector_parts(coupling) * self.slice

    def pieces(self):
        return [(mz, my) for my in range(self.split) for mz in range(self.n_row)]


def call(body, outs, specs, scratch, args):
    return pl.pallas_call(
        body,
        out_shape=outs,
        in_specs=specs,
        out_specs=[pl.BlockSpec(memory_space=pltpu.VMEM)] * len(outs),
        scratch_shapes=scratch,
        compiler_params=pltpu.CompilerParams(vmem_limit_bytes=VMEM_BYTES),
    )(*args)


def vmem(count):
    return [pl.BlockSpec(memory_space=pltpu.VMEM)] * count


def smem(count):
    return [pl.BlockSpec(memory_space=pltpu.SMEM)] * count


def low_lanes(shape, half):
    return lax.broadcasted_iota(jnp.int32, shape, len(shape) - 1) < half


def split_rows(value):
    high = value.astype(BF16)
    return jnp.concatenate([high, (value - high.astype(F32)).astype(BF16)], axis=0)


def apply_pair(inverse, value, half):
    n = value.shape[0]
    both = jnp.concatenate([value, pltpu.roll(value, half, 1)], axis=0)[:, :half]
    out = jnp.dot(split_rows(both), inverse, preferred_element_type=F32)
    out = out[: 2 * n] + out[2 * n :]
    return jnp.where(low_lanes((n, 2 * half), half), out[:n], out[n:])


def apply_pair_transposed(inverse, value, half):
    n = value.shape[0]
    low = low_lanes(value.shape, half)
    both = jnp.concatenate([jnp.where(low, value, 0.0), jnp.where(low, 0.0, value)], axis=0)
    out = lax.dot_general(split_rows(both), inverse, NT, preferred_element_type=F32)
    out = out[: 2 * n] + out[2 * n :]
    return jnp.concatenate([out[:n], out[n:]], axis=1)


def pack_tiles(plan, coupling, tiles, rows, cols, payloads):
    lane = lax.broadcasted_iota(jnp.int32, (16, 128), 1)
    index = jnp.zeros((16, 128), F32)
    for t in range(plan.tiles):
        index = jnp.where(lane == t, rows[coupling, t, 0].astype(F32), index)
        index = jnp.where(lane == t + 64, cols[coupling, t, 0].astype(F32), index)
    index = index.astype(BF16)
    for k in range(plan.tiles // 2):
        pair = jnp.concatenate([tiles[coupling, 2 * k], tiles[coupling, 2 * k + 1]], axis=1)
        for payload in payloads:
            payload[k * plan.block : (k + 1) * plan.block, :] = pair
    for payload in payloads:
        payload[plan.index_at : plan.index_at + 16, :] = index


def put_slices(plan, coupling, part, place, scratch, payloads):
    width = plan.slice
    for mz, payload in enumerate(payloads):
        for my in range(plan.split):
            number = (place[0] ^ mz) * plan.split + (place[1] ^ my)
            at = plan.vectors_at(coupling) + (my * plan.vector_parts(coupling) + part) * width
            payload[at : at + width, :] = scratch[number]


def first_kernel(plan, place, rows, cols, tiles, sides, inverse, *rest):
    payloads, x0, scratch = rest[: plan.n_row], rest[plan.n_row], rest[plan.n_row + 1]
    half = plan.block
    parts = []
    for b in range(plan.rows_dev):
        matrix = inverse[0, :, b * half : (b + 1) * half]
        parts.append(lax.dot_general(matrix, sides[0, b], (((0,), (0,)), ((), ())),
                                     precision=lax.Precision.HIGHEST, preferred_element_type=F32))
    solved = jnp.concatenate(parts, axis=0)
    x0[...] = solved
    scratch[...] = solved.T.astype(BF16).reshape(scratch.shape)
    pack_tiles(plan, 0, tiles, rows, cols, payloads)
    put_slices(plan, 0, 0, place, scratch, payloads)


def second_kernel(plan, place, rows, cols, tiles, sides, inverse, *rest):
    scratch = rest[-1]
    half = plan.block
    for coupling in range(1, plan.levels):
        payloads = rest[(coupling - 1) * plan.n_row : coupling * plan.n_row]
        pack_tiles(plan, coupling, tiles, rows, cols, payloads)
        for at, level in enumerate(plan.levels_in[coupling]):
            start = plan.inverse_at + at * half
            matrix = inverse[level].astype(BF16)
            for payload in payloads:
                payload[start : start + half, :] = matrix
            both = jnp.concatenate([sides[level, b] for b in range(plan.rows_dev)], axis=0).T
            high = both.astype(BF16)
            low = (both - high.astype(F32)).astype(BF16)
            for part, value in enumerate((high, low)):
                scratch[at, part] = value.reshape(scratch.shape[2:])
                put_slices(plan, coupling, 2 * at + part, place, scratch.at[at, part], payloads)


def vector_slice(plan, coupling, piece, my, part):
    at = plan.vectors_at(coupling) + (my * plan.vector_parts(coupling) + part) * plan.slice
    return piece[at : at + plan.slice, :]


def source(plan, place, mz, my):
    return (place[1] ^ my) * plan.n_row + (place[0] ^ mz)


def decode(plan, place, pieces, index):
    lane = lax.broadcasted_iota(jnp.int32, (1, 128), 1)
    for p, (mz, my) in enumerate(plan.pieces()):
        raw = pieces[p][plan.index_at : plan.index_at + 16, :].astype(F32).astype(jnp.int32)[0:1]
        owner = raw // plan.rows_dev
        group, part = owner % plan.groups, owner // plan.groups
        row = group * plan.owned + (part * plan.n_row + (place[0] ^ mz)) * plan.rows_dev + raw % plan.rows_dev
        col = (place[1] ^ my) * (plan.n_row * plan.rows_dev) + raw
        index[p : p + 1, :] = jnp.where(lane < 64, row, col)


def store_halves(left, right, at, value, half):
    low = low_lanes(value.shape, half)
    other = pltpu.roll(value, half, 1)
    left[2 * at] = jnp.where(low, value, 0.0).astype(BF16)
    right[2 * at] = jnp.where(low, 0.0, other).astype(BF16)
    left[2 * at + 1] = jnp.where(low, other, 0.0).astype(BF16)
    right[2 * at + 1] = jnp.where(low, 0.0, value).astype(BF16)


def forward_kernel(plan, coupling, *refs):
    refs = list(refs)
    place = refs.pop(0)
    take = lambda count: [refs.pop(0) for _ in range(count)]
    pieces = take(plan.sources)
    sums = take(plan.groups) if coupling else None
    out = take(plan.groups)
    index_out = refs.pop(0)
    solved = refs.pop(0) if coupling else None
    left, right, total, index, sem = refs
    half, width = plan.block, plan.slice
    decode(plan, place, pieces, index_out)
    copy = pltpu.make_async_copy(index_out, index, sem)
    copy.start()
    for p, (mz, my) in enumerate(plan.pieces()):
        at = source(plan, place, mz, my)
        if coupling == 0:
            value = vector_slice(plan, 0, pieces[p], my, 0).astype(F32)
        else:
            value = level_solve(plan, coupling, 0, pieces[p], my, sums, at)
            solved[at] = value
        store_halves(left, right, at, value, half)
    total[...] = jnp.zeros_like(total)
    copy.wait()
    for p in range(plan.sources):
        for k in range(plan.tiles // 2):
            pair = pieces[p][k * half : (k + 1) * half, :]
            vectors = jnp.concatenate([left[index[p, 2 * k + 64]], right[index[p, 2 * k + 65]]], axis=0)
            product = lax.dot_general(vectors, pair, NT, preferred_element_type=F32)
            total[index[p, 2 * k]] += product[:width]
            total[index[p, 2 * k + 1]] += product[width:]
    for m in range(plan.groups):
        base = (place[2] ^ m) * plan.owned
        for u in range(plan.sources):
            value = jnp.concatenate([total[base + 2 * u], total[base + 2 * u + 1]], axis=1)
            out[m][u] = value.astype(out[m].dtype)


def level_solve(plan, coupling, at_level, piece, my, sums, at):
    coupled = sums[0][at]
    for received in sums[1:]:
        coupled = coupled + received[at].astype(F32)
    value = vector_slice(plan, coupling, piece, my, 2 * at_level).astype(F32)
    value = value + vector_slice(plan, coupling, piece, my, 2 * at_level + 1).astype(F32)
    start = plan.inverse_at + at_level * plan.block
    return apply_pair(piece[start : start + plan.block, :], value - coupled, plan.block)


def top_kernel(plan, place, *refs):
    pieces, sums, out = refs[: plan.sources], refs[plan.sources : -1], refs[-1]
    start = plan.inverse_at + plan.block
    for p, (mz, my) in enumerate(plan.pieces()):
        at = source(plan, place, mz, my)
        value = level_solve(plan, plan.levels - 1, 1, pieces[p], my, sums, at)
        out[at] = apply_pair_transposed(pieces[p][start : start + plan.block, :], value, plan.block).astype(BF16)


def backward_kernel(plan, coupling, *refs):
    refs = list(refs)
    place, index = refs.pop(0), refs.pop(0)
    take = lambda count: [refs.pop(0) for _ in range(count)]
    pieces = take(plan.sources)
    upper = take(plan.groups)
    solved = refs.pop(0) if coupling else None
    earlier = None if coupling else take(plan.levels)
    out = [refs.pop(0)] if coupling else take(plan.sources)
    rows, left, right = refs
    half, width = plan.block, plan.slice
    for m in range(plan.groups):
        base = (place[2] ^ m) * plan.owned
        for u in range(plan.sources):
            value = upper[m][u]
            rows[base + 2 * u] = value[:, :half]
            rows[base + 2 * u + 1] = value[:, half:]
    left[...] = jnp.zeros_like(left)
    right[...] = jnp.zeros_like(right)
    for p in range(plan.sources):
        for k in range(plan.tiles // 2):
            pair = pieces[p][k * half : (k + 1) * half, :]
            vectors = jnp.concatenate([rows[index[p, 2 * k]], rows[index[p, 2 * k + 1]]], axis=0)
            product = jnp.dot(vectors, pair, preferred_element_type=F32)
            left[index[p, 2 * k + 64]] += product[:width]
            right[index[p, 2 * k + 65]] += product[width:]
    low = low_lanes((width, plan.lanes), half)
    for p, (mz, my) in enumerate(plan.pieces()):
        at = source(plan, place, mz, my)
        first = left[2 * at] + pltpu.roll(right[2 * at], half, 1)
        other = right[2 * at + 1] + pltpu.roll(left[2 * at + 1], half, 1)
        back = jnp.where(low, first, other)
        if coupling:
            start = plan.inverse_at
            value = apply_pair_transposed(pieces[p][start : start + half, :], solved[at] - back, half)
            out[0][at] = value.astype(BF16)
        else:
            for n, level in enumerate(earlier):
                out[p][n * width : (n + 1) * width, :] = level[at]
            out[p][plan.levels * width :, :] = back.astype(BF16)


def last_kernel(plan, place, inverse, x0, *refs):
    pieces, out, scratch = refs[: plan.sources], refs[plan.sources], refs[plan.sources + 1]
    half, width = plan.block, plan.slice
    for p, (mz, my) in enumerate(plan.pieces()):
        number = (place[0] ^ mz) * plan.split + (place[1] ^ my)
        for n in range(plan.levels + 1):
            scratch[n, number] = pieces[p][n * width : (n + 1) * width, :]
    for n in range(plan.levels + 1):
        value = scratch[n].astype(F32).reshape(plan.vectors, plan.lanes).T
        if n == plan.levels:
            value = x0[...] - value
        for b in range(plan.rows_dev):
            part = value[b * half : (b + 1) * half, :]
            if n == plan.levels:
                part = jnp.dot(inverse[0, :, b * half : (b + 1) * half], part,
                               precision=lax.Precision.HIGHEST, preferred_element_type=F32)
            out[plan.levels - n if n < plan.levels else 0, b] = part


def on_device(n_row, n_col, factor_tiles, tile_row, tile_col, right_sides, diag_inverse):
    plan = Plan(n_row, n_col, factor_tiles, right_sides)
    levels, groups, sources = plan.levels, plan.groups, plan.sources
    shape = jax.ShapeDtypeStruct
    r, c = lax.axis_index("row"), lax.axis_index("col")
    place = jnp.stack([r, c // groups, c % groups]).astype(jnp.int32)

    def move(value, mz, my, mg):
        if mz == 0:
            pairs = [(i, i ^ (my * groups + mg)) for i in range(n_col)]
            return lax.ppermute(value, "col", pairs)
        if my == 0 and mg == 0:
            return lax.ppermute(value, "row", [(i, i ^ mz) for i in range(n_row)])
        pairs = [(i, i ^ (mz * n_col + my * groups + mg)) for i in range(n_row * n_col)]
        return lax.ppermute(value, ("row", "col"), pairs)

    def gather(payloads):
        near = [payloads[0]] + [move(payloads[mz], mz, 0, 0) for mz in range(1, n_row)]
        return [near[mz] if my == 0 else move(near[mz], 0, my, 0) for mz, my in plan.pieces()]

    piece_shape = (sources, plan.slice, plan.lanes)
    common = (place, tile_row, tile_col, factor_tiles, right_sides, diag_inverse)
    specs = smem(3) + vmem(3)
    made = call(
        functools.partial(first_kernel, plan),
        [shape((plan.payload_rows(0), plan.lanes), BF16)] * n_row + [shape((plan.lanes, plan.vectors), F32)],
        specs,
        [pltpu.VMEM(piece_shape, BF16)],
        common,
    )
    x0 = made[n_row]
    payloads = [made[:n_row]]
    made = call(
        functools.partial(second_kernel, plan),
        [shape((plan.payload_rows(s), plan.lanes), BF16) for s in range(1, levels) for _ in range(n_row)],
        specs,
        [pltpu.VMEM((2, 2) + piece_shape, BF16)],
        common,
    )
    payloads += [made[s * n_row : (s + 1) * n_row] for s in range(levels - 1)]
    pieces = [gather(payload) for payload in payloads]

    piece = shape(piece_shape, BF16)
    index_shape = (max(8, sources), 128)
    scratch = [
        pltpu.VMEM((plan.owned, plan.slice, plan.lanes), BF16),
        pltpu.VMEM((plan.owned, plan.slice, plan.lanes), BF16),
        pltpu.VMEM((plan.blocks, plan.slice, plan.block), F32),
        pltpu.SMEM(index_shape, jnp.int32),
        pltpu.SemaphoreType.DMA(()),
    ]
    index, solved, sums = [], [None], None
    for s in range(levels):
        args = [place] + pieces[s] + (sums if s else [])
        outs = [shape(piece_shape, F32)] + [piece] * (groups - 1) + [shape(index_shape, jnp.int32)]
        outs += [shape(piece_shape, F32)] if s else []
        body = functools.partial(forward_kernel, plan, s)
        made = call(body, outs, smem(1) + vmem(len(args) - 1), scratch, args)
        sums = [made[0]] + [move(made[m], 0, 0, m) for m in range(1, groups)]
        index.append(made[groups])
        if s:
            solved.append(made[groups + 1])
    args = [place] + pieces[levels - 1] + sums
    current = call(functools.partial(top_kernel, plan), [piece], smem(1) + vmem(len(args) - 1), [], args)[0]
    results = [current]
    scratch = [
        pltpu.VMEM((plan.blocks, plan.slice, plan.block), BF16),
        pltpu.VMEM((plan.owned, plan.slice, plan.lanes), F32),
        pltpu.VMEM((plan.owned, plan.slice, plan.lanes), F32),
    ]
    for s in range(levels - 1, -1, -1):
        upper = [current] + [move(current, 0, 0, m) for m in range(1, groups)]
        args = [place, index[s]] + pieces[s] + upper + ([solved[s]] if s else results)
        outs = [piece] if s else [shape(((levels + 1) * plan.slice, plan.lanes), BF16)] * sources
        made = call(functools.partial(backward_kernel, plan, s), outs, smem(2) + vmem(len(args) - 2), scratch, args)
        if s:
            current = made[0]
            results.append(current)
    final = [made[p] if (mz, my) == (0, 0) else move(made[p], mz, my, 0) for p, (mz, my) in enumerate(plan.pieces())]
    args = [place, diag_inverse, x0] + final
    return call(
        functools.partial(last_kernel, plan),
        [shape(right_sides.shape, F32)],
        smem(1) + vmem(len(args) - 1),
        [pltpu.VMEM((levels + 1,) + piece_shape, BF16)],
        args,
    )[0]


def solution(mesh):
    return jax.shard_map(
        functools.partial(on_device, mesh.shape["row"], mesh.shape["col"]),
        mesh=mesh,
        in_specs=(
            P(None, "row", None, "col"),
            P(None, "row", "col"),
            P(None, "row", "col"),
            P(None, ("col", "row"), None, None),
            P(None, None, ("col", "row")),
        ),
        out_specs=P(None, ("col", "row"), None, None),
        check_vma=False,
    )
```

time: 262 us -> 113 us (0.43)
  waiting for transfers between devices: 153 us -> 36.5 us
  blocking collectives: 69.9 us -> 0 us
  starting transfers between devices: 0.21 us -> 55 us
  Pallas kernels: 0 us -> 16.7 us
  between operations: 13.7 us -> 0.16 us
  matrix products: 11.1 us -> 0 us
  local copies, waits for them, and re-layouts: 11.1 us -> 4.39 us
    reduce_scatter x6 -> x0, waiting for transfers between devices: 153 us -> none  [the longest x3 101 us: solve_all(): lax.psum_scatter(term(jnp.int32(0), lax.axis_size('col') * rows_dev).asty...]
    all_gather x6 -> x0, blocking collectives: 69.9 us -> none  [the longest x3 42 us: solve_all(): lax.all_gather(current.astype(jnp.bfloat16), 'row', axis=0, tiled=True)]
    ppermute x0 -> x46, starting transfers between devices: none -> 55 us  [the longest x31 28 us: move(): return lax.ppermute(value, 'col', pairs)]
    ppermute x0 -> x46, waiting for transfers between devices: none -> 36.5 us  [the longest x31 19.5 us: move(): return lax.ppermute(value, 'col', pairs)]
    pallas_call x0 -> x10, Pallas kernels: none -> 16.7 us  [call(): pl.pallas_call(body, out_shape=outs, in_specs=specs, out_specs=[pl.BlockS...]
    dot_general x20 -> x0, matrix products: 11.1 us -> none  [the longest x4 3.32 us: apply_inverse(): jnp.einsum('cir,irn->icn', matrix, vector, precision=lax.Precision.HIGHEST)]
    gather x6 -> x0, local copies, waits for them, and re-layouts: 3.49 us -> none  [the longest x3 1.75 us: solve_all(): picked = gathered[col_ids[section_no - 1]]]
    unnamed x8 -> x14, local copies, waits for them, and re-layouts: 1.28 us -> 4.39 us
  transfers between devices with their start and end apart: 6 -> 46, of which waited for: 6 -> 17; matrix products, arithmetic and copies ran while one was open for 0% -> 0% of each run, Pallas kernels for 0% -> 5%
where the time goes in v1:
time: 113 us
  starting transfers between devices  55 us (49%)
  waiting for transfers between devices  36.5 us (32%)
  Pallas kernels  16.7 us (15%)
  local copies, waits for them, and re-layouts  4.39 us (4%)
    ppermute x31, starting transfers between devices, move(): return lax.ppermute(value, 'col', pairs)  28 us
    ppermute x12, starting transfers between devices, move(): return lax.ppermute(value, 'row', [(i, i ^ mz) for i in range(n_row)])  21.9 us
    ppermute x31, waiting for transfers between devices, move(): return lax.ppermute(value, 'col', pairs)  19.5 us
    pallas_call x10, Pallas kernels, call(): pl.pallas_call(body, out_shape=outs, in_specs=specs, out_specs=[pl.BlockS...  16.7 us
    ppermute x12, waiting for transfers between devices, move(): return lax.ppermute(value, 'row', [(i, i ^ mz) for i in range(n_row)])  12.2 us
    ppermute x3, starting transfers between devices, move(): return lax.ppermute(value, ('row', 'col'), pairs)  5.09 us
    ppermute x3, waiting for transfers between devices, move(): return lax.ppermute(value, ('row', 'col'), pairs)  4.75 us
    unnamed x14, local copies, waits for them, and re-layouts  4.39 us
  transfers between devices with their start and end apart: 46, of which 17 were waited for; matrix products, arithmetic and copies ran while one was open for 0% of the time, Pallas kernels for 5%

profile of v1, /device:TPU:0, one launch (start us, length us, event | category | flops | bytes accessed | tf_op | source)
XLA Modules:
  0.0 112.9 jit_solution(3934873143416953635)
XLA Ops:
  4.5 1.7 %shard_map.55 = (bf16[432,128]{1,0:T(8,128)(2,1)S(1)}, bf16[432,128]{1,0:T(8,128)(2,1)S(1)}, bf16[432,128]{1,0:T(8,128)(2,1)S(1)}, bf16[432,128]{1,0:T(8,128)(2,1)S(1)}, f32[128,128]{1,0:T(8,128)S(1)}) custom-call(s32[3]{0:T(128)S(1)} %pad_add_fusion.place.refs_0_, s32[3,12,1]{2,1,0:T(8,128)S(1)} %copy.6.rows, s32[3,12,1]{2,1,0:T(8,128)S(1)} %copy.7.cols, ...), custom_call_target="tpu_custom_call" | custom-call | tf_op jit(solution)/shard_map/pallas_call | solution.py:53
  6.2 3.1 %collective-permute-start = (bf16[432,128]{1,0:T(8,128)(2,1)S(1)}, bf16[432,128]{1,0:T(8,128)(2,1)S(1)}, u32[]{:S(2)}, u32[]{:S(2)}) collective-permute-start(bf16[432,128]{1,0:T(8,128)(2,1)S(1)} %get-tuple-element.45), channel_id=1, source_target_pairs={{0,8},{8,0},{16,24},{24,16},{1,9},{9,1},{17,25},{25,17},{2,10},{10... | collective-permute-start | bytes 331784 | tf_op jit(solution)/shard_map/ppermute | solution.py:314
  9.3 2.6 %collective-permute-start.1 = (bf16[432,128]{1,0:T(8,128)(2,1)S(1)}, bf16[432,128]{1,0:T(8,128)(2,1)S(1)}, u32[]{:S(2)}, u32[]{:S(2)}) collective-permute-start(bf16[432,128]{1,0:T(8,128)(2,1)S(1)} %get-tuple-element.46), channel_id=1, source_target_pairs={{0,16},{8,24},{16,0},{24,8},{1,17},{9,25},{17,1},{25,9},{2,18},{10... | collective-permute-start | bytes 331784 | tf_op jit(solution)/shard_map/ppermute | solution.py:314
  11.9 1.7 %collective-permute-start.3 = (bf16[432,128]{1,0:T(8,128)(2,1)S(1)}, bf16[432,128]{1,0:T(8,128)(2,1)S(1)}, u32[]{:S(2)}, u32[]{:S(2)}) collective-permute-start(bf16[432,128]{1,0:T(8,128)(2,1)S(1)} %get-tuple-element.44.refs_1_.refs_2_), channel_id=1, source_target_pairs={{0,4},{1,5},{2,6},{3,7},{4,0},{5,1},{6,2},{7,3},{8,12},{9,13},{10,... | collective-permute-start | bytes 331784 | tf_op jit(solution)/shard_map/ppermute | solution.py:312
  16.0 3.5 %collective-permute-start.8 = (bf16[528,128]{1,0:T(8,128)(2,1)S(1)}, bf16[528,128]{1,0:T(8,128)(2,1)S(1)}, u32[]{:S(2)}, u32[]{:S(2)}) collective-permute-start(bf16[528,128]{1,0:T(8,128)(2,1)S(1)} %get-tuple-element.51), channel_id=1, source_target_pairs={{0,16},{8,24},{16,0},{24,8},{1,17},{9,25},{17,1},{25,9},{2,18},{10... | collective-permute-start | bytes 405512 | tf_op jit(solution)/shard_map/ppermute | solution.py:314
  20.8 3.2 %collective-permute-start.9 = (bf16[528,128]{1,0:T(8,128)(2,1)S(1)}, bf16[528,128]{1,0:T(8,128)(2,1)S(1)}, u32[]{:S(2)}, u32[]{:S(2)}) collective-permute-start(bf16[528,128]{1,0:T(8,128)(2,1)S(1)} %get-tuple-element.52), channel_id=1, source_target_pairs={{0,24},{8,16},{16,8},{24,0},{1,25},{9,17},{17,9},{25,1},{2,26},{10... | collective-permute-start | bytes 405512 | tf_op jit(solution)/shard_map/ppermute | solution.py:314
  23.9 1.7 %collective-permute-start.10 = (bf16[528,128]{1,0:T(8,128)(2,1)S(1)}, bf16[528,128]{1,0:T(8,128)(2,1)S(1)}, u32[]{:S(2)}, u32[]{:S(2)}) collective-permute-start(bf16[528,128]{1,0:T(8,128)(2,1)S(1)} %get-tuple-element.49.refs_1_.refs_2_), channel_id=1, source_target_pairs={{0,4},{1,5},{2,6},{3,7},{4,0},{5,1},{6,2},{7,3},{8,12},{9,13},{10,... | collective-permute-start | bytes 405512 | tf_op jit(solution)/shard_map/ppermute | solution.py:312
  27.7 4.1 %collective-permute-done.8.refs_3_.refs_4_ = bf16[528,128]{1,0:T(8,128)(2,1)S(1)} collective-permute-done((bf16[528,128]{1,0:T(8,128)(2,1)S(1)}, bf16[528,128]{1,0:T(8,128)(2,1)S(1)}, u32[]{:S(2)}, u32[]{:S(2)}) %collective-permute-start.8) | collective-permute-done | bytes 135200 | tf_op jit(solution)/shard_map/ppermute | solution.py:314
  34.0 2.3 %collective-permute-start.18 = (bf16[656,128]{1,0:T(8,128)(2,1)S(1)}, bf16[656,128]{1,0:T(8,128)(2,1)S(1)}, u32[]{:S(2)}, u32[]{:S(2)}) collective-permute-start(bf16[656,128]{1,0:T(8,128)(2,1)S(1)} %get-tuple-element.60), channel_id=1, source_target_pairs={{0,16},{8,24},{16,0},{24,8},{1,17},{9,25},{17,1},{25,9},{2,18},{10... | collective-permute-start | bytes 503816 | tf_op jit(solution)/shard_map/ppermute | solution.py:314
  39.8 2.0 %shard_map.56 = (f32[8,16,128]{2,1,0:T(8,128)S(1)}, bf16[8,16,128]{2,1,0:T(8,128)(2,1)S(1)}, bf16[8,16,128]{2,1,0:T(8,128)(2,1)S(1)}, bf16[8,16,128]{2,1,0:T(8,128)(2,1)S(1)}, s32[8,128]{1,0:T(8,128)S(1)}) custom-call(s32[3]{0:T(128)S(1)} %pad_add_fusion.place.refs_0_, bf16[432,128]{1,0:T(8,128)(2,1)S(1)} %get-tuple-element.44.refs_1_.refs_2_, ...), custom_call_target="tpu_custom_call" | custom-call | tf_op jit(solution)/shard_map/pallas_call | solution.py:53
  41.8 6.8 %collective-permute-done.18.refs_3_.refs_2_.refs_4_ = bf16[656,128]{1,0:T(8,128)(2,1)S(1)} collective-permute-done((bf16[656,128]{1,0:T(8,128)(2,1)S(1)}, bf16[656,128]{1,0:T(8,128)(2,1)S(1)}, u32[]{:S(2)}, u32[]{:S(2)}) %collective-permute-start.18) | collective-permute-done | bytes 167968 | tf_op jit(solution)/shard_map/ppermute | solution.py:314
  52.5 3.6 %collective-permute-done.16.refs_12_ = bf16[8,16,128]{2,1,0:T(8,128)(2,1)S(1)} collective-permute-done((bf16[8,16,128]{2,1,0:T(8,128)(2,1)S(1)}, bf16[8,16,128]{2,1,0:T(8,128)(2,1)S(1)}, u32[]{:S(2)}, u32[]{:S(2)}) %collective-permute-start.16) | collective-permute-done | bytes 32800 | tf_op jit(solution)/shard_map/ppermute | solution.py:312
  56.1 1.8 %collective-permute-start.21 = (bf16[656,128]{1,0:T(8,128)(2,1)S(1)}, bf16[656,128]{1,0:T(8,128)(2,1)S(1)}, u32[]{:S(2)}, u32[]{:S(2)}) collective-permute-start(bf16[656,128]{1,0:T(8,128)(2,1)S(1)} %collective-permute-done.17.refs_2_.refs_1_.refs_3_), channel_id=1, source_target_pairs={{0,4},{1,5},{2,6},{3,7},{4,0},{5,1},{6,2},{7,3},{8,12},{9,13},{10,... | collective-permute-start | bytes 503816 | tf_op jit(solution)/shard_map/ppermute | solution.py:312
  58.1 1.8 %collective-permute-start.23 = (bf16[656,128]{1,0:T(8,128)(2,1)S(1)}, bf16[656,128]{1,0:T(8,128)(2,1)S(1)}, u32[]{:S(2)}, u32[]{:S(2)}) collective-permute-start(bf16[656,128]{1,0:T(8,128)(2,1)S(1)} %collective-permute-done.19.refs_4_.refs_3_.refs_5_), channel_id=1, source_target_pairs={{0,4},{1,5},{2,6},{3,7},{4,0},{5,1},{6,2},{7,3},{8,12},{9,13},{10,... | collective-permute-start | bytes 503816 | tf_op jit(solution)/shard_map/ppermute | solution.py:312
  59.9 2.2 %shard_map.58 = (f32[8,16,128]{2,1,0:T(8,128)S(1)}, bf16[8,16,128]{2,1,0:T(8,128)(2,1)S(1)}, bf16[8,16,128]{2,1,0:T(8,128)(2,1)S(1)}, bf16[8,16,128]{2,1,0:T(8,1...) custom-call(s32[3]{0:T(128)S(1)} %pad_add_fusion.place.refs_0_, ...), custom_call_target="tpu_custom_call" | custom-call | tf_op jit(solution)/shard_map/pallas_call | solution.py:53
  64.3 1.8 %collective-permute-done.25.refs_11_ = bf16[8,16,128]{2,1,0:T(8,128)(2,1)S(1)} collective-permute-done((bf16[8,16,128]{2,1,0:T(8,128)(2,1)S(1)}, bf16[8,16,128]{2,1,0:T(8,128)(2,1)S(1)}, u32[]{:S(2)}, u32[]{:S(2)}) %collective-permute-start.25) | collective-permute-done | bytes 32800 | tf_op jit(solution)/shard_map/ppermute | solution.py:312
  66.8 2.9 %collective-permute-done.23.refs_8_.refs_7_.refs_9_ = bf16[656,128]{1,0:T(8,128)(2,1)S(1)} collective-permute-done((bf16[656,128]{1,0:T(8,128)(2,1)S(1)}, bf16[656,128]{1,0:T(8,128)(2,1)S(1)}, u32[]{:S(2)}, u32[]{:S(2)}) %collective-permute-start.23) | collective-permute-done | bytes 167968 | tf_op jit(solution)/shard_map/ppermute | solution.py:312
  69.7 2.2 %shard_map.59 = (f32[8,16,128]{2,1,0:T(8,128)S(1)}, bf16[8,16,128]{2,1,0:T(8,128)(2,1)S(1)}, bf16[8,16,128]{2,1,0:T(8,128)(2,1)S(1)}, bf16[8,16,128]{2,1,0:T(8,1...) custom-call(s32[3]{0:T(128)S(1)} %pad_add_fusion.place.refs_0_, ...), custom_call_target="tpu_custom_call" | custom-call | tf_op jit(solution)/shard_map/pallas_call | solution.py:53
  73.9 2.3 %collective-permute-done.28.refs_10_ = bf16[8,16,128]{2,1,0:T(8,128)(2,1)S(1)} collective-permute-done((bf16[8,16,128]{2,1,0:T(8,128)(2,1)S(1)}, bf16[8,16,128]{2,1,0:T(8,128)(2,1)S(1)}, u32[]{:S(2)}, u32[]{:S(2)}) %collective-permute-start.28) | collective-permute-done | bytes 32800 | tf_op jit(solution)/shard_map/ppermute | solution.py:312
  91.6 1.7 %collective-permute-done.38.refs_13_ = bf16[8,16,128]{2,1,0:T(8,128)(2,1)S(1)} collective-permute-done((bf16[8,16,128]{2,1,0:T(8,128)(2,1)S(1)}, bf16[8,16,128]{2,1,0:T(8,128)(2,1)S(1)}, u32[]{:S(2)}, u32[]{:S(2)}) %collective-permute-start.38) | collective-permute-done | bytes 32800 | tf_op jit(solution)/shard_map/ppermute | solution.py:312
  95.9 2.1 %collective-permute-start.40 = (bf16[64,128]{1,0:T(8,128)(2,1)S(1)}, bf16[64,128]{1,0:T(8,128)(2,1)S(1)}, u32[]{:S(2)}, u32[]{:S(2)}) collective-permute-start(bf16[64,128]{1,0:T(8,128)(2,1)S(1)} %get-tuple-element.75), channel_id=1, source_target_pairs={{0,16},{8,24},{16,0},{24,8},{1,17},{9,25},{17,1},{25,9},{2,18},{10... | collective-permute-start | bytes 49160 | tf_op jit(solution)/shard_map/ppermute | solution.py:314
  98.0 1.8 %collective-permute-start.41 = (bf16[64,128]{1,0:T(8,128)(2,1)S(1)}, bf16[64,128]{1,0:T(8,128)(2,1)S(1)}, u32[]{:S(2)}, u32[]{:S(2)}) collective-permute-start(bf16[64,128]{1,0:T(8,128)(2,1)S(1)} %get-tuple-element.76), channel_id=1, source_target_pairs={{0,24},{8,16},{16,8},{24,0},{1,25},{9,17},{17,9},{25,1},{2,26},{10... | collective-permute-start | bytes 49160 | tf_op jit(solution)/shard_map/ppermute | solution.py:314
  101.5 3.4 %collective-permute-start.44 = (bf16[64,128]{1,0:T(8,128)(2,1)S(1)}, bf16[64,128]{1,0:T(8,128)(2,1)S(1)}, u32[]{:S(2)}, u32[]{:S(2)}) collective-permute-start(bf16[64,128]{1,0:T(8,128)(2,1)S(1)} %get-tuple-element.79), channel_id=1, source_target_pairs={{0,20},{1,21},{2,22},{3,23},{4,16},{5,17},{6,18},{7,19},{8,28},{9,... | collective-permute-start | bytes 49160 | tf_op jit(solution)/shard_map/ppermute | solution.py:316
  107.0 4.3 %collective-permute-done.45.refs_7_ = bf16[64,128]{1,0:T(8,128)(2,1)S(1)} collective-permute-done((bf16[64,128]{1,0:T(8,128)(2,1)S(1)}, bf16[64,128]{1,0:T(8,128)(2,1)S(1)}, u32[]{:S(2)}, u32[]{:S(2)}) %collective-permute-start.45) | collective-permute-done | bytes 16416 | tf_op jit(solution)/shard_map/ppermute | solution.py:316
  (93 shorter events, 48.2 us)
Async XLA Ops:
  6.2 9.8 %collective-permute-start = (bf16[432,128]{1,0:T(8,128)(2,1)S(1)}, bf16[432,128]{1,0:T(8,128)(2,1)S(1)}, u32[]{:S(2)}, u32[]{:S(2)}) collective-permute-start(bf16[432,128]{1,0:T(8,128)(2,1)S(1)} %get-tuple-element.45), channel_id=1, source_target_pairs={{0,8},{8,0},{16,24},{24,16},{1,9},{9,1},{17,25},{25,17},{2,10},{10... | collective-permute-start | bytes 331784 | tf_op jit(solution)/shard_map/ppermute | solution.py:314
  9.3 11.5 %collective-permute-start.1 = (bf16[432,128]{1,0:T(8,128)(2,1)S(1)}, bf16[432,128]{1,0:T(8,128)(2,1)S(1)}, u32[]{:S(2)}, u32[]{:S(2)}) collective-permute-start(bf16[432,128]{1,0:T(8,128)(2,1)S(1)} %get-tuple-element.46), channel_id=1, source_target_pairs={{0,16},{8,24},{16,0},{24,8},{1,17},{9,25},{17,1},{25,9},{2,18},{10... | collective-permute-start | bytes 331784 | tf_op jit(solution)/shard_map/ppermute | solution.py:314
  11.9 12.0 %collective-permute-start.2 = (bf16[432,128]{1,0:T(8,128)(2,1)S(1)}, bf16[432,128]{1,0:T(8,128)(2,1)S(1)}, u32[]{:S(2)}, u32[]{:S(2)}) collective-permute-start(bf16[432,128]{1,0:T(8,128)(2,1)S(1)} %get-tuple-element.47), channel_id=1, source_target_pairs={{0,24},{8,16},{16,8},{24,0},{1,25},{9,17},{17,9},{25,1},{2,26},{10... | collective-permute-start | bytes 331784 | tf_op jit(solution)/shard_map/ppermute | solution.py:314
  11.9 13.7 %collective-permute-start.3 = (bf16[432,128]{1,0:T(8,128)(2,1)S(1)}, bf16[432,128]{1,0:T(8,128)(2,1)S(1)}, u32[]{:S(2)}, u32[]{:S(2)}) collective-permute-start(bf16[432,128]{1,0:T(8,128)(2,1)S(1)} %get-tuple-element.44.refs_1_.refs_2_), channel_id=1, source_target_pairs={{0,4},{1,5},{2,6},{3,7},{4,0},{5,1},{6,2},{7,3},{8,12},{9,13},{10,... | collective-permute-start | bytes 331784 | tf_op jit(solution)/shard_map/ppermute | solution.py:312
  15.2 10.7 %collective-permute-start.7 = (bf16[528,128]{1,0:T(8,128)(2,1)S(1)}, bf16[528,128]{1,0:T(8,128)(2,1)S(1)}, u32[]{:S(2)}, u32[]{:S(2)}) collective-permute-start(bf16[528,128]{1,0:T(8,128)(2,1)S(1)} %get-tuple-element.50), channel_id=1, source_target_pairs={{0,8},{8,0},{16,24},{24,16},{1,9},{9,1},{17,25},{25,17},{2,10},{10... | collective-permute-start | bytes 405512 | tf_op jit(solution)/shard_map/ppermute | solution.py:314
  16.0 15.8 %collective-permute-start.8 = (bf16[528,128]{1,0:T(8,128)(2,1)S(1)}, bf16[528,128]{1,0:T(8,128)(2,1)S(1)}, u32[]{:S(2)}, u32[]{:S(2)}) collective-permute-start(bf16[528,128]{1,0:T(8,128)(2,1)S(1)} %get-tuple-element.51), channel_id=1, source_target_pairs={{0,16},{8,24},{16,0},{24,8},{1,17},{9,25},{17,1},{25,9},{2,18},{10... | collective-permute-start | bytes 405512 | tf_op jit(solution)/shard_map/ppermute | solution.py:314
  20.8 12.6 %collective-permute-start.9 = (bf16[528,128]{1,0:T(8,128)(2,1)S(1)}, bf16[528,128]{1,0:T(8,128)(2,1)S(1)}, u32[]{:S(2)}, u32[]{:S(2)}) collective-permute-start(bf16[528,128]{1,0:T(8,128)(2,1)S(1)} %get-tuple-element.52), channel_id=1, source_target_pairs={{0,24},{8,16},{16,8},{24,0},{1,25},{9,17},{17,9},{25,1},{2,26},{10... | collective-permute-start | bytes 405512 | tf_op jit(solution)/shard_map/ppermute | solution.py:314
  23.9 10.0 %collective-permute-start.10 = (bf16[528,128]{1,0:T(8,128)(2,1)S(1)}, bf16[528,128]{1,0:T(8,128)(2,1)S(1)}, u32[]{:S(2)}, u32[]{:S(2)}) collective-permute-start(bf16[528,128]{1,0:T(8,128)(2,1)S(1)} %get-tuple-element.49.refs_1_.refs_2_), channel_id=1, source_target_pairs={{0,4},{1,5},{2,6},{3,7},{4,0},{5,1},{6,2},{7,3},{8,12},{9,13},{10,... | collective-permute-start | bytes 405512 | tf_op jit(solution)/shard_map/ppermute | solution.py:312
  25.6 10.7 %collective-permute-start.4 = (bf16[432,128]{1,0:T(8,128)(2,1)S(1)}, bf16[432,128]{1,0:T(8,128)(2,1)S(1)}, u32[]{:S(2)}, u32[]{:S(2)}) collective-permute-start(bf16[432,128]{1,0:T(8,128)(2,1)S(1)} %collective-permute-done.refs_2_.refs_3_), channel_id=1, source_target_pairs={{0,4},{1,5},{2,6},{3,7},{4,0},{5,1},{6,2},{7,3},{8,12},{9,13},{10,... | collective-permute-start | bytes 331784 | tf_op jit(solution)/shard_map/ppermute | solution.py:312
  26.0 11.8 %collective-permute-start.5 = (bf16[432,128]{1,0:T(8,128)(2,1)S(1)}, bf16[432,128]{1,0:T(8,128)(2,1)S(1)}, u32[]{:S(2)}, u32[]{:S(2)}) collective-permute-start(bf16[432,128]{1,0:T(8,128)(2,1)S(1)} %collective-permute-done.1.refs_3_.refs_4_), channel_id=1, source_target_pairs={{0,4},{1,5},{2,6},{3,7},{4,0},{5,1},{6,2},{7,3},{8,12},{9,13},{10,... | collective-permute-start | bytes 331784 | tf_op jit(solution)/shard_map/ppermute | solution.py:312
  33.3 8.4 %collective-permute-start.17 = (bf16[656,128]{1,0:T(8,128)(2,1)S(1)}, bf16[656,128]{1,0:T(8,128)(2,1)S(1)}, u32[]{:S(2)}, u32[]{:S(2)}) collective-permute-start(bf16[656,128]{1,0:T(8,128)(2,1)S(1)} %get-tuple-element.59), channel_id=1, source_target_pairs={{0,8},{8,0},{16,24},{24,16},{1,9},{9,1},{17,25},{25,17},{2,10},{10... | collective-permute-start | bytes 503816 | tf_op jit(solution)/shard_map/ppermute | solution.py:314
  34.0 14.6 %collective-permute-start.18 = (bf16[656,128]{1,0:T(8,128)(2,1)S(1)}, bf16[656,128]{1,0:T(8,128)(2,1)S(1)}, u32[]{:S(2)}, u32[]{:S(2)}) collective-permute-start(bf16[656,128]{1,0:T(8,128)(2,1)S(1)} %get-tuple-element.60), channel_id=1, source_target_pairs={{0,16},{8,24},{16,0},{24,8},{1,17},{9,25},{17,1},{25,9},{2,18},{10... | collective-permute-start | bytes 503816 | tf_op jit(solution)/shard_map/ppermute | solution.py:314
  36.3 13.9 %collective-permute-start.19 = (bf16[656,128]{1,0:T(8,128)(2,1)S(1)}, bf16[656,128]{1,0:T(8,128)(2,1)S(1)}, u32[]{:S(2)}, u32[]{:S(2)}) collective-permute-start(bf16[656,128]{1,0:T(8,128)(2,1)S(1)} %get-tuple-element.61), channel_id=1, source_target_pairs={{0,24},{8,16},{16,8},{24,0},{1,25},{9,17},{17,9},{25,1},{2,26},{10... | collective-permute-start | bytes 503816 | tf_op jit(solution)/shard_map/ppermute | solution.py:314
  37.7 20.1 %collective-permute-start.11 = (bf16[528,128]{1,0:T(8,128)(2,1)S(1)}, bf16[528,128]{1,0:T(8,128)(2,1)S(1)}, u32[]{:S(2)}, u32[]{:S(2)}) collective-permute-start(bf16[528,128]{1,0:T(8,128)(2,1)S(1)} %collective-permute-done.7.refs_2_.refs_3_), channel_id=1, source_target_pairs={{0,4},{1,5},{2,6},{3,7},{4,0},{5,1},{6,2},{7,3},{8,12},{9,13},{10,... | collective-permute-start | bytes 405512 | tf_op jit(solution)/shard_map/ppermute | solution.py:312
  38.4 19.7 %collective-permute-start.12 = (bf16[528,128]{1,0:T(8,128)(2,1)S(1)}, bf16[528,128]{1,0:T(8,128)(2,1)S(1)}, u32[]{:S(2)}, u32[]{:S(2)}) collective-permute-start(bf16[528,128]{1,0:T(8,128)(2,1)S(1)} %collective-permute-done.8.refs_3_.refs_4_), channel_id=1, source_target_pairs={{0,4},{1,5},{2,6},{3,7},{4,0},{5,1},{6,2},{7,3},{8,12},{9,13},{10,... | collective-permute-start | bytes 405512 | tf_op jit(solution)/shard_map/ppermute | solution.py:312
  41.7 10.0 %collective-permute-start.14 = (bf16[8,16,128]{2,1,0:T(8,128)(2,1)S(1)}, bf16[8,16,128]{2,1,0:T(8,128)(2,1)S(1)}, u32[]{:S(2)}, u32[]{:S(2)}) collective-permute-start(bf16[8,16,128]{2,1,0:T(8,128)(2,1)S(1)} %get-tuple-element.54), channel_id=1, source_target_pairs={{0,1},{1,0},{2,3},{3,2},{4,5},{5,4},{6,7},{7,6},{8,9},{9,8},{10,11... | collective-permute-start | bytes 98312 | tf_op jit(solution)/shard_map/ppermute | solution.py:312
  50.2 9.7 %collective-permute-start.13 = (bf16[528,128]{1,0:T(8,128)(2,1)S(1)}, bf16[528,128]{1,0:T(8,128)(2,1)S(1)}, u32[]{:S(2)}, u32[]{:S(2)}) collective-permute-start(bf16[528,128]{1,0:T(8,128)(2,1)S(1)} %collective-permute-done.9.refs_4_.refs_5_), channel_id=1, source_target_pairs={{0,4},{1,5},{2,6},{3,7},{4,0},{5,1},{6,2},{7,3},{8,12},{9,13},{10,... | collective-permute-start | bytes 405512 | tf_op jit(solution)/shard_map/ppermute | solution.py:312
  51.8 10.4 %collective-permute-start.20 = (bf16[656,128]{1,0:T(8,128)(2,1)S(1)}, bf16[656,128]{1,0:T(8,128)(2,1)S(1)}, u32[]{:S(2)}, u32[]{:S(2)}) collective-permute-start(bf16[656,128]{1,0:T(8,128)(2,1)S(1)} %get-tuple-element.58.refs_1_.refs_0_.refs_2_), channel_id=1, source_target_pairs={{0,4},{1,5},{2,6},{3,7},{4,0},{5,1},{6,2},{7,3},{8,12},{9,13},{10,... | collective-permute-start | bytes 503816 | tf_op jit(solution)/shard_map/ppermute | solution.py:312
  56.1 10.7 %collective-permute-start.21 = (bf16[656,128]{1,0:T(8,128)(2,1)S(1)}, bf16[656,128]{1,0:T(8,128)(2,1)S(1)}, u32[]{:S(2)}, u32[]{:S(2)}) collective-permute-start(bf16[656,128]{1,0:T(8,128)(2,1)S(1)} %collective-permute-done.17.refs_2_.refs_1_.refs_3_), channel_id=1, source_target_pairs={{0,4},{1,5},{2,6},{3,7},{4,0},{5,1},{6,2},{7,3},{8,12},{9,13},{10,... | collective-permute-start | bytes 503816 | tf_op jit(solution)/shard_map/ppermute | solution.py:312
  57.8 9.0 %collective-permute-start.22 = (bf16[656,128]{1,0:T(8,128)(2,1)S(1)}, bf16[656,128]{1,0:T(8,128)(2,1)S(1)}, u32[]{:S(2)}, u32[]{:S(2)}) collective-permute-start(bf16[656,128]{1,0:T(8,128)(2,1)S(1)} %collective-permute-done.18.refs_3_.refs_2_.refs_4_), channel_id=1, source_target_pairs={{0,4},{1,5},{2,6},{3,7},{4,0},{5,1},{6,2},{7,3},{8,12},{9,13},{10,... | collective-permute-start | bytes 503816 | tf_op jit(solution)/shard_map/ppermute | solution.py:312
  58.1 11.6 %collective-permute-start.23 = (bf16[656,128]{1,0:T(8,128)(2,1)S(1)}, bf16[656,128]{1,0:T(8,128)(2,1)S(1)}, u32[]{:S(2)}, u32[]{:S(2)}) collective-permute-start(bf16[656,128]{1,0:T(8,128)(2,1)S(1)} %collective-permute-done.19.refs_4_.refs_3_.refs_5_), channel_id=1, source_target_pairs={{0,4},{1,5},{2,6},{3,7},{4,0},{5,1},{6,2},{7,3},{8,12},{9,13},{10,... | collective-permute-start | bytes 503816 | tf_op jit(solution)/shard_map/ppermute | solution.py:312
  95.9 9.0 %collective-permute-start.40 = (bf16[64,128]{1,0:T(8,128)(2,1)S(1)}, bf16[64,128]{1,0:T(8,128)(2,1)S(1)}, u32[]{:S(2)}, u32[]{:S(2)}) collective-permute-start(bf16[64,128]{1,0:T(8,128)(2,1)S(1)} %get-tuple-element.75), channel_id=1, source_target_pairs={{0,16},{8,24},{16,0},{24,8},{1,17},{9,25},{17,1},{25,9},{2,18},{10... | collective-permute-start | bytes 49160 | tf_op jit(solution)/shard_map/ppermute | solution.py:314
  98.0 8.6 %collective-permute-start.41 = (bf16[64,128]{1,0:T(8,128)(2,1)S(1)}, bf16[64,128]{1,0:T(8,128)(2,1)S(1)}, u32[]{:S(2)}, u32[]{:S(2)}) collective-permute-start(bf16[64,128]{1,0:T(8,128)(2,1)S(1)} %get-tuple-element.76), channel_id=1, source_target_pairs={{0,24},{8,16},{16,8},{24,0},{1,25},{9,17},{17,9},{25,1},{2,26},{10... | collective-permute-start | bytes 49160 | tf_op jit(solution)/shard_map/ppermute | solution.py:314
  99.8 6.8 %collective-permute-start.42 = (bf16[64,128]{1,0:T(8,128)(2,1)S(1)}, bf16[64,128]{1,0:T(8,128)(2,1)S(1)}, u32[]{:S(2)}, u32[]{:S(2)}) collective-permute-start(bf16[64,128]{1,0:T(8,128)(2,1)S(1)} %get-tuple-element.77), channel_id=1, source_target_pairs={{0,4},{1,5},{2,6},{3,7},{4,0},{5,1},{6,2},{7,3},{8,12},{9,13},{10,... | collective-permute-start | bytes 49160 | tf_op jit(solution)/shard_map/ppermute | solution.py:312
  (28 other events, 109.2 us)

commit v2 on v0

v2 whole, which is shorter than its diff:
```python
import functools

import jax
import jax.numpy as jnp
from jax import lax
from jax.experimental import pallas as pl
from jax.experimental.pallas import tpu as pltpu
from jax.sharding import PartitionSpec as P

BF16 = jnp.bfloat16
F32 = jnp.float32
NT = (((1,), (1,)), ((), ()))
TN = (((0,), (0,)), ((), ()))
SLICE_ROWS = 16


class Plan:
    def __init__(self, n_row, n_col, factor_tiles, right_sides):
        self.levels, self.tiles, self.block, _ = factor_tiles.shape
        self.rows_dev = right_sides.shape[1]
        self.vectors = right_sides.shape[3]
        self.n_row, self.n_col, self.chips = n_row, n_col, n_col // 2
        self.real = self.vectors // n_col
        self.slice = max(SLICE_ROWS, self.real)
        self.padded = self.slice * n_col
        self.lanes = self.rows_dev * self.block
        self.own = n_col * self.rows_dev
        self.blocks = n_row * self.own
        self.tile_rows = self.tiles // 2 * self.block
        self.index_at = self.tile_rows
        self.inverse_at = self.index_at + 16
        self.vmem_bytes = (24 if n_col <= 8 else 48) << 20

    def inverse_rows(self, level):
        return pl.ds(self.inverse_at + (level - 1) * self.block, self.block)

    def sides_at(self, level, core=0):
        start = self.inverse_at + self.levels * self.block
        return start + ((level - 1) * 2 + core) * self.slice

    def first_rows(self):
        return self.sides_at(self.levels + 1)

    def sources(self):
        return [2 * chip + core for core in range(2) for chip in range(self.chips)]


def call(plan, body, outs, args, scratch=(), scalars=1, raw=()):
    specs = [pl.BlockSpec(memory_space=pltpu.SMEM)] * scalars
    specs += [pl.BlockSpec(memory_space=pltpu.HBM if n in raw else pltpu.VMEM) for n in range(scalars, len(args))]
    return pl.pallas_call(
        functools.partial(body, plan),
        out_shape=outs,
        in_specs=specs,
        out_specs=[pl.BlockSpec(memory_space=pltpu.VMEM)] * len(outs),
        scratch_shapes=list(scratch),
        compiler_params=pltpu.CompilerParams(vmem_limit_bytes=plan.vmem_bytes),
    )(*args)


def take(refs, count):
    return [refs.pop(0) for _ in range(count)]


def low_lanes(shape, half):
    return lax.broadcasted_iota(jnp.int32, shape, len(shape) - 1) < half


def split_rows(value):
    high = value.astype(BF16)
    return jnp.concatenate([high, (value - high.astype(F32)).astype(BF16)], axis=0)


def apply_pair(inverse, value, half):
    n = value.shape[0]
    both = jnp.concatenate([value, pltpu.roll(value, half, 1)], axis=0)[:, :half]
    out = jnp.dot(split_rows(both), inverse, preferred_element_type=F32)
    out = out[: 2 * n] + out[2 * n :]
    return jnp.where(low_lanes((n, 2 * half), half), out[:n], out[n:])


def apply_pair_transposed(inverse, value, half):
    n = value.shape[0]
    low = low_lanes(value.shape, half)
    both = jnp.concatenate([jnp.where(low, value, 0.0), jnp.where(low, 0.0, value)], axis=0)
    out = lax.dot_general(split_rows(both), inverse, NT, preferred_element_type=F32)
    out = out[: 2 * n] + out[2 * n :]
    return jnp.concatenate([out[:n], out[n:]], axis=1)


def pad_slices(plan, value, out):
    if plan.real == plan.slice:
        out[...] = value.astype(out.dtype)
        return
    out[...] = jnp.zeros_like(out)
    for c in range(plan.n_col):
        out[c * plan.slice : c * plan.slice + plan.real, :] = value[c * plan.real : (c + 1) * plan.real].astype(out.dtype)


def drop_padding(plan, value):
    if plan.real == plan.slice:
        return value
    return jnp.concatenate([value[c * plan.slice : c * plan.slice + plan.real] for c in range(plan.n_col)], axis=0)


def store_halves(left, right, at, value, half):
    low = low_lanes(value.shape, half)
    other = pltpu.roll(value, half, 1)
    left[2 * at] = jnp.where(low, value, 0.0).astype(BF16)
    right[2 * at] = jnp.where(low, 0.0, other).astype(BF16)
    left[2 * at + 1] = jnp.where(low, other, 0.0).astype(BF16)
    right[2 * at + 1] = jnp.where(low, 0.0, value).astype(BF16)


def join_halves(left, right, at, half):
    first = left[2 * at] + pltpu.roll(right[2 * at], half, 1)
    second = right[2 * at + 1] + pltpu.roll(left[2 * at + 1], half, 1)
    return jnp.where(low_lanes(first.shape, half), first, second)


def first_kernel(plan, sides, inverse, solved, message, sides_here, inverse_here, sems):
    copies = [
        pltpu.make_async_copy(sides.at[0], sides_here, sems.at[0]),
        pltpu.make_async_copy(inverse.at[0], inverse_here, sems.at[1]),
    ]
    for copy in copies:
        copy.start()
    for copy in copies:
        copy.wait()
    parts = [
        lax.dot_general(sides_here[b], inverse_here[:, b * plan.block : (b + 1) * plan.block], TN,
                        precision=lax.Precision.HIGHEST, preferred_element_type=F32)
        for b in range(plan.rows_dev)
    ]
    pad_slices(plan, jnp.concatenate(parts, axis=1), solved)
    message[...] = solved[...].astype(BF16)


def pack_kernel(plan, place, rows, cols, *refs):
    refs = list(refs)
    tiles, sides, inverse = take(refs, 3)
    first = refs.pop(0)
    payloads = [None, take(refs, plan.chips)] + [[ref.at[0]] for ref in take(refs, plan.levels - 2)]
    tiles_here, sides_here, inverse_here, slices, sems = refs
    copies = [
        pltpu.make_async_copy(tiles, tiles_here, sems.at[0]),
        pltpu.make_async_copy(sides, sides_here, sems.at[1]),
        pltpu.make_async_copy(inverse, inverse_here, sems.at[2]),
    ]
    for copy in copies:
        copy.start()
    for copy in copies:
        copy.wait()
    half, width = plan.block, plan.slice
    lane = lax.broadcasted_iota(jnp.int32, (16, 128), 1)
    for coupling in range(plan.levels):
        targets = [first] if coupling == 0 else payloads[coupling]
        for k in range(plan.tiles // 2):
            pair = jnp.concatenate([tiles_here[coupling, 2 * k], tiles_here[coupling, 2 * k + 1]], axis=1)
            for target in targets:
                target[k * half : (k + 1) * half, :] = pair
        if coupling == 0:
            continue
        index = jnp.zeros((16, 128), F32)
        for t in range(plan.tiles):
            index = jnp.where(lane == t, rows[coupling, t, 0].astype(F32), index)
            index = jnp.where(lane == t + 64, cols[coupling, t, 0].astype(F32), index)
        for target in targets:
            target[plan.index_at : plan.index_at + 16, :] = index.astype(BF16)
        if coupling > 1:
            continue
        for level in range(1, plan.levels + 1):
            matrix = inverse_here[level].astype(BF16)
            both = jnp.concatenate([sides_here[level, b] for b in range(plan.rows_dev)], axis=0).T
            pad_slices(plan, both, slices)
            for chip, target in enumerate(targets):
                target[plan.inverse_rows(level), :] = matrix
                base = (place[1] ^ (2 * chip)) // 2 * 2
                for core in range(2):
                    here = pl.ds(pl.multiple_of((base + core) * width, 16), width)
                    start = plan.sides_at(level, core)
                    target[start : start + width, :] = slices[here, :]


def near_forward_kernel(plan, place, rows, cols, pairs, *refs):
    refs = list(refs)
    received = take(refs, plan.n_row)
    keep, send, left, right, total = refs
    half, width = plan.block, plan.slice
    for m in range(plan.n_row):
        store_halves(left, right, place[0] ^ m, received[m][...].astype(F32), half)
    total[...] = jnp.zeros_like(total)
    for k in range(plan.tiles // 2):
        pair = pairs[k * half : (k + 1) * half, :]
        vectors = jnp.concatenate([left[cols[0, 2 * k, 0]], right[cols[0, 2 * k + 1, 0]]], axis=0)
        product = lax.dot_general(vectors, pair, NT, preferred_element_type=F32)
        total[rows[0, 2 * k, 0]] += product[: plan.padded]
        total[rows[0, 2 * k + 1, 0]] += product[plan.padded :]
    for chip in range(plan.chips):
        for core, out in enumerate((keep, send)):
            number = place[1] ^ (2 * chip + core)
            here = pl.ds(pl.multiple_of(number * width, 16), width)
            for u in range(plan.n_col):
                value = jnp.concatenate([total[2 * u, here, :], total[2 * u + 1, here, :]], axis=1)
                out[chip, u] = value.astype(out.dtype)


def add_kernel(plan, keep, received, *out):
    for chip in range(plan.chips):
        out[chip][...] = (keep[chip] + received[chip].astype(F32)).astype(out[chip].dtype)


def near_backward_kernel(plan, place, rows, cols, pairs, *refs):
    refs = list(refs)
    received = take(refs, plan.n_col)
    out = take(refs, plan.n_row)
    upper, left, right = refs
    half, width = plan.block, plan.slice
    for piece, offset in zip(received, plan.sources()):
        here = pl.ds(pl.multiple_of((place[1] ^ offset) * width, 16), width)
        for u in range(plan.n_col):
            value = piece[u]
            upper[2 * u, here, :] = value[:, :half]
            upper[2 * u + 1, here, :] = value[:, half:]
    left[...] = jnp.zeros_like(left)
    right[...] = jnp.zeros_like(right)
    for k in range(plan.tiles // 2):
        pair = pairs[k * half : (k + 1) * half, :]
        vectors = jnp.concatenate([upper[rows[0, 2 * k, 0]], upper[rows[0, 2 * k + 1, 0]]], axis=0)
        product = jnp.dot(vectors, pair, preferred_element_type=F32)
        left[cols[0, 2 * k, 0]] += product[: plan.padded]
        right[cols[0, 2 * k + 1, 0]] += product[plan.padded :]
    for m in range(plan.n_row):
        out[m][...] = join_halves(left, right, place[0] ^ m, half).astype(out[m].dtype)


def last_kernel(plan, place, *refs):
    refs = list(refs)
    inverse, solved = take(refs, 2)
    shares = take(refs, plan.n_row)
    pieces = take(refs, plan.n_col)
    out, all_slices = refs
    half, width = plan.block, plan.slice
    core = place[1] & 1
    for piece, offset in zip(pieces, plan.sources()):
        here = pl.ds(pl.multiple_of((place[1] ^ offset) * width, 16), width)
        all_slices[0, here, :] = piece[place[1]]
        for n in range(1, plan.levels):
            all_slices[n, here, :] = piece[plan.n_col + core * (plan.levels - 1) + n - 1]
    for n in range(plan.levels):
        value = drop_padding(plan, all_slices[n].astype(F32)).T
        for b in range(plan.rows_dev):
            out[n + 1, b] = value[b * half : (b + 1) * half, :]
    back = shares[0][...]
    for share in shares[1:]:
        back = back + share[...].astype(F32)
    value = drop_padding(plan, solved[...] - back)
    for b in range(plan.rows_dev):
        cut = slice(b * half, (b + 1) * half)
        out[0, b] = lax.dot_general(inverse[0, :, cut], value[:, cut], NT,
                                    precision=lax.Precision.HIGHEST, preferred_element_type=F32)


def level_forward(plan, place, level, pieces, coupled, write):
    for piece, offset in zip(pieces, plan.sources()):
        u = place[1] ^ offset
        start = plan.sides_at(level) + (place[1] & 1) * plan.slice
        side = piece[pl.ds(pl.multiple_of(start, 16), plan.slice), :].astype(F32)
        write(piece, u, apply_pair(piece[plan.inverse_rows(level), :], side - coupled(u), plan.block))


def level_backward(plan, place, level, pieces, value, write):
    for piece, offset in zip(pieces, plan.sources()):
        u = place[1] ^ offset
        write(u, apply_pair_transposed(piece[plan.inverse_rows(level), :], value(u), plan.block))


def join_kernel(plan, first, second, out):
    count = first.shape[0]
    out[:count] = first[...]
    out[count:] = second[...]


def views(plan, refs):
    if len(refs) == plan.n_col:
        return refs
    return [ref.at[chip] for ref in refs for chip in range(plan.chips)]


def add_up(refs):
    def total(u):
        value = refs[0][u]
        for ref in refs[1:]:
            value = value + ref[u].astype(F32)
        return value

    return total


def enter_kernel(plan, place, *refs):
    refs = list(refs)
    pieces, sums = take(refs, plan.n_col), take(refs, plan.chips)
    solved, message = refs

    def write(piece, u, value):
        solved[u] = value
        message[u] = value.astype(BF16)

    level_forward(plan, place, 1, pieces, add_up(sums), write)


def decode(plan, place, pieces, index):
    lane = lax.broadcasted_iota(jnp.int32, (1, 128), 1)
    for p, offset in enumerate(plan.sources()):
        raw = pieces[p][plan.index_at : plan.index_at + 16, :].astype(F32).astype(jnp.int32)[0:1]
        owner = raw // plan.rows_dev * plan.n_col + (place[1] ^ offset)
        col = owner * plan.rows_dev + raw % plan.rows_dev
        index[p : p + 1, :] = jnp.where(lane < 64, raw, col)


def multiply_forward(plan, place, pieces, received, index, left, right, total, ready):
    half, width = plan.block, plan.slice
    for m in range(plan.n_row):
        for u in range(plan.n_col):
            store_halves(left, right, (place[0] ^ m) * plan.n_col + u, received[m][u].astype(F32), half)
    total[...] = jnp.zeros_like(total)
    ready()
    for p in range(plan.n_col):
        for k in range(plan.tiles // 2):
            pair = pieces[p][k * half : (k + 1) * half, :]
            vectors = jnp.concatenate([left[index[p, 2 * k + 64]], right[index[p, 2 * k + 65]]], axis=0)
            product = lax.dot_general(vectors, pair, NT, preferred_element_type=F32)
            total[index[p, 2 * k]] += product[:width]
            total[index[p, 2 * k + 1]] += product[width:]


def multiply_backward(plan, place, pieces, index, upper, left, right, out):
    half, width = plan.block, plan.slice
    for p in range(plan.n_col):
        for k in range(plan.tiles // 2):
            pair = pieces[p][k * half : (k + 1) * half, :]
            vectors = jnp.concatenate([upper[index[p, 2 * k]], upper[index[p, 2 * k + 1]]], axis=0)
            product = jnp.dot(vectors, pair, preferred_element_type=F32)
            left[index[p, 2 * k + 64]] += product[:width]
            right[index[p, 2 * k + 65]] += product[width:]
    for m in range(plan.n_row):
        for u in range(plan.n_col):
            at = (place[0] ^ m) * plan.n_col + u
            out[m][u] = join_halves(left, right, at, half).astype(out[m].dtype)


def put_upper(plan, upper, u, value):
    upper[2 * u] = value[:, : plan.block].astype(BF16)
    upper[2 * u + 1] = value[:, plan.block :].astype(BF16)


def forward_kernel(coupling, plan, place, *refs):
    refs = list(refs)
    last = coupling == plan.levels - 1
    solvers = take(refs, plan.n_col)
    pieces = solvers if coupling == 1 else views(plan, take(refs, 2))
    received = take(refs, plan.n_row)
    keep = refs.pop(0)
    if last:
        out = take(refs, plan.n_row)
    else:
        message, index_out = take(refs, 2)
    left, right, total, index, sem = take(refs, 5)
    if last:
        index_out, upper, back_left, back_right = refs
    decode(plan, place, pieces, index_out)
    copy = pltpu.make_async_copy(index_out, index, sem)
    copy.start()
    multiply_forward(plan, place, pieces, received, index, left, right, total, copy.wait)

    def coupled(u):
        return jnp.concatenate([total[2 * u], total[2 * u + 1]], axis=1)

    if not last:

        def write(piece, u, value):
            keep[u] = value
            message[u] = value.astype(BF16)

        level_forward(plan, place, coupling + 1, solvers, coupled, write)
        return
    back_left[...] = jnp.zeros_like(back_left)
    back_right[...] = jnp.zeros_like(back_right)

    def write_top(piece, u, value):
        value = apply_pair_transposed(piece[plan.inverse_rows(plan.levels), :], value, plan.block)
        keep[u] = value.astype(BF16)
        put_upper(plan, upper, u, value)

    level_forward(plan, place, plan.levels, solvers, coupled, write_top)
    multiply_backward(plan, place, pieces, index, upper, back_left, back_right, out)


def backward_kernel(level, plan, place, index, *refs):
    refs = list(refs)
    solvers = take(refs, plan.n_col)
    pieces = solvers if level == 2 else views(plan, take(refs, 2))
    shares = take(refs, plan.n_row)
    solved, keep = take(refs, 2)
    out = take(refs, plan.n_row)
    upper, left, right = refs
    left[...] = jnp.zeros_like(left)
    right[...] = jnp.zeros_like(right)
    back = add_up(shares)

    def write(u, value):
        keep[u] = value.astype(BF16)
        put_upper(plan, upper, u, value)

    level_backward(plan, place, level, solvers, lambda u: solved[u] - back(u), write)
    multiply_backward(plan, place, pieces, index, upper, left, right, out)


def leave_kernel(plan, place, *refs):
    refs = list(refs)
    pieces, shares = take(refs, plan.n_col), take(refs, plan.n_row)
    solved = refs.pop(0)
    above, out = take(refs, plan.levels - 1), refs
    back = add_up(shares)

    def write(u, value):
        for message in out:
            message[u] = value.astype(BF16)

    level_backward(plan, place, 1, pieces, lambda u: solved[u] - back(u), write)
    for chip, message in enumerate(out):
        base = (place[1] ^ (2 * chip)) // 2 * 2
        for core in range(2):
            for n, level in enumerate(above):
                message[plan.n_col + core * (plan.levels - 1) + n] = level[base + core]


def on_device(n_row, n_col, factor_tiles, tile_row, tile_col, right_sides, diag_inverse):
    plan = Plan(n_row, n_col, factor_tiles, right_sides)
    levels, chips = plan.levels, plan.chips
    place = jnp.stack([lax.axis_index("row"), lax.axis_index("col")]).astype(jnp.int32)

    def array(shape, kind=BF16):
        return jax.ShapeDtypeStruct(shape, kind)

    def over_row(value, m):
        return lax.ppermute(value, "row", [(i, i ^ m) for i in range(n_row)])

    def over_col(value, m):
        return lax.ppermute(value, "col", [(i, i ^ m) for i in range(n_col)])

    def exchange_row(values, order=1):
        got = {m: over_row(values[m], m) for m in range(1, n_row)[::order]}
        return [values[0]] + [got[m] for m in range(1, n_row)]

    def exchange_chips(values):
        return [values[0]] + [over_col(values[m], 2 * m) for m in range(1, chips)]

    def after(values, *others):
        return lax.optimization_barrier((values, others))[0]

    column = (plan.padded, plan.lanes)
    slices = (n_col, plan.slice, plan.lanes)
    dma = pltpu.SemaphoreType.DMA
    x0, message = call(
        plan, first_kernel, [array(column, F32), array(column)], (right_sides, diag_inverse),
        [pltpu.VMEM(right_sides.shape[1:], F32), pltpu.VMEM(diag_inverse.shape[1:], F32), dma((2,))],
        scalars=0, raw=(0, 1),
    )
    (message, place, tile_row, tile_col) = lax.optimization_barrier((message, place, tile_row, tile_col))
    received = exchange_row([message] * n_row)
    made = call(
        plan, pack_kernel,
        [array((plan.tile_rows, plan.lanes))]
        + [array((plan.first_rows(), plan.lanes))] * chips
        + [array((1, plan.inverse_at, plan.lanes)) for s in range(2, levels)],
        (place, tile_row, tile_col, factor_tiles, right_sides, diag_inverse),
        [pltpu.VMEM(factor_tiles.shape, BF16), pltpu.VMEM(right_sides.shape, F32),
         pltpu.VMEM(diag_inverse.shape, F32), pltpu.VMEM(column, BF16), dma((3,))],
        scalars=3, raw=(3, 4, 5),
    )
    pairs = made[0]
    payloads = [None, list(made[1 : 1 + chips])] + list(made[1 + chips :])

    def swap_cores(values):
        return [over_col(value, 1) for value in values]

    gathered = exchange_chips(after(payloads[1], received))
    near, late = gathered[:3], gathered[3:]
    keep, send = call(
        plan, near_forward_kernel, [array((chips,) + slices, F32), array((chips,) + slices)],
        [place, tile_row, tile_col, pairs] + received,
        [pltpu.VMEM((n_row * plan.rows_dev,) + column, BF16), pltpu.VMEM((n_row * plan.rows_dev,) + column, BF16),
         pltpu.VMEM((plan.own, plan.padded, plan.block), F32)],
        scalars=3,
    )
    near, send = lax.optimization_barrier((near, send))
    swapped, far = over_col(send, 1), swap_cores(near)
    swapped, near, far = lax.optimization_barrier((swapped, near, far))
    sums = call(plan, add_kernel, [array(slices, F32)] + [array(slices)] * (chips - 1), [keep, swapped], scalars=0)
    sums = exchange_chips(sums)
    first = near + late + far + swap_cores(late)
    solved, message = call(
        plan, enter_kernel, [array(slices, F32), array(slices)], [place] + first + sums
    )
    solved = [None, solved]

    index_shape = (max(8, n_col), 128)
    forward = [
        pltpu.VMEM((plan.blocks, plan.slice, plan.lanes), BF16),
        pltpu.VMEM((plan.blocks, plan.slice, plan.lanes), BF16),
        pltpu.VMEM((plan.own, plan.slice, plan.block), F32),
        pltpu.SMEM(index_shape, jnp.int32),
        dma(()),
    ]
    backward = [
        pltpu.VMEM((plan.own, plan.slice, plan.block), BF16),
        pltpu.VMEM((plan.blocks, plan.slice, plan.lanes), F32),
        pltpu.VMEM((plan.blocks, plan.slice, plan.lanes), F32),
    ]
    partial = [array(slices, F32)] + [array(slices)] * (n_row - 1)
    index = [None] * levels
    def double(held, step):
        other = over_col(held, 2 * step)
        return call(plan, join_kernel, [array((2 * step,) + held.shape[1:])], [held, other], scalars=0)[0]

    pieces = [None, []]
    for s in range(1, levels):
        if s + 1 < levels:
            held, step = double(after(payloads[s + 1], message), 1) if chips > 1 else payloads[s + 1], 2
        received = exchange_row([message] * n_row)
        if s + 1 < levels:
            held = after(held, received)
            while step < chips:
                held, step = double(held, step), 2 * step
        args = [place] + first + pieces[s] + received
        if s < levels - 1:
            value, message, index[s] = call(
                plan, functools.partial(forward_kernel, s),
                [array(slices, F32), array(slices), array(index_shape, jnp.int32)], args, forward,
            )
            solved.append(value)
            pieces.append([held, over_col(after(held, message), 1)])
        else:
            made = call(
                plan, functools.partial(forward_kernel, s), [array(slices)] + partial, args,
                forward + [pltpu.VMEM(index_shape, jnp.int32)] + backward,
            )
    results = [made[0]]
    shares = exchange_row(made[1:], -1)
    for level in range(levels - 1, 1, -1):
        made = call(
            plan, functools.partial(backward_kernel, level), [array(slices)] + partial,
            [place, index[level - 1]] + first + pieces[level - 1] + shares + [solved[level]],
            backward, scalars=2,
        )
        results.insert(0, made[0])
        shares = exchange_row(made[1:], -1)
    messages = call(
        plan, leave_kernel, [array((n_col + 2 * (levels - 1),) + slices[1:])] * chips,
        [place] + first + shares + [solved[1]] + results,
    )
    messages = exchange_chips(messages)
    messages = messages + swap_cores(messages)
    shares = call(
        plan, near_backward_kernel, [array(column, F32)] + [array(column)] * (n_row - 1),
        [place, tile_row, tile_col, pairs] + messages,
        [pltpu.VMEM((plan.own, plan.padded, plan.block), BF16),
         pltpu.VMEM((n_row * plan.rows_dev,) + column, F32), pltpu.VMEM((n_row * plan.rows_dev,) + column, F32)],
        scalars=3,
    )
    shares = exchange_row(shares, -1)
    return call(
        plan, last_kernel, [array(right_sides.shape, F32)], [place, diag_inverse, x0] + shares + messages,
        [pltpu.VMEM((levels,) + column, BF16)],
    )[0]


def solution(mesh):
    return jax.shard_map(
        functools.partial(on_device, mesh.shape["row"], mesh.shape["col"]),
        mesh=mesh,
        in_specs=(
            P(None, "row", None, "col"),
            P(None, "row", "col"),
            P(None, "row", "col"),
            P(None, ("col", "row"), None, None),
            P(None, None, ("col", "row")),
        ),
        out_specs=P(None, ("col", "row"), None, None),
        check_vma=False,
    )
```

time: 262 us -> 97 us (0.37)
  waiting for transfers between devices: 153 us -> 34.6 us
  blocking collectives: 69.9 us -> 0 us
  starting transfers between devices: 0.21 us -> 42 us
  Pallas kernels: 0 us -> 16.8 us
  between operations: 13.7 us -> 0.2 us
  matrix products: 11.1 us -> 0 us
  local copies, waits for them, and re-layouts: 11.1 us -> 3.14 us
    reduce_scatter x6 -> x0, waiting for transfers between devices: 153 us -> none  [the longest x3 101 us: solve_all(): lax.psum_scatter(term(jnp.int32(0), lax.axis_size('col') * rows_dev).asty...]
    all_gather x6 -> x0, blocking collectives: 69.9 us -> none  [the longest x3 42 us: solve_all(): lax.all_gather(current.astype(jnp.bfloat16), 'row', axis=0, tiled=True)]
    ppermute x0 -> x39, starting transfers between devices: none -> 42 us  [the longest x18 27.9 us: over_row(): return lax.ppermute(value, 'row', [(i, i ^ m) for i in range(n_row)])]
    ppermute x0 -> x39, waiting for transfers between devices: none -> 34.6 us  [the longest x18 19 us: over_row(): return lax.ppermute(value, 'row', [(i, i ^ m) for i in range(n_row)])]
    pallas_call x0 -> x13, Pallas kernels: none -> 16.8 us  [call(): pl.pallas_call(functools.partial(body, plan), out_shape=outs, in_specs=sp...]
    dot_general x20 -> x0, matrix products: 11.1 us -> none  [the longest x4 3.32 us: apply_inverse(): jnp.einsum('cir,irn->icn', matrix, vector, precision=lax.Precision.HIGHEST)]
    gather x6 -> x0, local copies, waits for them, and re-layouts: 3.49 us -> none  [the longest x3 1.75 us: solve_all(): picked = gathered[col_ids[section_no - 1]]]
  transfers between devices with their start and end apart: 6 -> 39, of which waited for: 6 -> 23; matrix products, arithmetic and copies ran while one was open for 0% -> 0% of each run, Pallas kernels for 0% -> 6%
where the time goes in v2:
time: 97 us; the launch traced here: 96.8 us
  starting transfers between devices  42 us (43%)
  waiting for transfers between devices  34.6 us (36%)
  Pallas kernels  16.8 us (17%)
  local copies, waits for them, and re-layouts  3.14 us (3%)
    ppermute x18, starting transfers between devices, over_row(): return lax.ppermute(value, 'row', [(i, i ^ m) for i in range(n_row)])  27.9 us
    ppermute x18, waiting for transfers between devices, over_row(): return lax.ppermute(value, 'row', [(i, i ^ m) for i in range(n_row)])  19 us
    pallas_call x13, Pallas kernels, call(): pl.pallas_call(functools.partial(body, plan), out_shape=outs, in_specs=sp...  16.8 us
    ppermute x21, waiting for transfers between devices, over_col(): return lax.ppermute(value, 'col', [(i, i ^ m) for i in range(n_col)])  15.6 us
    ppermute x21, starting transfers between devices, over_col(): return lax.ppermute(value, 'col', [(i, i ^ m) for i in range(n_col)])  14 us
    unnamed x14, local copies, waits for them, and re-layouts  2.93 us
  transfers between devices with their start and end apart: 39, of which 23 were waited for; matrix products, arithmetic and copies ran while one was open for 0% of the time, Pallas kernels for 6%

profile of v2, /device:TPU:0, one launch (start us, length us, event | category | flops | bytes accessed | tf_op | source)
XLA Modules:
  0.0 96.8 jit_solution(3345265740695654220)
XLA Ops:
  2.5 5.1 %collective-permute-start.2 = (bf16[128,128]{1,0:T(8,128)(2,1)S(1)}, bf16[128,128]{1,0:T(8,128)(2,1)S(1)}, u32[]{:S(2)}, u32[]{:S(2)}) collective-permute-start(bf16[128,128]{1,0:T(8,128)(2,1)S(1)} %get-tuple-element.74.refs_0_), channel_id=1, source_target_pairs={{0,24},{8,16},{16,8},{24,0},{1,25},{9,17},{17,9},{25,1},{2,26},{10... | collective-permute-start | bytes 98312 | tf_op jit(solution)/shard_map/ppermute | solution.py:447
  9.5 1.9 %shard_map.56 = (bf16[384,128]{1,0:T(8,128)(2,1)S(1)}, bf16[688,128]{1,0:T(8,128)(2,1)S(1)}, bf16[688,128]{1,0:T(8,128)(2,1)S(1)}, bf16[688,128]{1,0:T(8,128)(2,...) custom-call(s32[2]{0:T(128)S(1)} %pad_add_fusion.place, s32[3,12,1]{2,1,0:T(8,128)S(1)} %copy.10.rows, ...), custom_call_target="tpu_custom_call" | custom-call | tf_op jit(solution)/shard_map/pallas_call | solution.py:51
  15.9 1.9 %shard_map.57 = (f32[4,8,16,128]{3,2,1,0:T(8,128)S(1)}, bf16[4,8,16,128]{3,2,1,0:T(8,128)(2,1)S(1)}) custom-call(s32[2]{0:T(128)S(1)} %pad_add_fusion.place, s32[3,12,1]{2,1,0:T(8,128)S(1)} %copy.10.rows, s32[3,12,1]{2,1,0:T(8,128)S(1)} %copy.11.cols, bf16[384,128]{1,0:T(8,128)(2,1)S(1)} %get-tuple-element.69.pairs, ...), custom_call_target="tpu_custom_call" | custom-call | tf_op jit(solution)/shard_map/pallas_call | solution.py:51
  17.8 1.8 %collective-permute-done.3.refs_1_ = bf16[688,128]{1,0:T(8,128)(2,1)S(1)} collective-permute-done((bf16[688,128]{1,0:T(8,128)(2,1)S(1)}, bf16[688,128]{1,0:T(8,128)(2,1)S(1)}, u32[]{:S(2)}, u32[]{:S(2)}) %collective-permute-start.3) | collective-permute-done | bytes 176160 | tf_op jit(solution)/shard_map/ppermute | solution.py:450
  19.6 3.1 %collective-permute-done.4.refs_2_ = bf16[688,128]{1,0:T(8,128)(2,1)S(1)} collective-permute-done((bf16[688,128]{1,0:T(8,128)(2,1)S(1)}, bf16[688,128]{1,0:T(8,128)(2,1)S(1)}, u32[]{:S(2)}, u32[]{:S(2)}) %collective-permute-start.4) | collective-permute-done | bytes 176160 | tf_op jit(solution)/shard_map/ppermute | solution.py:450
  26.7 2.0 %collective-permute-start.13 = (bf16[8,16,128]{2,1,0:T(8,128)(2,1)S(1)}, bf16[8,16,128]{2,1,0:T(8,128)(2,1)S(1)}, u32[]{:S(2)}, u32[]{:S(2)}) collective-permute-start(bf16[8,16,128]{2,1,0:T(8,128)(2,1)S(1)} %get-tuple-element.95), channel_id=1, source_target_pairs={{0,6},{1,7},{2,4},{3,5},{4,2},{5,3},{6,0},{7,1},{8,14},{9,15},{10,... | collective-permute-start | bytes 98312 | tf_op jit(solution)/shard_map/ppermute | solution.py:450
  29.2 2.4 %collective-permute-done.13.refs_11_ = bf16[8,16,128]{2,1,0:T(8,128)(2,1)S(1)} collective-permute-done((bf16[8,16,128]{2,1,0:T(8,128)(2,1)S(1)}, bf16[8,16,128]{2,1,0:T(8,128)(2,1)S(1)}, u32[]{:S(2)}, u32[]{:S(2)}) %collective-permute-start.13) | collective-permute-done | bytes 32800 | tf_op jit(solution)/shard_map/ppermute | solution.py:450
  33.9 3.4 %collective-permute-start.16 = (bf16[8,16,128]{2,1,0:T(8,128)(2,1)S(1)}, bf16[8,16,128]{2,1,0:T(8,128)(2,1)S(1)}, u32[]{:S(2)}, u32[]{:S(2)}) collective-permute-start(bf16[8,16,128]{2,1,0:T(8,128)(2,1)S(1)} %get-tuple-element.96.refs_8_), channel_id=1, source_target_pairs={{0,24},{8,16},{16,8},{24,0},{1,25},{9,17},{17,9},{25,1},{2,26},{10... | collective-permute-start | bytes 98312 | tf_op jit(solution)/shard_map/ppermute | solution.py:447
  39.6 2.5 %collective-permute-done.15.refs_10_ = bf16[8,16,128]{2,1,0:T(8,128)(2,1)S(1)} collective-permute-done((bf16[8,16,128]{2,1,0:T(8,128)(2,1)S(1)}, bf16[8,16,128]{2,1,0:T(8,128)(2,1)S(1)}, u32[]{:S(2)}, u32[]{:S(2)}) %collective-permute-start.15) | collective-permute-done | bytes 32800 | tf_op jit(solution)/shard_map/ppermute | solution.py:447
  42.9 2.2 %shard_map.60 = (f32[8,16,128]{2,1,0:T(8,128)S(1)}, bf16[8,16,128]{2,1,0:T(8,128)(2,1)S(1)}, s32[8,128]{1,0:T(8,128)S(1)}) custom-call(s32[2]{0:T(128)S(1)} %pad_add_fusion.place, bf16[688,128]{1,0:T(8,128)(2,1)S(1)} %get-tuple-element.83.refs_0_, bf16[688,128]{1,0:T(8,128)(2,1)S(1)} %collective-permute-done.3.refs_1_, ...), custom_call_target="tpu_custom_call" | custom-call | tf_op jit(solution)/shard_map/pallas_call | solution.py:51
  45.1 2.8 %collective-permute-done.18.second = bf16[2,400,128]{2,1,0:T(8,128)(2,1)S(1)} collective-permute-done((bf16[2,400,128]{2,1,0:T(8,128)(2,1)S(1)}, bf16[2,400,128]{2,1,0:T(8,128)(2,1)S(1)}, u32[]{:S(2)}, u32[]{:S(2)}) %collective-permute-start.18) | collective-permute-done | bytes 204832 | tf_op jit(solution)/shard_map/ppermute | solution.py:450
  50.2 2.3 %collective-permute-start.20 = (bf16[8,16,128]{2,1,0:T(8,128)(2,1)S(1)}, bf16[8,16,128]{2,1,0:T(8,128)(2,1)S(1)}, u32[]{:S(2)}, u32[]{:S(2)}) collective-permute-start(bf16[8,16,128]{2,1,0:T(8,128)(2,1)S(1)} %get-tuple-element.101.refs_10_), channel_id=1, source_target_pairs={{0,8},{8,0},{16,24},{24,16},{1,9},{9,1},{17,25},{25,17},{2,10},{10... | collective-permute-start | bytes 98312 | tf_op jit(solution)/shard_map/ppermute | solution.py:447
  55.0 3.5 %shard_map.63 = (bf16[8,16,128]{2,1,0:T(8,128)(2,1)S(1)}, f32[8,16,128]{2,1,0:T(8,128)S(1)}, bf16[8,16,128]{2,1,0:T(8,128)(2,1)S(1)}, bf16[8,16,128]{2,1,0:T(8,128)(2,1)S(1)}, bf16[8,16,128]{2,1,0:T(8,128)(2,1)S(1)}) custom-call(s32[2]{0:T(128)S(1)} %pad_add_fusion.place, bf16[688,128]{1,0:T(8,128)(2,1)S(1)} %get-tuple-element.83.refs_0_, ...), custom_call_target="tpu_custom_call" | custom-call | tf_op jit(solution)/shard_map/pallas_call | solution.py:51
  61.3 1.7 %collective-permute-start.25 = (bf16[8,16,128]{2,1,0:T(8,128)(2,1)S(1)}, bf16[8,16,128]{2,1,0:T(8,128)(2,1)S(1)}, u32[]{:S(2)}, u32[]{:S(2)}) collective-permute-start(bf16[8,16,128]{2,1,0:T(8,128)(2,1)S(1)} %get-tuple-element.106), channel_id=1, source_target_pairs={{0,24},{8,16},{16,8},{24,0},{1,25},{9,17},{17,9},{25,1},{2,26},{10... | collective-permute-start | bytes 98312 | tf_op jit(solution)/shard_map/ppermute | solution.py:447
  63.0 2.5 %collective-permute-done.24.refs_10_ = bf16[8,16,128]{2,1,0:T(8,128)(2,1)S(1)} collective-permute-done((bf16[8,16,128]{2,1,0:T(8,128)(2,1)S(1)}, bf16[8,16,128]{2,1,0:T(8,128)(2,1)S(1)}, u32[]{:S(2)}, u32[]{:S(2)}) %collective-permute-start.24) | collective-permute-done | bytes 32800 | tf_op jit(solution)/shard_map/ppermute | solution.py:447
  68.7 2.2 %collective-permute-start.27 = (bf16[8,16,128]{2,1,0:T(8,128)(2,1)S(1)}, bf16[8,16,128]{2,1,0:T(8,128)(2,1)S(1)}, u32[]{:S(2)}, u32[]{:S(2)}) collective-permute-start(bf16[8,16,128]{2,1,0:T(8,128)(2,1)S(1)} %get-tuple-element.110), channel_id=1, source_target_pairs={{0,16},{8,24},{16,0},{24,8},{1,17},{9,25},{17,1},{25,9},{2,18},{10... | collective-permute-start | bytes 98312 | tf_op jit(solution)/shard_map/ppermute | solution.py:447
  70.8 2.2 %collective-permute-start.28 = (bf16[8,16,128]{2,1,0:T(8,128)(2,1)S(1)}, bf16[8,16,128]{2,1,0:T(8,128)(2,1)S(1)}, u32[]{:S(2)}, u32[]{:S(2)}) collective-permute-start(bf16[8,16,128]{2,1,0:T(8,128)(2,1)S(1)} %get-tuple-element.111), channel_id=1, source_target_pairs={{0,24},{8,16},{16,8},{24,0},{1,25},{9,17},{17,9},{25,1},{2,26},{10... | collective-permute-start | bytes 98312 | tf_op jit(solution)/shard_map/ppermute | solution.py:447
  73.9 2.7 %collective-permute-done.28.refs_11_ = bf16[8,16,128]{2,1,0:T(8,128)(2,1)S(1)} collective-permute-done((bf16[8,16,128]{2,1,0:T(8,128)(2,1)S(1)}, bf16[8,16,128]{2,1,0:T(8,128)(2,1)S(1)}, u32[]{:S(2)}, u32[]{:S(2)}) %collective-permute-start.28) | collective-permute-done | bytes 32800 | tf_op jit(solution)/shard_map/ppermute | solution.py:447
  78.4 2.5 %collective-permute-start.31 = (bf16[12,16,128]{2,1,0:T(8,128)(2,1)S(1)}, bf16[12,16,128]{2,1,0:T(8,128)(2,1)S(1)}, u32[]{:S(2)}, u32[]{:S(2)}) collective-permute-start(bf16[12,16,128]{2,1,0:T(8,128)(2,1)S(1)} %get-tuple-element.118), channel_id=1, source_target_pairs={{0,6},{1,7},{2,4},{3,5},{4,2},{5,3},{6,0},{7,1},{8,14},{9,15},{10,... | collective-permute-start | bytes 147464 | tf_op jit(solution)/shard_map/ppermute | solution.py:450
  84.6 2.0 %shard_map.66 = (f32[128,128]{1,0:T(8,128)S(1)}, bf16[128,128]{1,0:T(8,128)(2,1)S(1)}, bf16[128,128]{1,0:T(8,128)(2,1)S(1)}, bf16[128,128]{1,0:T(8,128)(2,1)S(1)}) custom-call(s32[2]{0:T(128)S(1)} %pad_add_fusion.place, s32[3,12,1]{2,1,0:T(8,128)S(1)} %copy.10.rows, s32[3,12,1]{2,1,0:T(8,128)S(1)} %copy.11.cols, ...), custom_call_target="tpu_custom_call" | custom-call | tf_op jit(solution)/shard_map/pallas_call | solution.py:51
  86.7 2.7 %collective-permute-start.37 = (bf16[128,128]{1,0:T(8,128)(2,1)S(1)}, bf16[128,128]{1,0:T(8,128)(2,1)S(1)}, u32[]{:S(2)}, u32[]{:S(2)}) collective-permute-start(bf16[128,128]{1,0:T(8,128)(2,1)S(1)} %get-tuple-element.121), channel_id=1, source_target_pairs={{0,16},{8,24},{16,0},{24,8},{1,17},{9,25},{17,1},{25,9},{2,18},{10... | collective-permute-start | bytes 98312 | tf_op jit(solution)/shard_map/ppermute | solution.py:447
  89.4 1.6 %collective-permute-start.38 = (bf16[128,128]{1,0:T(8,128)(2,1)S(1)}, bf16[128,128]{1,0:T(8,128)(2,1)S(1)}, u32[]{:S(2)}, u32[]{:S(2)}) collective-permute-start(bf16[128,128]{1,0:T(8,128)(2,1)S(1)} %get-tuple-element.122), channel_id=1, source_target_pairs={{0,24},{8,16},{16,8},{24,0},{1,25},{9,17},{17,9},{25,1},{2,26},{10... | collective-permute-start | bytes 98312 | tf_op jit(solution)/shard_map/ppermute | solution.py:447
  92.1 3.1 %collective-permute-done.38.refs_5_ = bf16[128,128]{1,0:T(8,128)(2,1)S(1)} collective-permute-done((bf16[128,128]{1,0:T(8,128)(2,1)S(1)}, bf16[128,128]{1,0:T(8,128)(2,1)S(1)}, u32[]{:S(2)}, u32[]{:S(2)}) %collective-permute-start.38) | collective-permute-done | bytes 32800 | tf_op jit(solution)/shard_map/ppermute | solution.py:447
  95.2 1.7 %shard_map.67 = f32[4,2,64,128]{3,2,1,0:T(8,128)} custom-call(s32[2]{0:T(128)S(1)} %pad_add_fusion.place, f32[4,64,128]{2,1,0:T(8,128)S(1)} %copy-done.1, f32[128,128]{1,0:T(8,128)S(1)} %get-tuple-element.66.refs_1_, f32[128,128]{1,0:T(8,128)S(1)} %get-tuple-element.119.refs_2_, bf16[128,128]{1,0:T(8,128)(2,1)S(1)} %collective-permute-done.36.refs_3_, ...), custom_call_target="tpu_custom_call" | custom-call | tf_op jit(solution)/shard_map/pallas_call | solution.py:51
  (84 shorter events, 37.0 us)
Async XLA Ops:
  2.5 9.0 %collective-permute-start.2 = (bf16[128,128]{1,0:T(8,128)(2,1)S(1)}, bf16[128,128]{1,0:T(8,128)(2,1)S(1)}, u32[]{:S(2)}, u32[]{:S(2)}) collective-permute-start(bf16[128,128]{1,0:T(8,128)(2,1)S(1)} %get-tuple-element.74.refs_0_), channel_id=1, source_target_pairs={{0,24},{8,16},{16,8},{24,0},{1,25},{9,17},{17,9},{25,1},{2,26},{10... | collective-permute-start | bytes 98312 | tf_op jit(solution)/shard_map/ppermute | solution.py:447
  7.6 4.8 %collective-permute-start.1 = (bf16[128,128]{1,0:T(8,128)(2,1)S(1)}, bf16[128,128]{1,0:T(8,128)(2,1)S(1)}, u32[]{:S(2)}, u32[]{:S(2)}) collective-permute-start(bf16[128,128]{1,0:T(8,128)(2,1)S(1)} %get-tuple-element.74.refs_0_), channel_id=1, source_target_pairs={{0,16},{8,24},{16,0},{24,8},{1,17},{9,25},{17,1},{25,9},{2,18},{10... | collective-permute-start | bytes 98312 | tf_op jit(solution)/shard_map/ppermute | solution.py:447
  7.6 4.8 %collective-permute-start = (bf16[128,128]{1,0:T(8,128)(2,1)S(1)}, bf16[128,128]{1,0:T(8,128)(2,1)S(1)}, u32[]{:S(2)}, u32[]{:S(2)}) collective-permute-start(bf16[128,128]{1,0:T(8,128)(2,1)S(1)} %get-tuple-element.74.refs_0_), channel_id=1, source_target_pairs={{0,8},{8,0},{16,24},{24,16},{1,9},{9,1},{17,25},{25,17},{2,10},{10... | collective-permute-start | bytes 98312 | tf_op jit(solution)/shard_map/ppermute | solution.py:447
  12.4 7.2 %collective-permute-start.3 = (bf16[688,128]{1,0:T(8,128)(2,1)S(1)}, bf16[688,128]{1,0:T(8,128)(2,1)S(1)}, u32[]{:S(2)}, u32[]{:S(2)}) collective-permute-start(bf16[688,128]{1,0:T(8,128)(2,1)S(1)} %get-tuple-element.76), channel_id=1, source_target_pairs={{0,2},{1,3},{2,0},{3,1},{4,6},{5,7},{6,4},{7,5},{8,10},{9,11},{10,... | collective-permute-start | bytes 528392 | tf_op jit(solution)/shard_map/ppermute | solution.py:450
  13.9 8.8 %collective-permute-start.4 = (bf16[688,128]{1,0:T(8,128)(2,1)S(1)}, bf16[688,128]{1,0:T(8,128)(2,1)S(1)}, u32[]{:S(2)}, u32[]{:S(2)}) collective-permute-start(bf16[688,128]{1,0:T(8,128)(2,1)S(1)} %get-tuple-element.77), channel_id=1, source_target_pairs={{0,4},{1,5},{2,6},{3,7},{4,0},{5,1},{6,2},{7,3},{8,12},{9,13},{10,... | collective-permute-start | bytes 528392 | tf_op jit(solution)/shard_map/ppermute | solution.py:450
  15.4 7.8 %collective-permute-start.9 = (bf16[688,128]{1,0:T(8,128)(2,1)S(1)}, bf16[688,128]{1,0:T(8,128)(2,1)S(1)}, u32[]{:S(2)}, u32[]{:S(2)}) collective-permute-start(bf16[688,128]{1,0:T(8,128)(2,1)S(1)} %get-tuple-element.86), channel_id=1, source_target_pairs={{0,6},{1,7},{2,4},{3,5},{4,2},{5,3},{6,0},{7,1},{8,14},{9,15},{10,... | collective-permute-start | bytes 528392 | tf_op jit(solution)/shard_map/ppermute | solution.py:450
  23.2 5.5 %collective-permute-start.10 = (bf16[688,128]{1,0:T(8,128)(2,1)S(1)}, bf16[688,128]{1,0:T(8,128)(2,1)S(1)}, u32[]{:S(2)}, u32[]{:S(2)}) collective-permute-start(bf16[688,128]{1,0:T(8,128)(2,1)S(1)} %collective-permute-done.9.refs_3_), channel_id=1, source_target_pairs={{0,1},{1,0},{2,3},{3,2},{4,5},{5,4},{6,7},{7,6},{8,9},{9,8},{10,11... | collective-permute-start | bytes 528392 | tf_op jit(solution)/shard_map/ppermute | solution.py:450
  26.7 4.8 %collective-permute-start.13 = (bf16[8,16,128]{2,1,0:T(8,128)(2,1)S(1)}, bf16[8,16,128]{2,1,0:T(8,128)(2,1)S(1)}, u32[]{:S(2)}, u32[]{:S(2)}) collective-permute-start(bf16[8,16,128]{2,1,0:T(8,128)(2,1)S(1)} %get-tuple-element.95), channel_id=1, source_target_pairs={{0,6},{1,7},{2,4},{3,5},{4,2},{5,3},{6,0},{7,1},{8,14},{9,15},{10,... | collective-permute-start | bytes 98312 | tf_op jit(solution)/shard_map/ppermute | solution.py:450
  32.3 6.0 %collective-permute-start.17 = (bf16[1,400,128]{2,1,0:T(8,128)(2,1)S(1)}, bf16[1,400,128]{2,1,0:T(8,128)(2,1)S(1)}, u32[]{:S(2)}, u32[]{:S(2)}) collective-permute-start(bf16[1,400,128]{2,1,0:T(8,128)(2,1)S(1)} %get-tuple-element.99.first), channel_id=1, source_target_pairs={{0,2},{1,3},{2,0},{3,1},{4,6},{5,7},{6,4},{7,5},{8,10},{9,11},{10,... | collective-permute-start | bytes 307208 | tf_op jit(solution)/shard_map/ppermute | solution.py:450
  33.9 5.7 %collective-permute-start.16 = (bf16[8,16,128]{2,1,0:T(8,128)(2,1)S(1)}, bf16[8,16,128]{2,1,0:T(8,128)(2,1)S(1)}, u32[]{:S(2)}, u32[]{:S(2)}) collective-permute-start(bf16[8,16,128]{2,1,0:T(8,128)(2,1)S(1)} %get-tuple-element.96.refs_8_), channel_id=1, source_target_pairs={{0,24},{8,16},{16,8},{24,0},{1,25},{9,17},{17,9},{25,1},{2,26},{10... | collective-permute-start | bytes 98312 | tf_op jit(solution)/shard_map/ppermute | solution.py:447
  37.3 4.8 %collective-permute-start.15 = (bf16[8,16,128]{2,1,0:T(8,128)(2,1)S(1)}, bf16[8,16,128]{2,1,0:T(8,128)(2,1)S(1)}, u32[]{:S(2)}, u32[]{:S(2)}) collective-permute-start(bf16[8,16,128]{2,1,0:T(8,128)(2,1)S(1)} %get-tuple-element.96.refs_8_), channel_id=1, source_target_pairs={{0,16},{8,24},{16,0},{24,8},{1,17},{9,25},{17,1},{25,9},{2,18},{10... | collective-permute-start | bytes 98312 | tf_op jit(solution)/shard_map/ppermute | solution.py:447
  37.3 4.8 %collective-permute-start.14 = (bf16[8,16,128]{2,1,0:T(8,128)(2,1)S(1)}, bf16[8,16,128]{2,1,0:T(8,128)(2,1)S(1)}, u32[]{:S(2)}, u32[]{:S(2)}) collective-permute-start(bf16[8,16,128]{2,1,0:T(8,128)(2,1)S(1)} %get-tuple-element.96.refs_8_), channel_id=1, source_target_pairs={{0,8},{8,0},{16,24},{24,16},{1,9},{9,1},{17,25},{25,17},{2,10},{10... | collective-permute-start | bytes 98312 | tf_op jit(solution)/shard_map/ppermute | solution.py:447
  42.2 5.8 %collective-permute-start.18 = (bf16[2,400,128]{2,1,0:T(8,128)(2,1)S(1)}, bf16[2,400,128]{2,1,0:T(8,128)(2,1)S(1)}, u32[]{:S(2)}, u32[]{:S(2)}) collective-permute-start(bf16[2,400,128]{2,1,0:T(8,128)(2,1)S(1)} %shard_map.61.first), channel_id=1, source_target_pairs={{0,4},{1,5},{2,6},{3,7},{4,0},{5,1},{6,2},{7,3},{8,12},{9,13},{10,... | collective-permute-start | bytes 614408 | tf_op jit(solution)/shard_map/ppermute | solution.py:450
  47.9 7.1 %collective-permute-start.19 = (bf16[4,400,128]{2,1,0:T(8,128)(2,1)S(1)}, bf16[4,400,128]{2,1,0:T(8,128)(2,1)S(1)}, u32[]{:S(2)}, u32[]{:S(2)}) collective-permute-start(bf16[4,400,128]{2,1,0:T(8,128)(2,1)S(1)} %shard_map.62.refs_8_), channel_id=1, source_target_pairs={{0,1},{1,0},{2,3},{3,2},{4,5},{5,4},{6,7},{7,6},{8,9},{9,8},{10,11... | collective-permute-start | bytes 1228808 | tf_op jit(solution)/shard_map/ppermute | solution.py:450
  48.0 5.8 %collective-permute-start.22 = (bf16[8,16,128]{2,1,0:T(8,128)(2,1)S(1)}, bf16[8,16,128]{2,1,0:T(8,128)(2,1)S(1)}, u32[]{:S(2)}, u32[]{:S(2)}) collective-permute-start(bf16[8,16,128]{2,1,0:T(8,128)(2,1)S(1)} %get-tuple-element.101.refs_10_), channel_id=1, source_target_pairs={{0,24},{8,16},{16,8},{24,0},{1,25},{9,17},{17,9},{25,1},{2,26},{10... | collective-permute-start | bytes 98312 | tf_op jit(solution)/shard_map/ppermute | solution.py:447
  49.6 5.2 %collective-permute-start.21 = (bf16[8,16,128]{2,1,0:T(8,128)(2,1)S(1)}, bf16[8,16,128]{2,1,0:T(8,128)(2,1)S(1)}, u32[]{:S(2)}, u32[]{:S(2)}) collective-permute-start(bf16[8,16,128]{2,1,0:T(8,128)(2,1)S(1)} %get-tuple-element.101.refs_10_), channel_id=1, source_target_pairs={{0,16},{8,24},{16,0},{24,8},{1,17},{9,25},{17,1},{25,9},{2,18},{10... | collective-permute-start | bytes 98312 | tf_op jit(solution)/shard_map/ppermute | solution.py:447
  50.2 4.8 %collective-permute-start.20 = (bf16[8,16,128]{2,1,0:T(8,128)(2,1)S(1)}, bf16[8,16,128]{2,1,0:T(8,128)(2,1)S(1)}, u32[]{:S(2)}, u32[]{:S(2)}) collective-permute-start(bf16[8,16,128]{2,1,0:T(8,128)(2,1)S(1)} %get-tuple-element.101.refs_10_), channel_id=1, source_target_pairs={{0,8},{8,0},{16,24},{24,16},{1,9},{9,1},{17,25},{25,17},{2,10},{10... | collective-permute-start | bytes 98312 | tf_op jit(solution)/shard_map/ppermute | solution.py:447
  59.9 5.5 %collective-permute-start.24 = (bf16[8,16,128]{2,1,0:T(8,128)(2,1)S(1)}, bf16[8,16,128]{2,1,0:T(8,128)(2,1)S(1)}, u32[]{:S(2)}, u32[]{:S(2)}) collective-permute-start(bf16[8,16,128]{2,1,0:T(8,128)(2,1)S(1)} %get-tuple-element.105), channel_id=1, source_target_pairs={{0,16},{8,24},{16,0},{24,8},{1,17},{9,25},{17,1},{25,9},{2,18},{10... | collective-permute-start | bytes 98312 | tf_op jit(solution)/shard_map/ppermute | solution.py:447
  61.3 5.7 %collective-permute-start.25 = (bf16[8,16,128]{2,1,0:T(8,128)(2,1)S(1)}, bf16[8,16,128]{2,1,0:T(8,128)(2,1)S(1)}, u32[]{:S(2)}, u32[]{:S(2)}) collective-permute-start(bf16[8,16,128]{2,1,0:T(8,128)(2,1)S(1)} %get-tuple-element.106), channel_id=1, source_target_pairs={{0,24},{8,16},{16,8},{24,0},{1,25},{9,17},{17,9},{25,1},{2,26},{10... | collective-permute-start | bytes 98312 | tf_op jit(solution)/shard_map/ppermute | solution.py:447
  68.7 5.2 %collective-permute-start.27 = (bf16[8,16,128]{2,1,0:T(8,128)(2,1)S(1)}, bf16[8,16,128]{2,1,0:T(8,128)(2,1)S(1)}, u32[]{:S(2)}, u32[]{:S(2)}) collective-permute-start(bf16[8,16,128]{2,1,0:T(8,128)(2,1)S(1)} %get-tuple-element.110), channel_id=1, source_target_pairs={{0,16},{8,24},{16,0},{24,8},{1,17},{9,25},{17,1},{25,9},{2,18},{10... | collective-permute-start | bytes 98312 | tf_op jit(solution)/shard_map/ppermute | solution.py:447
  70.8 5.7 %collective-permute-start.28 = (bf16[8,16,128]{2,1,0:T(8,128)(2,1)S(1)}, bf16[8,16,128]{2,1,0:T(8,128)(2,1)S(1)}, u32[]{:S(2)}, u32[]{:S(2)}) collective-permute-start(bf16[8,16,128]{2,1,0:T(8,128)(2,1)S(1)} %get-tuple-element.111), channel_id=1, source_target_pairs={{0,24},{8,16},{16,8},{24,0},{1,25},{9,17},{17,9},{25,1},{2,26},{10... | collective-permute-start | bytes 98312 | tf_op jit(solution)/shard_map/ppermute | solution.py:447
  78.4 5.0 %collective-permute-start.31 = (bf16[12,16,128]{2,1,0:T(8,128)(2,1)S(1)}, bf16[12,16,128]{2,1,0:T(8,128)(2,1)S(1)}, u32[]{:S(2)}, u32[]{:S(2)}) collective-permute-start(bf16[12,16,128]{2,1,0:T(8,128)(2,1)S(1)} %get-tuple-element.118), channel_id=1, source_target_pairs={{0,6},{1,7},{2,4},{3,5},{4,2},{5,3},{6,0},{7,1},{8,14},{9,15},{10,... | collective-permute-start | bytes 147464 | tf_op jit(solution)/shard_map/ppermute | solution.py:450
  86.7 5.4 %collective-permute-start.37 = (bf16[128,128]{1,0:T(8,128)(2,1)S(1)}, bf16[128,128]{1,0:T(8,128)(2,1)S(1)}, u32[]{:S(2)}, u32[]{:S(2)}) collective-permute-start(bf16[128,128]{1,0:T(8,128)(2,1)S(1)} %get-tuple-element.121), channel_id=1, source_target_pairs={{0,16},{8,24},{16,0},{24,8},{1,17},{9,25},{17,1},{25,9},{2,18},{10... | collective-permute-start | bytes 98312 | tf_op jit(solution)/shard_map/ppermute | solution.py:447
  89.4 5.7 %collective-permute-start.38 = (bf16[128,128]{1,0:T(8,128)(2,1)S(1)}, bf16[128,128]{1,0:T(8,128)(2,1)S(1)}, u32[]{:S(2)}, u32[]{:S(2)}) collective-permute-start(bf16[128,128]{1,0:T(8,128)(2,1)S(1)} %get-tuple-element.122), channel_id=1, source_target_pairs={{0,24},{8,16},{16,8},{24,0},{1,25},{9,17},{17,9},{25,1},{2,26},{10... | collective-permute-start | bytes 98312 | tf_op jit(solution)/shard_map/ppermute | solution.py:447
  (22 other events, 72.2 us)

commit v3 on v2

--- a/solution.py
+++ b/solution.py
@@ -27,19 +27,14 @@
         self.own = n_col * self.rows_dev
         self.blocks = n_row * self.own
         self.tile_rows = self.tiles // 2 * self.block
-        self.index_at = self.tile_rows
-        self.inverse_at = self.index_at + 16
+        self.inverse_at = self.tile_rows + 16
         self.vmem_bytes = (24 if n_col <= 8 else 48) << 20
 
-    def inverse_rows(self, level):
-        return pl.ds(self.inverse_at + (level - 1) * self.block, self.block)
-
-    def sides_at(self, level, core=0):
-        start = self.inverse_at + self.levels * self.block
-        return start + ((level - 1) * 2 + core) * self.slice
-
-    def first_rows(self):
-        return self.sides_at(self.levels + 1)
+    def payload_rows(self):
+        return self.inverse_at + self.block
+
+    def extra(self):
+        return self.levels + self.block // self.slice
 
     def sources(self):
         return [2 * chip + core for core in range(2) for chip in range(self.chips)]
@@ -56,6 +51,16 @@
         scratch_shapes=list(scratch),
         compiler_params=pltpu.CompilerParams(vmem_limit_bytes=plan.vmem_bytes),
     )(*args)
+
+
+def row_order(values):
+    values = list(values)
+    return values[:1] + values[-1:] + values[1:-1]
+
+
+def chip_order(values):
+    values = list(values)
+    return values[:1] + values[:0:-1]
 
 
 def take(refs, count):
@@ -139,9 +144,9 @@
 def pack_kernel(plan, place, rows, cols, *refs):
     refs = list(refs)
     tiles, sides, inverse = take(refs, 3)
-    first = refs.pop(0)
-    payloads = [None, take(refs, plan.chips)] + [[ref.at[0]] for ref in take(refs, plan.levels - 2)]
-    tiles_here, sides_here, inverse_here, slices, sems = refs
+    first, side_slices, inverse_one = take(refs, 3)
+    payloads = take(refs, plan.levels - 1)
+    tiles_here, sides_here, inverse_here, sems = refs
     copies = [
         pltpu.make_async_copy(tiles, tiles_here, sems.at[0]),
         pltpu.make_async_copy(sides, sides_here, sems.at[1]),
@@ -151,41 +156,33 @@
         copy.start()
     for copy in copies:
         copy.wait()
-    half, width = plan.block, plan.slice
+    half = plan.block
     lane = lax.broadcasted_iota(jnp.int32, (16, 128), 1)
     for coupling in range(plan.levels):
-        targets = [first] if coupling == 0 else payloads[coupling]
+        target = payloads[coupling - 1].at[0] if coupling else first
         for k in range(plan.tiles // 2):
             pair = jnp.concatenate([tiles_here[coupling, 2 * k], tiles_here[coupling, 2 * k + 1]], axis=1)
-            for target in targets:
-                target[k * half : (k + 1) * half, :] = pair
+            target[k * half : (k + 1) * half, :] = pair
         if coupling == 0:
             continue
         index = jnp.zeros((16, 128), F32)
         for t in range(plan.tiles):
             index = jnp.where(lane == t, rows[coupling, t, 0].astype(F32), index)
             index = jnp.where(lane == t + 64, cols[coupling, t, 0].astype(F32), index)
-        for target in targets:
-            target[plan.index_at : plan.index_at + 16, :] = index.astype(BF16)
-        if coupling > 1:
-            continue
-        for level in range(1, plan.levels + 1):
-            matrix = inverse_here[level].astype(BF16)
-            both = jnp.concatenate([sides_here[level, b] for b in range(plan.rows_dev)], axis=0).T
-            pad_slices(plan, both, slices)
-            for chip, target in enumerate(targets):
-                target[plan.inverse_rows(level), :] = matrix
-                base = (place[1] ^ (2 * chip)) // 2 * 2
-                for core in range(2):
-                    here = pl.ds(pl.multiple_of((base + core) * width, 16), width)
-                    start = plan.sides_at(level, core)
-                    target[start : start + width, :] = slices[here, :]
+        target[plan.tile_rows : plan.inverse_at, :] = index.astype(BF16)
+    inverse_one[...] = inverse_here[1].astype(BF16).reshape(inverse_one.shape)
+    for level in range(1, plan.levels + 1):
+        if level > 1:
+            payloads[level - 2][0, plan.inverse_at :, :] = inverse_here[level].astype(BF16)
+        both = jnp.concatenate([sides_here[level, b] for b in range(plan.rows_dev)], axis=0).T
+        pad_slices(plan, both, side_slices.at[level - 1])
 
 
 def near_forward_kernel(plan, place, rows, cols, pairs, *refs):
     refs = list(refs)
     received = take(refs, plan.n_row)
-    keep, send, left, right, total = refs
+    side_slices, inverse_one = take(refs, 2)
+    keep, keep_extra, send, left, right, total = refs
     half, width = plan.block, plan.slice
     for m in range(plan.n_row):
         store_halves(left, right, place[0] ^ m, received[m][...].astype(F32), half)
@@ -197,23 +194,34 @@
         total[rows[0, 2 * k, 0]] += product[: plan.padded]
         total[rows[0, 2 * k + 1, 0]] += product[plan.padded :]
     for chip in range(plan.chips):
-        for core, out in enumerate((keep, send)):
+        for core, (out, extra, at) in enumerate(((keep, keep_extra, 0), (send, send, plan.n_col))):
             number = place[1] ^ (2 * chip + core)
             here = pl.ds(pl.multiple_of(number * width, 16), width)
             for u in range(plan.n_col):
                 value = jnp.concatenate([total[2 * u, here, :], total[2 * u + 1, here, :]], axis=1)
                 out[chip, u] = value.astype(out.dtype)
-
-
-def add_kernel(plan, keep, received, *out):
+            for level in range(plan.levels):
+                extra[chip, at + level] = side_slices[level, here, :]
+            extra[chip, at + plan.levels : at + plan.extra()] = inverse_one[...]
+
+
+def add_kernel(plan, place, keep, keep_extra, received, own, *out):
+    here = plan.n_col + (place[1] & 1) * plan.extra()
+    there = plan.n_col + (1 - (place[1] & 1)) * plan.extra()
+    out = chip_order(out)
+    own[...] = keep[0] + received[0, : plan.n_col].astype(F32)
     for chip in range(plan.chips):
-        out[chip][...] = (keep[chip] + received[chip].astype(F32)).astype(out[chip].dtype)
+        if chip:
+            total = keep[chip] + received[chip, : plan.n_col].astype(F32)
+            out[chip][: plan.n_col] = total.astype(BF16)
+        out[chip][pl.ds(here, plan.extra())] = keep_extra[chip]
+        out[chip][pl.ds(there, plan.extra())] = received[chip, plan.n_col :]
 
 
 def near_backward_kernel(plan, place, rows, cols, pairs, *refs):
     refs = list(refs)
     received = take(refs, plan.n_col)
-    out = take(refs, plan.n_row)
+    out = row_order(take(refs, plan.n_row))
     upper, left, right = refs
     half, width = plan.block, plan.slice
     for piece, offset in zip(received, plan.sources()):
@@ -251,7 +259,7 @@
         value = drop_padding(plan, all_slices[n].astype(F32)).T
         for b in range(plan.rows_dev):
             out[n + 1, b] = value[b * half : (b + 1) * half, :]
-    back = shares[0][...]
+    back = shares[0][...].astype(F32)
     for share in shares[1:]:
         back = back + share[...].astype(F32)
     value = drop_padding(plan, solved[...] - back)
@@ -261,18 +269,30 @@
                                     precision=lax.Precision.HIGHEST, preferred_element_type=F32)
 
 
-def level_forward(plan, place, level, pieces, coupled, write):
-    for piece, offset in zip(pieces, plan.sources()):
+def extras(plan, place, sums):
+    core = place[1] & 1
+    return [(sums[chip], plan.n_col + (core ^ other) * plan.extra()) for other in range(2) for chip in range(plan.chips)]
+
+
+def inverse_of(plan, level, extra, piece):
+    if level == 1:
+        ref, at = extra
+        return ref[pl.ds(at + plan.levels, plan.block // plan.slice)].reshape(plan.block, plan.lanes)
+    return piece[plan.inverse_at :, :]
+
+
+def level_forward(plan, place, level, sums, pieces, coupled, write):
+    for extra, piece, offset in zip(extras(plan, place, sums), pieces, plan.sources()):
         u = place[1] ^ offset
-        start = plan.sides_at(level) + (place[1] & 1) * plan.slice
-        side = piece[pl.ds(pl.multiple_of(start, 16), plan.slice), :].astype(F32)
-        write(piece, u, apply_pair(piece[plan.inverse_rows(level), :], side - coupled(u), plan.block))
-
-
-def level_backward(plan, place, level, pieces, value, write):
-    for piece, offset in zip(pieces, plan.sources()):
+        side = extra[0][extra[1] + level - 1].astype(F32)
+        inverse = inverse_of(plan, level, extra, piece)
+        write(inverse, u, apply_pair(inverse, side - coupled(u), plan.block))
+
+
+def level_backward(plan, place, level, sums, pieces, value, write):
+    for extra, piece, offset in zip(extras(plan, place, sums), pieces, plan.sources()):
         u = place[1] ^ offset
-        write(u, apply_pair_transposed(piece[plan.inverse_rows(level), :], value(u), plan.block))
+        write(u, apply_pair_transposed(inverse_of(plan, level, extra, piece), value(u), plan.block))
 
 
 def join_kernel(plan, first, second, out):
@@ -281,15 +301,17 @@
     out[count:] = second[...]
 
 
-def views(plan, refs):
-    if len(refs) == plan.n_col:
-        return refs
-    return [ref.at[chip] for ref in refs for chip in range(plan.chips)]
+def views(plan, coupling, refs):
+    order = list(range(plan.chips))
+    if coupling % 2 == 0:
+        bits = plan.chips.bit_length() - 1
+        order = [sum(((chip >> n) & 1) << (bits - 1 - n) for n in range(bits)) for chip in order]
+    return [ref.at[chip] for ref in refs for chip in order]
 
 
 def add_up(refs):
     def total(u):
-        value = refs[0][u]
+        value = refs[0][u].astype(F32)
         for ref in refs[1:]:
             value = value + ref[u].astype(F32)
         return value
@@ -299,20 +321,21 @@
 
 def enter_kernel(plan, place, *refs):
     refs = list(refs)
-    pieces, sums = take(refs, plan.n_col), take(refs, plan.chips)
+    sums = take(refs, plan.chips + 1)
     solved, message = refs
 
-    def write(piece, u, value):
+    def write(inverse, u, value):
         solved[u] = value
         message[u] = value.astype(BF16)
 
-    level_forward(plan, place, 1, pieces, add_up(sums), write)
+    coupled = add_up([sums[0]] + sums[2:])
+    level_forward(plan, place, 1, sums[1:], [None] * plan.n_col, coupled, write)
 
 
 def decode(plan, place, pieces, index):
     lane = lax.broadcasted_iota(jnp.int32, (1, 128), 1)
     for p, offset in enumerate(plan.sources()):
-        raw = pieces[p][plan.index_at : plan.index_at + 16, :].astype(F32).astype(jnp.int32)[0:1]
+        raw = pieces[p][plan.tile_rows : plan.inverse_at, :].astype(F32).astype(jnp.int32)[0:1]
         owner = raw // plan.rows_dev * plan.n_col + (place[1] ^ offset)
         col = owner * plan.rows_dev + raw % plan.rows_dev
         index[p : p + 1, :] = jnp.where(lane < 64, raw, col)
@@ -357,12 +380,11 @@
 def forward_kernel(coupling, plan, place, *refs):
     refs = list(refs)
     last = coupling == plan.levels - 1
-    solvers = take(refs, plan.n_col)
-    pieces = solvers if coupling == 1 else views(plan, take(refs, 2))
+    sums, pieces = take(refs, plan.chips), views(plan, coupling, take(refs, 2))
     received = take(refs, plan.n_row)
     keep = refs.pop(0)
     if last:
-        out = take(refs, plan.n_row)
+        out = row_order(take(refs, plan.n_row))
     else:
         message, index_out = take(refs, 2)
     left, right, total, index, sem = take(refs, 5)
@@ -378,31 +400,30 @@
 
     if not last:
 
-        def write(piece, u, value):
+        def write(inverse, u, value):
             keep[u] = value
             message[u] = value.astype(BF16)
 
-        level_forward(plan, place, coupling + 1, solvers, coupled, write)
+        level_forward(plan, place, coupling + 1, sums, pieces, coupled, write)
         return
     back_left[...] = jnp.zeros_like(back_left)
     back_right[...] = jnp.zeros_like(back_right)
 
-    def write_top(piece, u, value):
-        value = apply_pair_transposed(piece[plan.inverse_rows(plan.levels), :], value, plan.block)
+    def write_top(inverse, u, value):
+        value = apply_pair_transposed(inverse, value, plan.block)
         keep[u] = value.astype(BF16)
         put_upper(plan, upper, u, value)
 
-    level_forward(plan, place, plan.levels, solvers, coupled, write_top)
+    level_forward(plan, place, plan.levels, sums, pieces, coupled, write_top)
     multiply_backward(plan, place, pieces, index, upper, back_left, back_right, out)
 
 
 def backward_kernel(level, plan, place, index, *refs):
     refs = list(refs)
-    solvers = take(refs, plan.n_col)
-    pieces = solvers if level == 2 else views(plan, take(refs, 2))
+    sums, pieces = take(refs, plan.chips), views(plan, level - 1, take(refs, 2))
     shares = take(refs, plan.n_row)
     solved, keep = take(refs, 2)
-    out = take(refs, plan.n_row)
+    out = row_order(take(refs, plan.n_row))
     upper, left, right = refs
     left[...] = jnp.zeros_like(left)
     right[...] = jnp.zeros_like(right)
@@ -412,22 +433,22 @@
         keep[u] = value.astype(BF16)
         put_upper(plan, upper, u, value)
 
-    level_backward(plan, place, level, solvers, lambda u: solved[u] - back(u), write)
+    level_backward(plan, place, level, sums, pieces, lambda u: solved[u] - back(u), write)
     multiply_backward(plan, place, pieces, index, upper, left, right, out)
 
 
 def leave_kernel(plan, place, *refs):
     refs = list(refs)
-    pieces, shares = take(refs, plan.n_col), take(refs, plan.n_row)
+    sums, shares = take(refs, plan.chips), take(refs, plan.n_row)
     solved = refs.pop(0)
-    above, out = take(refs, plan.levels - 1), refs
+    above, out = take(refs, plan.levels - 1), chip_order(refs)
     back = add_up(shares)
 
     def write(u, value):
         for message in out:
             message[u] = value.astype(BF16)
 
-    level_backward(plan, place, 1, pieces, lambda u: solved[u] - back(u), write)
+    level_backward(plan, place, 1, sums, [None] * plan.n_col, lambda u: solved[u] - back(u), write)
     for chip, message in enumerate(out):
         base = (place[1] ^ (2 * chip)) // 2 * 2
         for core in range(2):
@@ -449,8 +470,8 @@
     def over_col(value, m):
         return lax.ppermute(value, "col", [(i, i ^ m) for i in range(n_col)])
 
-    def exchange_row(values, order=1):
-        got = {m: over_row(values[m], m) for m in range(1, n_row)[::order]}
+    def exchange_row(values):
+        got = {m: over_row(values[m], m) for m in [*range(2, n_row), 1]}
         return [values[0]] + [got[m] for m in range(1, n_row)]
 
     def exchange_chips(values):
@@ -469,39 +490,46 @@
     )
     (message, place, tile_row, tile_col) = lax.optimization_barrier((message, place, tile_row, tile_col))
     received = exchange_row([message] * n_row)
-    made = call(
+    pairs, side_slices, inverse_one, *held = call(
         plan, pack_kernel,
-        [array((plan.tile_rows, plan.lanes))]
-        + [array((plan.first_rows(), plan.lanes))] * chips
-        + [array((1, plan.inverse_at, plan.lanes)) for s in range(2, levels)],
+        [array((plan.tile_rows, plan.lanes)), array((levels,) + column),
+         array((plan.block // plan.slice, plan.slice, plan.lanes))]
+        + [array((1, plan.payload_rows(), plan.lanes))] * (levels - 1),
         (place, tile_row, tile_col, factor_tiles, right_sides, diag_inverse),
         [pltpu.VMEM(factor_tiles.shape, BF16), pltpu.VMEM(right_sides.shape, F32),
-         pltpu.VMEM(diag_inverse.shape, F32), pltpu.VMEM(column, BF16), dma((3,))],
+         pltpu.VMEM(diag_inverse.shape, F32), dma((3,))],
         scalars=3, raw=(3, 4, 5),
     )
-    pairs = made[0]
-    payloads = [None, list(made[1 : 1 + chips])] + list(made[1 + chips :])
-
-    def swap_cores(values):
-        return [over_col(value, 1) for value in values]
-
-    gathered = exchange_chips(after(payloads[1], received))
-    near, late = gathered[:3], gathered[3:]
-    keep, send = call(
-        plan, near_forward_kernel, [array((chips,) + slices, F32), array((chips,) + slices)],
-        [place, tile_row, tile_col, pairs] + received,
+
+    def join(held, other):
+        shape = (2 * held.shape[0],) + held.shape[1:]
+        return call(plan, join_kernel, [array(shape)], [held, other], scalars=0)[0]
+
+    def step(held, coupling):
+        bit = held.shape[0] if coupling % 2 else chips // 2 // held.shape[0]
+        return held, over_col(held, 2 * bit)
+
+    held = [step(value, s) for s, value in enumerate(after(held, received), 1)]
+    keep, keep_extra, send = call(
+        plan, near_forward_kernel,
+        [array((chips,) + slices, F32), array((chips, plan.extra()) + slices[1:]),
+         array((chips, n_col + plan.extra()) + slices[1:])],
+        [place, tile_row, tile_col, pairs] + received + [side_slices, inverse_one],
         [pltpu.VMEM((n_row * plan.rows_dev,) + column, BF16), pltpu.VMEM((n_row * plan.rows_dev,) + column, BF16),
          pltpu.VMEM((plan.own, plan.padded, plan.block), F32)],
         scalars=3,
     )
-    near, send = lax.optimization_barrier((near, send))
-    swapped, far = over_col(send, 1), swap_cores(near)
-    swapped, near, far = lax.optimization_barrier((swapped, near, far))
-    sums = call(plan, add_kernel, [array(slices, F32)] + [array(slices)] * (chips - 1), [keep, swapped], scalars=0)
-    sums = exchange_chips(sums)
-    first = near + late + far + swap_cores(late)
+    swapped = over_col(send, 1)
+    made = call(
+        plan, add_kernel, [array(slices, F32)] + [array((n_col + 2 * plan.extra(),) + slices[1:])] * chips,
+        [place, keep, keep_extra, swapped],
+    )
+    own, sums = made[0], exchange_chips(chip_order(made[1:]))
+    held = [join(*value) for value in after(held, sums)]
+    if chips > 2:
+        held = [step(value, s) for s, value in enumerate(held, 1)]
     solved, message = call(
-        plan, enter_kernel, [array(slices, F32), array(slices)], [place] + first + sums
+        plan, enter_kernel, [array(slices, F32), array(slices)], [place, own] + sums
     )
     solved = [None, solved]
 
@@ -520,48 +548,43 @@
     ]
     partial = [array(slices, F32)] + [array(slices)] * (n_row - 1)
     index = [None] * levels
-    def double(held, step):
-        other = over_col(held, 2 * step)
-        return call(plan, join_kernel, [array((2 * step,) + held.shape[1:])], [held, other], scalars=0)[0]
-
-    pieces = [None, []]
+    pieces = [None]
     for s in range(1, levels):
-        if s + 1 < levels:
-            held, step = double(after(payloads[s + 1], message), 1) if chips > 1 else payloads[s + 1], 2
         received = exchange_row([message] * n_row)
-        if s + 1 < levels:
-            held = after(held, received)
-            while step < chips:
-                held, step = double(held, step), 2 * step
-        args = [place] + first + pieces[s] + received
+        if s == 1 and chips > 2:
+            received, held = lax.optimization_barrier((received, held))
+            held = [join(*value) for value in held]
+            while held[0].shape[0] < chips:
+                held = [join(*step(value, n)) for n, value in enumerate(held, 1)]
+        pieces.append([held[s - 1], over_col(held[s - 1], 1)])
+        args = [place] + sums + pieces[s] + received
         if s < levels - 1:
             value, message, index[s] = call(
                 plan, functools.partial(forward_kernel, s),
                 [array(slices, F32), array(slices), array(index_shape, jnp.int32)], args, forward,
             )
             solved.append(value)
-            pieces.append([held, over_col(after(held, message), 1)])
         else:
             made = call(
                 plan, functools.partial(forward_kernel, s), [array(slices)] + partial, args,
                 forward + [pltpu.VMEM(index_shape, jnp.int32)] + backward,
             )
     results = [made[0]]
-    shares = exchange_row(made[1:], -1)
+    shares = exchange_row(row_order(made[1:]))
     for level in range(levels - 1, 1, -1):
         made = call(
             plan, functools.partial(backward_kernel, level), [array(slices)] + partial,
-            [place, index[level - 1]] + first + pieces[level - 1] + shares + [solved[level]],
+            [place, index[level - 1]] + sums + pieces[level - 1] + shares + [solved[level]],
             backward, scalars=2,
         )
         results.insert(0, made[0])
-        shares = exchange_row(made[1:], -1)
+        shares = exchange_row(row_order(made[1:]))
     messages = call(
         plan, leave_kernel, [array((n_col + 2 * (levels - 1),) + slices[1:])] * chips,
-        [place] + first + shares + [solved[1]] + results,
-    )
-    messages = exchange_chips(messages)
-    messages = messages + swap_cores(messages)
+        [place] + sums + shares + [solved[1]] + results,
+    )
+    messages = exchange_chips(chip_order(messages))
+    messages = messages + [over_col(value, 1) for value in messages]
     shares = call(
         plan, near_backward_kernel, [array(column, F32)] + [array(column)] * (n_row - 1),
         [place, tile_row, tile_col, pairs] + messages,
@@ -569,7 +592,7 @@
          pltpu.VMEM((n_row * plan.rows_dev,) + column, F32), pltpu.VMEM((n_row * plan.rows_dev,) + column, F32)],
         scalars=3,
     )
-    shares = exchange_row(shares, -1)
+    shares = exchange_row(row_order(shares))
     return call(
         plan, last_kernel, [array(right_sides.shape, F32)], [place, diag_inverse, x0] + shares + messages,
         [pltpu.VMEM((levels,) + column, BF16)],

time: 97 us -> 89.9 us (0.927)
  waiting for transfers between devices: 34.6 us -> 27.4 us
    ppermute x21 -> x17, waiting for transfers between devices: 15.6 us -> 9.02 us  [over_col(): return lax.ppermute(value, 'col', [(i, i ^ m) for i in range(n_col)])]
    pallas_call x13 -> x15, Pallas kernels: 16.8 us -> 17.4 us  [call(): pl.pallas_call(functools.partial(body, plan), out_shape=outs, in_specs=sp...]
    ppermute x21 -> x17, starting transfers between devices: 14 us -> 13.5 us  [over_col(): return lax.ppermute(value, 'col', [(i, i ^ m) for i in range(n_col)])]
  transfers between devices with their start and end apart: 39 -> 35, of which waited for: 23 -> 19; matrix products, arithmetic and copies ran while one was open for 0% -> 0% of each run, Pallas kernels for 6% -> 6%
where the time goes in v3:
time: 89.9 us; the launch traced here: 89.7 us
  starting transfers between devices  41.5 us (46%)
  waiting for transfers between devices  27.4 us (30%)
  Pallas kernels  17.4 us (19%)
  local copies, waits for them, and re-layouts  3.14 us (3%)
    ppermute x18, starting transfers between devices, over_row(): return lax.ppermute(value, 'row', [(i, i ^ m) for i in range(n_row)])  28 us
    ppermute x18, waiting for transfers between devices, over_row(): return lax.ppermute(value, 'row', [(i, i ^ m) for i in range(n_row)])  18.4 us
    pallas_call x15, Pallas kernels, call(): pl.pallas_call(functools.partial(body, plan), out_shape=outs, in_specs=sp...  17.4 us
    ppermute x17, starting transfers between devices, over_col(): return lax.ppermute(value, 'col', [(i, i ^ m) for i in range(n_col)])  13.5 us
    ppermute x17, waiting for transfers between devices, over_col(): return lax.ppermute(value, 'col', [(i, i ^ m) for i in range(n_col)])  9.02 us
    unnamed x14, local copies, waits for them, and re-layouts  2.93 us
  transfers between devices with their start and end apart: 35, of which 19 were waited for; matrix products, arithmetic and copies ran while one was open for 0% of the time, Pallas kernels for 6%

profile of v3, /device:TPU:0, one launch (start us, length us, event | category | flops | bytes accessed | tf_op | source)
XLA Modules:
  0.0 89.7 jit_solution(10889417015401243099)
XLA Ops:
  2.5 5.1 %collective-permute-start.2 = (bf16[128,128]{1,0:T(8,128)(2,1)S(1)}, bf16[128,128]{1,0:T(8,128)(2,1)S(1)}, u32[]{:S(2)}, u32[]{:S(2)}) collective-permute-start(bf16[128,128]{1,0:T(8,128)(2,1)S(1)} %get-tuple-element.67.refs_0_), channel_id=1, source_target_pairs={{0,24},{8,16},{16,8},{24,0},{1,25},{9,17},{17,9},{25,1},{2,26},{10... | collective-permute-start | bytes 98312 | tf_op jit(solution)/shard_map/ppermute | solution.py:468
  9.5 1.9 %shard_map.56 = (bf16[384,128]{1,0:T(8,128)(2,1)S(1)}, bf16[3,128,128]{2,1,0:T(8,128)(2,1)S(1)}, bf16[4,16,128]{2,1,0:T(8,128)(2,1)S(1)}, bf16[1,464,128]{2,1,0:T(8,128)(2,1)S(1)}, bf16[1,464,128]{2,1,0:T(8,128)(2,1)S(1)}) custom-call(s32[2]{0:T(128)S(1)} %pad_add_fusion.place, s32[3,12,1]{2,1,0:T(8,128)S(1)} %copy.10.rows, s32[3,12,1]{2,1,0:T(8,128)S(1)} %copy.11.cols, ...), custom_call_target="tpu_custom_call" | custom-call | tf_op jit(solution)/shard_map/pallas_call | solution.py:46
  12.4 1.9 %shard_map.57 = (f32[4,8,16,128]{3,2,1,0:T(8,128)S(1)}, bf16[4,7,16,128]{3,2,1,0:T(8,128)(2,1)S(1)}, bf16[4,15,16,128]{3,2,1,0:T(8,128)(2,1)S(1)}) custom-call(s32[2]{0:T(128)S(1)} %pad_add_fusion.place, s32[3,12,1]{2,1,0:T(8,128)S(1)} %copy.10.rows, s32[3,12,1]{2,1,0:T(8,128)S(1)} %copy.11.cols, bf16[384,128]{1,0:T(8,128)(2,1)S(1)} %get-tuple-element.66.pairs, ...), custom_call_target="tpu_custom_call" | custom-call | tf_op jit(solution)/shard_map/pallas_call | solution.py:46
  19.5 2.1 %collective-permute-start.6 = (bf16[22,16,128]{2,1,0:T(8,128)(2,1)S(1)}, bf16[22,16,128]{2,1,0:T(8,128)(2,1)S(1)}, u32[]{:S(2)}, u32[]{:S(2)}) collective-permute-start(bf16[22,16,128]{2,1,0:T(8,128)(2,1)S(1)} %get-tuple-element.76), channel_id=1, source_target_pairs={{0,6},{1,7},{2,4},{3,5},{4,2},{5,3},{6,0},{7,1},{8,14},{9,15},{10,... | collective-permute-start | bytes 270344 | tf_op jit(solution)/shard_map/ppermute | solution.py:471
  21.6 1.7 %collective-permute-done.4.refs_2_.refs_1_ = bf16[22,16,128]{2,1,0:T(8,128)(2,1)S(1)} collective-permute-done((bf16[22,16,128]{2,1,0:T(8,128)(2,1)S(1)}, bf16[22,16,128]{2,1,0:T(8,128)(2,1)S(1)}, u32[]{:S(2)}, u32[]{:S(2)}) %collective-permute-start.4) | collective-permute-done | bytes 90144 | tf_op jit(solution)/shard_map/ppermute | solution.py:471
  23.4 1.8 %collective-permute-done.5.refs_3_.refs_2_ = bf16[22,16,128]{2,1,0:T(8,128)(2,1)S(1)} collective-permute-done((bf16[22,16,128]{2,1,0:T(8,128)(2,1)S(1)}, bf16[22,16,128]{2,1,0:T(8,128)(2,1)S(1)}, u32[]{:S(2)}, u32[]{:S(2)}) %collective-permute-start.5) | collective-permute-done | bytes 90144 | tf_op jit(solution)/shard_map/ppermute | solution.py:471
  28.6 2.9 %collective-permute-start.9 = (bf16[8,16,128]{2,1,0:T(8,128)(2,1)S(1)}, bf16[8,16,128]{2,1,0:T(8,128)(2,1)S(1)}, u32[]{:S(2)}, u32[]{:S(2)}) collective-permute-start(bf16[8,16,128]{2,1,0:T(8,128)(2,1)S(1)} %get-tuple-element.89.refs_6_), channel_id=1, source_target_pairs={{0,24},{8,16},{16,8},{24,0},{1,25},{9,17},{17,9},{25,1},{2,26},{10... | collective-permute-start | bytes 98312 | tf_op jit(solution)/shard_map/ppermute | solution.py:468
  34.4 1.9 %collective-permute-done.8.refs_8_ = bf16[8,16,128]{2,1,0:T(8,128)(2,1)S(1)} collective-permute-done((bf16[8,16,128]{2,1,0:T(8,128)(2,1)S(1)}, bf16[8,16,128]{2,1,0:T(8,128)(2,1)S(1)}, u32[]{:S(2)}, u32[]{:S(2)}) %collective-permute-start.8) | collective-permute-done | bytes 32800 | tf_op jit(solution)/shard_map/ppermute | solution.py:468
  38.2 2.2 %shard_map.63 = (f32[8,16,128]{2,1,0:T(8,128)S(1)}, bf16[8,16,128]{2,1,0:T(8,128)(2,1)S(1)}, s32[8,128]{1,0:T(8,128)S(1)}) custom-call(s32[2]{0:T(128)S(1)} %pad_add_fusion.place, bf16[22,16,128]{2,1,0:T(8,128)(2,1)S(1)} %get-tuple-element.73.refs_1_.refs_0_, bf16[22,16,128]{2,1,0:T(8,128)(2,1)S(1)} %collective-permute-done.4.refs_2_.refs_1_, ...), custom_call_target="tpu_custom_call" | custom-call | tf_op jit(solution)/shard_map/pallas_call | solution.py:46
  40.4 1.8 %collective-permute-start.18 = (bf16[8,16,128]{2,1,0:T(8,128)(2,1)S(1)}, bf16[8,16,128]{2,1,0:T(8,128)(2,1)S(1)}, u32[]{:S(2)}, u32[]{:S(2)}) collective-permute-start(bf16[8,16,128]{2,1,0:T(8,128)(2,1)S(1)} %get-tuple-element.96.refs_6_), channel_id=1, source_target_pairs={{0,24},{8,16},{16,8},{24,0},{1,25},{9,17},{17,9},{25,1},{2,26},{10... | collective-permute-start | bytes 98312 | tf_op jit(solution)/shard_map/ppermute | solution.py:468
  42.6 2.3 %collective-permute-start.16 = (bf16[8,16,128]{2,1,0:T(8,128)(2,1)S(1)}, bf16[8,16,128]{2,1,0:T(8,128)(2,1)S(1)}, u32[]{:S(2)}, u32[]{:S(2)}) collective-permute-start(bf16[8,16,128]{2,1,0:T(8,128)(2,1)S(1)} %get-tuple-element.96.refs_6_), channel_id=1, source_target_pairs={{0,8},{8,0},{16,24},{24,16},{1,9},{9,1},{17,25},{25,17},{2,10},{10... | collective-permute-start | bytes 98312 | tf_op jit(solution)/shard_map/ppermute | solution.py:468
  44.8 1.8 %collective-permute-done.18.refs_9_ = bf16[8,16,128]{2,1,0:T(8,128)(2,1)S(1)} collective-permute-done((bf16[8,16,128]{2,1,0:T(8,128)(2,1)S(1)}, bf16[8,16,128]{2,1,0:T(8,128)(2,1)S(1)}, u32[]{:S(2)}, u32[]{:S(2)}) %collective-permute-start.18) | collective-permute-done | bytes 32800 | tf_op jit(solution)/shard_map/ppermute | solution.py:468
  47.2 3.4 %shard_map.65 = (bf16[8,16,128]{2,1,0:T(8,128)(2,1)S(1)}, f32[8,16,128]{2,1,0:T(8,128)S(1)}, bf16[8,16,128]{2,1,0:T(8,128)(2,1)S(1)}, bf16[8,16,128]{2,1,0:T(8,128)(2,1)S(1)}, bf16[8,16,128]{2,1,0:T(8,128)(2,1)S(1)}) custom-call(s32[2]{0:T(128)S(1)} %pad_add_fusion.place, bf16[22,16,128]{2,1,0:T(8,128)(2,1)S(1)} %get-tuple-element.73.refs_1_.refs_0_, ...), custom_call_target="tpu_custom_call" | custom-call | tf_op jit(solution)/shard_map/pallas_call | solution.py:46
  50.6 1.6 %collective-permute-start.19 = (bf16[8,16,128]{2,1,0:T(8,128)(2,1)S(1)}, bf16[8,16,128]{2,1,0:T(8,128)(2,1)S(1)}, u32[]{:S(2)}, u32[]{:S(2)}) collective-permute-start(bf16[8,16,128]{2,1,0:T(8,128)(2,1)S(1)} %get-tuple-element.98), channel_id=1, source_target_pairs={{0,8},{8,0},{16,24},{24,16},{1,9},{9,1},{17,25},{25,17},{2,10},{10... | collective-permute-start | bytes 98312 | tf_op jit(solution)/shard_map/ppermute | solution.py:468
  55.1 2.6 %collective-permute-done.20.refs_8_ = bf16[8,16,128]{2,1,0:T(8,128)(2,1)S(1)} collective-permute-done((bf16[8,16,128]{2,1,0:T(8,128)(2,1)S(1)}, bf16[8,16,128]{2,1,0:T(8,128)(2,1)S(1)}, u32[]{:S(2)}, u32[]{:S(2)}) %collective-permute-start.20) | collective-permute-done | bytes 32800 | tf_op jit(solution)/shard_map/ppermute | solution.py:468
  57.7 1.6 %collective-permute-done.21.refs_9_ = bf16[8,16,128]{2,1,0:T(8,128)(2,1)S(1)} collective-permute-done((bf16[8,16,128]{2,1,0:T(8,128)(2,1)S(1)}, bf16[8,16,128]{2,1,0:T(8,128)(2,1)S(1)}, u32[]{:S(2)}, u32[]{:S(2)}) %collective-permute-start.21) | collective-permute-done | bytes 32800 | tf_op jit(solution)/shard_map/ppermute | solution.py:468
  60.9 2.0 %collective-permute-start.23 = (bf16[8,16,128]{2,1,0:T(8,128)(2,1)S(1)}, bf16[8,16,128]{2,1,0:T(8,128)(2,1)S(1)}, u32[]{:S(2)}, u32[]{:S(2)}) collective-permute-start(bf16[8,16,128]{2,1,0:T(8,128)(2,1)S(1)} %get-tuple-element.104), channel_id=1, source_target_pairs={{0,16},{8,24},{16,0},{24,8},{1,17},{9,25},{17,1},{25,9},{2,18},{10... | collective-permute-start | bytes 98312 | tf_op jit(solution)/shard_map/ppermute | solution.py:468
  63.0 2.3 %collective-permute-start.24 = (bf16[8,16,128]{2,1,0:T(8,128)(2,1)S(1)}, bf16[8,16,128]{2,1,0:T(8,128)(2,1)S(1)}, u32[]{:S(2)}, u32[]{:S(2)}) collective-permute-start(bf16[8,16,128]{2,1,0:T(8,128)(2,1)S(1)} %get-tuple-element.105), channel_id=1, source_target_pairs={{0,24},{8,16},{16,8},{24,0},{1,25},{9,17},{17,9},{25,1},{2,26},{10... | collective-permute-start | bytes 98312 | tf_op jit(solution)/shard_map/ppermute | solution.py:468
  65.8 2.9 %collective-permute-done.24.refs_7_ = bf16[8,16,128]{2,1,0:T(8,128)(2,1)S(1)} collective-permute-done((bf16[8,16,128]{2,1,0:T(8,128)(2,1)S(1)}, bf16[8,16,128]{2,1,0:T(8,128)(2,1)S(1)}, u32[]{:S(2)}, u32[]{:S(2)}) %collective-permute-start.24) | collective-permute-done | bytes 32800 | tf_op jit(solution)/shard_map/ppermute | solution.py:468
  71.2 1.9 %collective-permute-start.27 = (bf16[12,16,128]{2,1,0:T(8,128)(2,1)S(1)}, bf16[12,16,128]{2,1,0:T(8,128)(2,1)S(1)}, u32[]{:S(2)}, u32[]{:S(2)}) collective-permute-start(bf16[12,16,128]{2,1,0:T(8,128)(2,1)S(1)} %get-tuple-element.112), channel_id=1, source_target_pairs={{0,6},{1,7},{2,4},{3,5},{4,2},{5,3},{6,0},{7,1},{8,14},{9,15},{10,... | collective-permute-start | bytes 147464 | tf_op jit(solution)/shard_map/ppermute | solution.py:471
  77.4 2.0 %shard_map.68 = (f32[128,128]{1,0:T(8,128)S(1)}, bf16[128,128]{1,0:T(8,128)(2,1)S(1)}, bf16[128,128]{1,0:T(8,128)(2,1)S(1)}, bf16[128,128]{1,0:T(8,128)(2,1)S(1)}) custom-call(s32[2]{0:T(128)S(1)} %pad_add_fusion.place, s32[3,12,1]{2,1,0:T(8,128)S(1)} %copy.10.rows, s32[3,12,1]{2,1,0:T(8,128)S(1)} %copy.11.cols, ...), custom_call_target="tpu_custom_call" | custom-call | tf_op jit(solution)/shard_map/pallas_call | solution.py:46
  79.4 2.9 %collective-permute-start.33 = (bf16[128,128]{1,0:T(8,128)(2,1)S(1)}, bf16[128,128]{1,0:T(8,128)(2,1)S(1)}, u32[]{:S(2)}, u32[]{:S(2)}) collective-permute-start(bf16[128,128]{1,0:T(8,128)(2,1)S(1)} %get-tuple-element.115), channel_id=1, source_target_pairs={{0,16},{8,24},{16,0},{24,8},{1,17},{9,25},{17,1},{25,9},{2,18},{10... | collective-permute-start | bytes 98312 | tf_op jit(solution)/shard_map/ppermute | solution.py:468
  84.3 3.7 %collective-permute-done.34.refs_5_ = bf16[128,128]{1,0:T(8,128)(2,1)S(1)} collective-permute-done((bf16[128,128]{1,0:T(8,128)(2,1)S(1)}, bf16[128,128]{1,0:T(8,128)(2,1)S(1)}, u32[]{:S(2)}, u32[]{:S(2)}) %collective-permute-start.34) | collective-permute-done | bytes 32800 | tf_op jit(solution)/shard_map/ppermute | solution.py:468
  88.1 1.7 %shard_map.69 = f32[4,2,64,128]{3,2,1,0:T(8,128)} custom-call(s32[2]{0:T(128)S(1)} %pad_add_fusion.place, f32[4,64,128]{2,1,0:T(8,128)S(1)} %copy-done.1, f32[128,128]{1,0:T(8,128)S(1)} %get-tuple-element.63.refs_1_, f32[128,128]{1,0:T(8,128)S(1)} %get-tuple-element.113.refs_2_, bf16[128,128]{1,0:T(8,128)(2,1)S(1)} %collective-permute-done.32.refs_3_, ...), custom_call_target="tpu_custom_call" | custom-call | tf_op jit(solution)/shard_map/pallas_call | solution.py:46
  (78 shorter events, 33.6 us)
Async XLA Ops:
  2.5 8.9 %collective-permute-start.2 = (bf16[128,128]{1,0:T(8,128)(2,1)S(1)}, bf16[128,128]{1,0:T(8,128)(2,1)S(1)}, u32[]{:S(2)}, u32[]{:S(2)}) collective-permute-start(bf16[128,128]{1,0:T(8,128)(2,1)S(1)} %get-tuple-element.67.refs_0_), channel_id=1, source_target_pairs={{0,24},{8,16},{16,8},{24,0},{1,25},{9,17},{17,9},{25,1},{2,26},{10... | collective-permute-start | bytes 98312 | tf_op jit(solution)/shard_map/ppermute | solution.py:468
  7.6 4.8 %collective-permute-start.1 = (bf16[128,128]{1,0:T(8,128)(2,1)S(1)}, bf16[128,128]{1,0:T(8,128)(2,1)S(1)}, u32[]{:S(2)}, u32[]{:S(2)}) collective-permute-start(bf16[128,128]{1,0:T(8,128)(2,1)S(1)} %get-tuple-element.67.refs_0_), channel_id=1, source_target_pairs={{0,16},{8,24},{16,0},{24,8},{1,17},{9,25},{17,1},{25,9},{2,18},{10... | collective-permute-start | bytes 98312 | tf_op jit(solution)/shard_map/ppermute | solution.py:468
  7.6 4.8 %collective-permute-start = (bf16[128,128]{1,0:T(8,128)(2,1)S(1)}, bf16[128,128]{1,0:T(8,128)(2,1)S(1)}, u32[]{:S(2)}, u32[]{:S(2)}) collective-permute-start(bf16[128,128]{1,0:T(8,128)(2,1)S(1)} %get-tuple-element.67.refs_0_), channel_id=1, source_target_pairs={{0,8},{8,0},{16,24},{24,16},{1,9},{9,1},{17,25},{25,17},{2,10},{10... | collective-permute-start | bytes 98312 | tf_op jit(solution)/shard_map/ppermute | solution.py:468
  14.4 7.2 %collective-permute-start.10 = (bf16[1,464,128]{2,1,0:T(8,128)(2,1)S(1)}, bf16[1,464,128]{2,1,0:T(8,128)(2,1)S(1)}, u32[]{:S(2)}, u32[]{:S(2)}) collective-permute-start(bf16[1,464,128]{2,1,0:T(8,128)(2,1)S(1)} %get-tuple-element.83.first), channel_id=1, source_target_pairs={{0,2},{1,3},{2,0},{3,1},{4,6},{5,7},{6,4},{7,5},{8,10},{9,11},{10,... | collective-permute-start | bytes 356360 | tf_op jit(solution)/shard_map/ppermute | solution.py:471
  15.9 5.7 %collective-permute-start.11 = (bf16[1,464,128]{2,1,0:T(8,128)(2,1)S(1)}, bf16[1,464,128]{2,1,0:T(8,128)(2,1)S(1)}, u32[]{:S(2)}, u32[]{:S(2)}) collective-permute-start(bf16[1,464,128]{2,1,0:T(8,128)(2,1)S(1)} %get-tuple-element.85.first), channel_id=1, source_target_pairs={{0,4},{1,5},{2,6},{3,7},{4,0},{5,1},{6,2},{7,3},{8,12},{9,13},{10,... | collective-permute-start | bytes 356360 | tf_op jit(solution)/shard_map/ppermute | solution.py:471
  18.1 5.3 %collective-permute-start.4 = (bf16[22,16,128]{2,1,0:T(8,128)(2,1)S(1)}, bf16[22,16,128]{2,1,0:T(8,128)(2,1)S(1)}, u32[]{:S(2)}, u32[]{:S(2)}) collective-permute-start(bf16[22,16,128]{2,1,0:T(8,128)(2,1)S(1)} %get-tuple-element.74), channel_id=1, source_target_pairs={{0,2},{1,3},{2,0},{3,1},{4,6},{5,7},{6,4},{7,5},{8,10},{9,11},{10,... | collective-permute-start | bytes 270344 | tf_op jit(solution)/shard_map/ppermute | solution.py:471
  18.7 6.5 %collective-permute-start.5 = (bf16[22,16,128]{2,1,0:T(8,128)(2,1)S(1)}, bf16[22,16,128]{2,1,0:T(8,128)(2,1)S(1)}, u32[]{:S(2)}, u32[]{:S(2)}) collective-permute-start(bf16[22,16,128]{2,1,0:T(8,128)(2,1)S(1)} %get-tuple-element.75), channel_id=1, source_target_pairs={{0,4},{1,5},{2,6},{3,7},{4,0},{5,1},{6,2},{7,3},{8,12},{9,13},{10,... | collective-permute-start | bytes 270344 | tf_op jit(solution)/shard_map/ppermute | solution.py:471
  19.5 5.6 %collective-permute-start.6 = (bf16[22,16,128]{2,1,0:T(8,128)(2,1)S(1)}, bf16[22,16,128]{2,1,0:T(8,128)(2,1)S(1)}, u32[]{:S(2)}, u32[]{:S(2)}) collective-permute-start(bf16[22,16,128]{2,1,0:T(8,128)(2,1)S(1)} %get-tuple-element.76), channel_id=1, source_target_pairs={{0,6},{1,7},{2,4},{3,5},{4,2},{5,3},{6,0},{7,1},{8,14},{9,15},{10,... | collective-permute-start | bytes 270344 | tf_op jit(solution)/shard_map/ppermute | solution.py:471
  25.1 11.1 %collective-permute-start.13 = (bf16[2,464,128]{2,1,0:T(8,128)(2,1)S(1)}, bf16[2,464,128]{2,1,0:T(8,128)(2,1)S(1)}, u32[]{:S(2)}, u32[]{:S(2)}) collective-permute-start(bf16[2,464,128]{2,1,0:T(8,128)(2,1)S(1)} %shard_map.61.first), channel_id=1, source_target_pairs={{0,2},{1,3},{2,0},{3,1},{4,6},{5,7},{6,4},{7,5},{8,10},{9,11},{10,... | collective-permute-start | bytes 712712 | tf_op jit(solution)/shard_map/ppermute | solution.py:471
  26.7 9.5 %collective-permute-start.12 = (bf16[2,464,128]{2,1,0:T(8,128)(2,1)S(1)}, bf16[2,464,128]{2,1,0:T(8,128)(2,1)S(1)}, u32[]{:S(2)}, u32[]{:S(2)}) collective-permute-start(bf16[2,464,128]{2,1,0:T(8,128)(2,1)S(1)} %shard_map.60.first), channel_id=1, source_target_pairs={{0,4},{1,5},{2,6},{3,7},{4,0},{5,1},{6,2},{7,3},{8,12},{9,13},{10,... | collective-permute-start | bytes 712712 | tf_op jit(solution)/shard_map/ppermute | solution.py:471
  28.6 5.8 %collective-permute-start.9 = (bf16[8,16,128]{2,1,0:T(8,128)(2,1)S(1)}, bf16[8,16,128]{2,1,0:T(8,128)(2,1)S(1)}, u32[]{:S(2)}, u32[]{:S(2)}) collective-permute-start(bf16[8,16,128]{2,1,0:T(8,128)(2,1)S(1)} %get-tuple-element.89.refs_6_), channel_id=1, source_target_pairs={{0,24},{8,16},{16,8},{24,0},{1,25},{9,17},{17,9},{25,1},{2,26},{10... | collective-permute-start | bytes 98312 | tf_op jit(solution)/shard_map/ppermute | solution.py:468
  31.4 4.8 %collective-permute-start.8 = (bf16[8,16,128]{2,1,0:T(8,128)(2,1)S(1)}, bf16[8,16,128]{2,1,0:T(8,128)(2,1)S(1)}, u32[]{:S(2)}, u32[]{:S(2)}) collective-permute-start(bf16[8,16,128]{2,1,0:T(8,128)(2,1)S(1)} %get-tuple-element.89.refs_6_), channel_id=1, source_target_pairs={{0,16},{8,24},{16,0},{24,8},{1,17},{9,25},{17,1},{25,9},{2,18},{10... | collective-permute-start | bytes 98312 | tf_op jit(solution)/shard_map/ppermute | solution.py:468
  31.4 4.8 %collective-permute-start.7 = (bf16[8,16,128]{2,1,0:T(8,128)(2,1)S(1)}, bf16[8,16,128]{2,1,0:T(8,128)(2,1)S(1)}, u32[]{:S(2)}, u32[]{:S(2)}) collective-permute-start(bf16[8,16,128]{2,1,0:T(8,128)(2,1)S(1)} %get-tuple-element.89.refs_6_), channel_id=1, source_target_pairs={{0,8},{8,0},{16,24},{24,16},{1,9},{9,1},{17,25},{25,17},{2,10},{10... | collective-permute-start | bytes 98312 | tf_op jit(solution)/shard_map/ppermute | solution.py:468
  36.4 8.4 %collective-permute-start.15 = (bf16[4,464,128]{2,1,0:T(8,128)(2,1)S(1)}, bf16[4,464,128]{2,1,0:T(8,128)(2,1)S(1)}, u32[]{:S(2)}, u32[]{:S(2)}) collective-permute-start(bf16[4,464,128]{2,1,0:T(8,128)(2,1)S(1)} %shard_map.64.refs_4_), channel_id=1, source_target_pairs={{0,1},{1,0},{2,3},{3,2},{4,5},{5,4},{6,7},{7,6},{8,9},{9,8},{10,11... | collective-permute-start | bytes 1425416 | tf_op jit(solution)/shard_map/ppermute | solution.py:471
  40.4 6.2 %collective-permute-start.18 = (bf16[8,16,128]{2,1,0:T(8,128)(2,1)S(1)}, bf16[8,16,128]{2,1,0:T(8,128)(2,1)S(1)}, u32[]{:S(2)}, u32[]{:S(2)}) collective-permute-start(bf16[8,16,128]{2,1,0:T(8,128)(2,1)S(1)} %get-tuple-element.96.refs_6_), channel_id=1, source_target_pairs={{0,24},{8,16},{16,8},{24,0},{1,25},{9,17},{17,9},{25,1},{2,26},{10... | collective-permute-start | bytes 98312 | tf_op jit(solution)/shard_map/ppermute | solution.py:468
  42.2 4.9 %collective-permute-start.17 = (bf16[8,16,128]{2,1,0:T(8,128)(2,1)S(1)}, bf16[8,16,128]{2,1,0:T(8,128)(2,1)S(1)}, u32[]{:S(2)}, u32[]{:S(2)}) collective-permute-start(bf16[8,16,128]{2,1,0:T(8,128)(2,1)S(1)} %get-tuple-element.96.refs_6_), channel_id=1, source_target_pairs={{0,16},{8,24},{16,0},{24,8},{1,17},{9,25},{17,1},{25,9},{2,18},{10... | collective-permute-start | bytes 98312 | tf_op jit(solution)/shard_map/ppermute | solution.py:468
  42.6 4.6 %collective-permute-start.16 = (bf16[8,16,128]{2,1,0:T(8,128)(2,1)S(1)}, bf16[8,16,128]{2,1,0:T(8,128)(2,1)S(1)}, u32[]{:S(2)}, u32[]{:S(2)}) collective-permute-start(bf16[8,16,128]{2,1,0:T(8,128)(2,1)S(1)} %get-tuple-element.96.refs_6_), channel_id=1, source_target_pairs={{0,8},{8,0},{16,24},{24,16},{1,9},{9,1},{17,25},{25,17},{2,10},{10... | collective-permute-start | bytes 98312 | tf_op jit(solution)/shard_map/ppermute | solution.py:468
  52.3 5.4 %collective-permute-start.20 = (bf16[8,16,128]{2,1,0:T(8,128)(2,1)S(1)}, bf16[8,16,128]{2,1,0:T(8,128)(2,1)S(1)}, u32[]{:S(2)}, u32[]{:S(2)}) collective-permute-start(bf16[8,16,128]{2,1,0:T(8,128)(2,1)S(1)} %get-tuple-element.99), channel_id=1, source_target_pairs={{0,16},{8,24},{16,0},{24,8},{1,17},{9,25},{17,1},{25,9},{2,18},{10... | collective-permute-start | bytes 98312 | tf_op jit(solution)/shard_map/ppermute | solution.py:468
  53.6 5.7 %collective-permute-start.21 = (bf16[8,16,128]{2,1,0:T(8,128)(2,1)S(1)}, bf16[8,16,128]{2,1,0:T(8,128)(2,1)S(1)}, u32[]{:S(2)}, u32[]{:S(2)}) collective-permute-start(bf16[8,16,128]{2,1,0:T(8,128)(2,1)S(1)} %get-tuple-element.100), channel_id=1, source_target_pairs={{0,24},{8,16},{16,8},{24,0},{1,25},{9,17},{17,9},{25,1},{2,26},{10... | collective-permute-start | bytes 98312 | tf_op jit(solution)/shard_map/ppermute | solution.py:468
  60.9 4.9 %collective-permute-start.23 = (bf16[8,16,128]{2,1,0:T(8,128)(2,1)S(1)}, bf16[8,16,128]{2,1,0:T(8,128)(2,1)S(1)}, u32[]{:S(2)}, u32[]{:S(2)}) collective-permute-start(bf16[8,16,128]{2,1,0:T(8,128)(2,1)S(1)} %get-tuple-element.104), channel_id=1, source_target_pairs={{0,16},{8,24},{16,0},{24,8},{1,17},{9,25},{17,1},{25,9},{2,18},{10... | collective-permute-start | bytes 98312 | tf_op jit(solution)/shard_map/ppermute | solution.py:468
  63.0 5.7 %collective-permute-start.24 = (bf16[8,16,128]{2,1,0:T(8,128)(2,1)S(1)}, bf16[8,16,128]{2,1,0:T(8,128)(2,1)S(1)}, u32[]{:S(2)}, u32[]{:S(2)}) collective-permute-start(bf16[8,16,128]{2,1,0:T(8,128)(2,1)S(1)} %get-tuple-element.105), channel_id=1, source_target_pairs={{0,24},{8,16},{16,8},{24,0},{1,25},{9,17},{17,9},{25,1},{2,26},{10... | collective-permute-start | bytes 98312 | tf_op jit(solution)/shard_map/ppermute | solution.py:468
  71.2 5.0 %collective-permute-start.27 = (bf16[12,16,128]{2,1,0:T(8,128)(2,1)S(1)}, bf16[12,16,128]{2,1,0:T(8,128)(2,1)S(1)}, u32[]{:S(2)}, u32[]{:S(2)}) collective-permute-start(bf16[12,16,128]{2,1,0:T(8,128)(2,1)S(1)} %get-tuple-element.112), channel_id=1, source_target_pairs={{0,6},{1,7},{2,4},{3,5},{4,2},{5,3},{6,0},{7,1},{8,14},{9,15},{10,... | collective-permute-start | bytes 147464 | tf_op jit(solution)/shard_map/ppermute | solution.py:471
  79.4 4.9 %collective-permute-start.33 = (bf16[128,128]{1,0:T(8,128)(2,1)S(1)}, bf16[128,128]{1,0:T(8,128)(2,1)S(1)}, u32[]{:S(2)}, u32[]{:S(2)}) collective-permute-start(bf16[128,128]{1,0:T(8,128)(2,1)S(1)} %get-tuple-element.115), channel_id=1, source_target_pairs={{0,16},{8,24},{16,0},{24,8},{1,17},{9,25},{17,1},{25,9},{2,18},{10... | collective-permute-start | bytes 98312 | tf_op jit(solution)/shard_map/ppermute | solution.py:468
  82.3 5.7 %collective-permute-start.34 = (bf16[128,128]{1,0:T(8,128)(2,1)S(1)}, bf16[128,128]{1,0:T(8,128)(2,1)S(1)}, u32[]{:S(2)}, u32[]{:S(2)}) collective-permute-start(bf16[128,128]{1,0:T(8,128)(2,1)S(1)} %get-tuple-element.116), channel_id=1, source_target_pairs={{0,24},{8,16},{16,8},{24,0},{1,25},{9,17},{17,9},{25,1},{2,26},{10... | collective-permute-start | bytes 98312 | tf_op jit(solution)/shard_map/ppermute | solution.py:468
  (18 other events, 62.5 us)

commit v4 on v3

--- a/solution.py
+++ b/solution.py
@@ -40,27 +40,25 @@
         return [2 * chip + core for core in range(2) for chip in range(self.chips)]
 
 
-def call(plan, body, outs, args, scratch=(), scalars=1, raw=()):
+def call(plan, body, outs, args, scratch=(), scalars=0, raw=(), raw_out=False, aliases=None):
+    def kernel(*refs):
+        body(plan, (lax.axis_index("row"), lax.axis_index("col")), *refs)
+
     specs = [pl.BlockSpec(memory_space=pltpu.SMEM)] * scalars
     specs += [pl.BlockSpec(memory_space=pltpu.HBM if n in raw else pltpu.VMEM) for n in range(scalars, len(args))]
     return pl.pallas_call(
-        functools.partial(body, plan),
+        kernel,
         out_shape=outs,
         in_specs=specs,
-        out_specs=[pl.BlockSpec(memory_space=pltpu.VMEM)] * len(outs),
+        out_specs=[pl.BlockSpec(memory_space=pltpu.HBM if raw_out else pltpu.VMEM)] * len(outs),
         scratch_shapes=list(scratch),
+        input_output_aliases=aliases or {},
         compiler_params=pltpu.CompilerParams(vmem_limit_bytes=plan.vmem_bytes),
     )(*args)
 
 
-def row_order(values):
-    values = list(values)
-    return values[:1] + values[-1:] + values[1:-1]
-
-
 def chip_order(values):
-    values = list(values)
-    return values[:1] + values[:0:-1]
+    return [values[0], *values[:0:-1]]
 
 
 def take(refs, count):
@@ -123,7 +121,7 @@
     return jnp.where(low_lanes(first.shape, half), first, second)
 
 
-def first_kernel(plan, sides, inverse, solved, message, sides_here, inverse_here, sems):
+def first_kernel(plan, place, sides, inverse, solved, message, sides_here, inverse_here, sems):
     copies = [
         pltpu.make_async_copy(sides.at[0], sides_here, sems.at[0]),
         pltpu.make_async_copy(inverse.at[0], inverse_here, sems.at[1]),
@@ -144,7 +142,7 @@
 def pack_kernel(plan, place, rows, cols, *refs):
     refs = list(refs)
     tiles, sides, inverse = take(refs, 3)
-    first, side_slices, inverse_one = take(refs, 3)
+    dense, side_slices, inverse_one = take(refs, 3)
     payloads = take(refs, plan.levels - 1)
     tiles_here, sides_here, inverse_here, sems = refs
     copies = [
@@ -159,12 +157,20 @@
     half = plan.block
     lane = lax.broadcasted_iota(jnp.int32, (16, 128), 1)
     for coupling in range(plan.levels):
-        target = payloads[coupling - 1].at[0] if coupling else first
+        if coupling == 0:
+            dense[...] = jnp.zeros_like(dense)
+            for t in range(plan.tiles):
+                tile = tiles_here[0, t]
+                col = cols[0, t, 0]
+                both = jnp.concatenate([tile, tile], axis=1).astype(F32)
+                here = (lax.broadcasted_iota(jnp.int32, both.shape, 1) // half) == col % 2
+                at = pl.ds(pl.multiple_of(rows[0, t, 0] * half, half), half)
+                dense[col // 2, at, :] += jnp.where(here, both, 0.0).astype(BF16)
+            continue
+        target = payloads[coupling - 1].at[0]
         for k in range(plan.tiles // 2):
             pair = jnp.concatenate([tiles_here[coupling, 2 * k], tiles_here[coupling, 2 * k + 1]], axis=1)
             target[k * half : (k + 1) * half, :] = pair
-        if coupling == 0:
-            continue
         index = jnp.zeros((16, 128), F32)
         for t in range(plan.tiles):
             index = jnp.where(lane == t, rows[coupling, t, 0].astype(F32), index)
@@ -178,28 +184,25 @@
         pad_slices(plan, both, side_slices.at[level - 1])
 
 
-def near_forward_kernel(plan, place, rows, cols, pairs, *refs):
+def near_forward_kernel(plan, place, dense, *refs):
     refs = list(refs)
     received = take(refs, plan.n_row)
     side_slices, inverse_one = take(refs, 2)
-    keep, keep_extra, send, left, right, total = refs
-    half, width = plan.block, plan.slice
-    for m in range(plan.n_row):
-        store_halves(left, right, place[0] ^ m, received[m][...].astype(F32), half)
-    total[...] = jnp.zeros_like(total)
-    for k in range(plan.tiles // 2):
-        pair = pairs[k * half : (k + 1) * half, :]
-        vectors = jnp.concatenate([left[cols[0, 2 * k, 0]], right[cols[0, 2 * k + 1, 0]]], axis=0)
-        product = lax.dot_general(vectors, pair, NT, preferred_element_type=F32)
-        total[rows[0, 2 * k, 0]] += product[: plan.padded]
-        total[rows[0, 2 * k + 1, 0]] += product[plan.padded :]
+    keep, keep_extra, send, total = refs
+    width, lanes = plan.slice, plan.lanes
+    vectors = jnp.concatenate([ref[...] for ref in received], axis=1)
+    for u in range(0, plan.n_col, 2):
+        matrix = [dense[place[0] ^ m, u * lanes : (u + 2) * lanes, :] for m in range(plan.n_row)]
+        matrix = jnp.concatenate(matrix, axis=1)
+        product = lax.dot_general(vectors, matrix, NT, preferred_element_type=F32)
+        for n in range(2):
+            total[u + n] = product[:, n * lanes : (n + 1) * lanes]
     for chip in range(plan.chips):
         for core, (out, extra, at) in enumerate(((keep, keep_extra, 0), (send, send, plan.n_col))):
             number = place[1] ^ (2 * chip + core)
             here = pl.ds(pl.multiple_of(number * width, 16), width)
             for u in range(plan.n_col):
-                value = jnp.concatenate([total[2 * u, here, :], total[2 * u + 1, here, :]], axis=1)
-                out[chip, u] = value.astype(out.dtype)
+                out[chip, u] = total[u, here, :].astype(out.dtype)
             for level in range(plan.levels):
                 extra[chip, at + level] = side_slices[level, here, :]
             extra[chip, at + plan.levels : at + plan.extra()] = inverse_one[...]
@@ -208,7 +211,6 @@
 def add_kernel(plan, place, keep, keep_extra, received, own, *out):
     here = plan.n_col + (place[1] & 1) * plan.extra()
     there = plan.n_col + (1 - (place[1] & 1)) * plan.extra()
-    out = chip_order(out)
     own[...] = keep[0] + received[0, : plan.n_col].astype(F32)
     for chip in range(plan.chips):
         if chip:
@@ -218,36 +220,28 @@
         out[chip][pl.ds(there, plan.extra())] = received[chip, plan.n_col :]
 
 
-def near_backward_kernel(plan, place, rows, cols, pairs, *refs):
+def near_backward_kernel(plan, place, dense, *refs):
     refs = list(refs)
     received = take(refs, plan.n_col)
-    out = row_order(take(refs, plan.n_row))
-    upper, left, right = refs
-    half, width = plan.block, plan.slice
+    out = take(refs, plan.n_row)
+    (upper,) = refs
+    width, lanes = plan.slice, plan.lanes
     for piece, offset in zip(received, plan.sources()):
         here = pl.ds(pl.multiple_of((place[1] ^ offset) * width, 16), width)
         for u in range(plan.n_col):
-            value = piece[u]
-            upper[2 * u, here, :] = value[:, :half]
-            upper[2 * u + 1, here, :] = value[:, half:]
-    left[...] = jnp.zeros_like(left)
-    right[...] = jnp.zeros_like(right)
-    for k in range(plan.tiles // 2):
-        pair = pairs[k * half : (k + 1) * half, :]
-        vectors = jnp.concatenate([upper[rows[0, 2 * k, 0]], upper[rows[0, 2 * k + 1, 0]]], axis=0)
-        product = jnp.dot(vectors, pair, preferred_element_type=F32)
-        left[cols[0, 2 * k, 0]] += product[: plan.padded]
-        right[cols[0, 2 * k + 1, 0]] += product[plan.padded :]
-    for m in range(plan.n_row):
-        out[m][...] = join_halves(left, right, place[0] ^ m, half).astype(out[m].dtype)
-
-
-def last_kernel(plan, place, *refs):
-    refs = list(refs)
-    inverse, solved = take(refs, 2)
-    shares = take(refs, plan.n_row)
+            upper[here, u * lanes : (u + 1) * lanes] = piece[u]
+    vectors = upper[...]
+    for m in range(0, plan.n_row, 2):
+        matrix = jnp.concatenate([dense[place[0] ^ m], dense[place[0] ^ (m + 1)]], axis=1)
+        product = jnp.dot(vectors, matrix, preferred_element_type=F32)
+        for n in range(2):
+            out[m + n][...] = product[:, n * lanes : (n + 1) * lanes].astype(out[m + n].dtype)
+
+
+def upper_out_kernel(plan, place, *refs):
+    refs = list(refs)
     pieces = take(refs, plan.n_col)
-    out, all_slices = refs
+    out, all_slices, result, sem = refs
     half, width = plan.block, plan.slice
     core = place[1] & 1
     for piece, offset in zip(pieces, plan.sources()):
@@ -258,15 +252,28 @@
     for n in range(plan.levels):
         value = drop_padding(plan, all_slices[n].astype(F32)).T
         for b in range(plan.rows_dev):
-            out[n + 1, b] = value[b * half : (b + 1) * half, :]
+            result[n, b] = value[b * half : (b + 1) * half, :]
+    copy = pltpu.make_async_copy(result, out.at[1:], sem)
+    copy.start()
+    copy.wait()
+
+
+def last_kernel(plan, place, inverse, solved, *refs):
+    refs = list(refs)
+    shares = take(refs, plan.n_row)
+    _, out, result, sem = refs
+    half = plan.block
     back = shares[0][...].astype(F32)
     for share in shares[1:]:
         back = back + share[...].astype(F32)
     value = drop_padding(plan, solved[...] - back)
     for b in range(plan.rows_dev):
         cut = slice(b * half, (b + 1) * half)
-        out[0, b] = lax.dot_general(inverse[0, :, cut], value[:, cut], NT,
+        result[b] = lax.dot_general(inverse[0, :, cut], value[:, cut], NT,
                                     precision=lax.Precision.HIGHEST, preferred_element_type=F32)
+    copy = pltpu.make_async_copy(result, out.at[0], sem)
+    copy.start()
+    copy.wait()
 
 
 def extras(plan, place, sums):
@@ -282,20 +289,25 @@
 
 
 def level_forward(plan, place, level, sums, pieces, coupled, write):
+    made = []
     for extra, piece, offset in zip(extras(plan, place, sums), pieces, plan.sources()):
         u = place[1] ^ offset
         side = extra[0][extra[1] + level - 1].astype(F32)
         inverse = inverse_of(plan, level, extra, piece)
-        write(inverse, u, apply_pair(inverse, side - coupled(u), plan.block))
+        made.append((inverse, u, apply_pair(inverse, side - coupled(u), plan.block)))
+    write(made)
 
 
 def level_backward(plan, place, level, sums, pieces, value, write):
+    made = []
     for extra, piece, offset in zip(extras(plan, place, sums), pieces, plan.sources()):
         u = place[1] ^ offset
-        write(u, apply_pair_transposed(inverse_of(plan, level, extra, piece), value(u), plan.block))
-
-
-def join_kernel(plan, first, second, out):
+        made.append((u, apply_pair_transposed(inverse_of(plan, level, extra, piece), value(u), plan.block)))
+    for u, value in made:
+        write(u, value)
+
+
+def join_kernel(plan, place, first, second, out):
     count = first.shape[0]
     out[:count] = first[...]
     out[count:] = second[...]
@@ -321,15 +333,16 @@
 
 def enter_kernel(plan, place, *refs):
     refs = list(refs)
-    sums = take(refs, plan.chips + 1)
+    own, sums = refs.pop(0), chip_order(take(refs, plan.chips))
     solved, message = refs
 
-    def write(inverse, u, value):
-        solved[u] = value
-        message[u] = value.astype(BF16)
-
-    coupled = add_up([sums[0]] + sums[2:])
-    level_forward(plan, place, 1, sums[1:], [None] * plan.n_col, coupled, write)
+    def write(made):
+        for _, u, value in made:
+            solved[u] = value
+            message[u] = value.astype(BF16)
+
+    coupled = add_up([own] + sums[1:])
+    level_forward(plan, place, 1, sums, [None] * plan.n_col, coupled, write)
 
 
 def decode(plan, place, pieces, index):
@@ -380,11 +393,11 @@
 def forward_kernel(coupling, plan, place, *refs):
     refs = list(refs)
     last = coupling == plan.levels - 1
-    sums, pieces = take(refs, plan.chips), views(plan, coupling, take(refs, 2))
+    sums, pieces = chip_order(take(refs, plan.chips)), views(plan, coupling, take(refs, 2))
     received = take(refs, plan.n_row)
     keep = refs.pop(0)
     if last:
-        out = row_order(take(refs, plan.n_row))
+        out = take(refs, plan.n_row)
     else:
         message, index_out = take(refs, 2)
     left, right, total, index, sem = take(refs, 5)
@@ -400,31 +413,35 @@
 
     if not last:
 
-        def write(inverse, u, value):
-            keep[u] = value
-            message[u] = value.astype(BF16)
+        def write(made):
+            for _, u, value in made:
+                keep[u] = value
+                message[u] = value.astype(BF16)
 
         level_forward(plan, place, coupling + 1, sums, pieces, coupled, write)
         return
     back_left[...] = jnp.zeros_like(back_left)
     back_right[...] = jnp.zeros_like(back_right)
 
-    def write_top(inverse, u, value):
-        value = apply_pair_transposed(inverse, value, plan.block)
-        keep[u] = value.astype(BF16)
-        put_upper(plan, upper, u, value)
+    def write_top(made):
+        made = [(u, apply_pair_transposed(inverse, value, plan.block)) for inverse, u, value in made]
+        for u, value in made:
+            keep[u] = value.astype(BF16)
+            put_upper(plan, upper, u, value)
 
     level_forward(plan, place, plan.levels, sums, pieces, coupled, write_top)
     multiply_backward(plan, place, pieces, index, upper, back_left, back_right, out)
 
 
-def backward_kernel(level, plan, place, index, *refs):
-    refs = list(refs)
-    sums, pieces = take(refs, plan.chips), views(plan, level - 1, take(refs, 2))
+def backward_kernel(level, plan, place, index_here, *refs):
+    refs = list(refs)
+    sums, pieces = chip_order(take(refs, plan.chips)), views(plan, level - 1, take(refs, 2))
     shares = take(refs, plan.n_row)
     solved, keep = take(refs, 2)
-    out = row_order(take(refs, plan.n_row))
-    upper, left, right = refs
+    out = take(refs, plan.n_row)
+    upper, left, right, index, sem = refs
+    copy = pltpu.make_async_copy(index_here, index, sem)
+    copy.start()
     left[...] = jnp.zeros_like(left)
     right[...] = jnp.zeros_like(right)
     back = add_up(shares)
@@ -434,14 +451,15 @@
         put_upper(plan, upper, u, value)
 
     level_backward(plan, place, level, sums, pieces, lambda u: solved[u] - back(u), write)
+    copy.wait()
     multiply_backward(plan, place, pieces, index, upper, left, right, out)
 
 
 def leave_kernel(plan, place, *refs):
     refs = list(refs)
-    sums, shares = take(refs, plan.chips), take(refs, plan.n_row)
+    sums, shares = chip_order(take(refs, plan.chips)), take(refs, plan.n_row)
     solved = refs.pop(0)
-    above, out = take(refs, plan.levels - 1), chip_order(refs)
+    above, out = take(refs, plan.levels - 1), refs
     back = add_up(shares)
 
     def write(u, value):
@@ -459,7 +477,6 @@
 def on_device(n_row, n_col, factor_tiles, tile_row, tile_col, right_sides, diag_inverse):
     plan = Plan(n_row, n_col, factor_tiles, right_sides)
     levels, chips = plan.levels, plan.chips
-    place = jnp.stack([lax.axis_index("row"), lax.axis_index("col")]).astype(jnp.int32)
 
     def array(shape, kind=BF16):
         return jax.ShapeDtypeStruct(shape, kind)
@@ -470,9 +487,11 @@
     def over_col(value, m):
         return lax.ppermute(value, "col", [(i, i ^ m) for i in range(n_col)])
 
+    def gather_row(value):
+        return [value] + [over_row(value, m) for m in range(1, n_row)]
+
     def exchange_row(values):
-        got = {m: over_row(values[m], m) for m in [*range(2, n_row), 1]}
-        return [values[0]] + [got[m] for m in range(1, n_row)]
+        return [values[0]] + [over_row(values[m], m) for m in range(n_row - 1, 0, -1)]
 
     def exchange_chips(values):
         return [values[0]] + [over_col(values[m], 2 * m) for m in range(1, chips)]
@@ -486,24 +505,24 @@
     x0, message = call(
         plan, first_kernel, [array(column, F32), array(column)], (right_sides, diag_inverse),
         [pltpu.VMEM(right_sides.shape[1:], F32), pltpu.VMEM(diag_inverse.shape[1:], F32), dma((2,))],
-        scalars=0, raw=(0, 1),
-    )
-    (message, place, tile_row, tile_col) = lax.optimization_barrier((message, place, tile_row, tile_col))
-    received = exchange_row([message] * n_row)
-    pairs, side_slices, inverse_one, *held = call(
+        raw=(0, 1),
+    )
+    message, tile_row, tile_col = lax.optimization_barrier((message, tile_row, tile_col))
+    received = gather_row(message)
+    dense, side_slices, inverse_one, *held = call(
         plan, pack_kernel,
-        [array((plan.tile_rows, plan.lanes)), array((levels,) + column),
+        [array((n_row, plan.own * plan.block, plan.lanes)), array((levels,) + column),
          array((plan.block // plan.slice, plan.slice, plan.lanes))]
         + [array((1, plan.payload_rows(), plan.lanes))] * (levels - 1),
-        (place, tile_row, tile_col, factor_tiles, right_sides, diag_inverse),
+        (tile_row, tile_col, factor_tiles, right_sides, diag_inverse),
         [pltpu.VMEM(factor_tiles.shape, BF16), pltpu.VMEM(right_sides.shape, F32),
          pltpu.VMEM(diag_inverse.shape, F32), dma((3,))],
-        scalars=3, raw=(3, 4, 5),
+        scalars=2, raw=(2, 3, 4),
     )
 
     def join(held, other):
         shape = (2 * held.shape[0],) + held.shape[1:]
-        return call(plan, join_kernel, [array(shape)], [held, other], scalars=0)[0]
+        return call(plan, join_kernel, [array(shape)], [held, other])[0]
 
     def step(held, coupling):
         bit = held.shape[0] if coupling % 2 else chips // 2 // held.shape[0]
@@ -514,22 +533,20 @@
         plan, near_forward_kernel,
         [array((chips,) + slices, F32), array((chips, plan.extra()) + slices[1:]),
          array((chips, n_col + plan.extra()) + slices[1:])],
-        [place, tile_row, tile_col, pairs] + received + [side_slices, inverse_one],
-        [pltpu.VMEM((n_row * plan.rows_dev,) + column, BF16), pltpu.VMEM((n_row * plan.rows_dev,) + column, BF16),
-         pltpu.VMEM((plan.own, plan.padded, plan.block), F32)],
-        scalars=3,
+        [dense] + received + [side_slices, inverse_one],
+        [pltpu.VMEM((n_col,) + column, F32)],
     )
     swapped = over_col(send, 1)
     made = call(
         plan, add_kernel, [array(slices, F32)] + [array((n_col + 2 * plan.extra(),) + slices[1:])] * chips,
-        [place, keep, keep_extra, swapped],
-    )
-    own, sums = made[0], exchange_chips(chip_order(made[1:]))
+        [keep, keep_extra, swapped],
+    )
+    own, sums = made[0], exchange_chips(made[1:])
     held = [join(*value) for value in after(held, sums)]
     if chips > 2:
         held = [step(value, s) for s, value in enumerate(held, 1)]
     solved, message = call(
-        plan, enter_kernel, [array(slices, F32), array(slices)], [place, own] + sums
+        plan, enter_kernel, [array(slices, F32), array(slices)], [own] + chip_order(sums)
     )
     solved = [None, solved]
 
@@ -550,14 +567,14 @@
     index = [None] * levels
     pieces = [None]
     for s in range(1, levels):
-        received = exchange_row([message] * n_row)
+        received = gather_row(message)
         if s == 1 and chips > 2:
             received, held = lax.optimization_barrier((received, held))
             held = [join(*value) for value in held]
             while held[0].shape[0] < chips:
                 held = [join(*step(value, n)) for n, value in enumerate(held, 1)]
         pieces.append([held[s - 1], over_col(held[s - 1], 1)])
-        args = [place] + sums + pieces[s] + received
+        args = chip_order(sums) + pieces[s] + received
         if s < levels - 1:
             value, message, index[s] = call(
                 plan, functools.partial(forward_kernel, s),
@@ -570,32 +587,36 @@
                 forward + [pltpu.VMEM(index_shape, jnp.int32)] + backward,
             )
     results = [made[0]]
-    shares = exchange_row(row_order(made[1:]))
+    shares = exchange_row(made[1:])
     for level in range(levels - 1, 1, -1):
         made = call(
             plan, functools.partial(backward_kernel, level), [array(slices)] + partial,
-            [place, index[level - 1]] + sums + pieces[level - 1] + shares + [solved[level]],
-            backward, scalars=2,
+            [index[level - 1]] + chip_order(sums) + pieces[level - 1] + shares + [solved[level]],
+            backward + [pltpu.SMEM(index_shape, jnp.int32), dma(())],
         )
         results.insert(0, made[0])
-        shares = exchange_row(row_order(made[1:]))
+        shares = exchange_row(made[1:])
     messages = call(
         plan, leave_kernel, [array((n_col + 2 * (levels - 1),) + slices[1:])] * chips,
-        [place] + sums + shares + [solved[1]] + results,
-    )
-    messages = exchange_chips(chip_order(messages))
+        chip_order(sums) + shares + [solved[1]] + results,
+    )
+    messages = exchange_chips(messages)
     messages = messages + [over_col(value, 1) for value in messages]
     shares = call(
-        plan, near_backward_kernel, [array(column, F32)] + [array(column)] * (n_row - 1),
-        [place, tile_row, tile_col, pairs] + messages,
-        [pltpu.VMEM((plan.own, plan.padded, plan.block), BF16),
-         pltpu.VMEM((n_row * plan.rows_dev,) + column, F32), pltpu.VMEM((n_row * plan.rows_dev,) + column, F32)],
-        scalars=3,
-    )
-    shares = exchange_row(row_order(shares))
+        plan, near_backward_kernel, [array(column, F32)] + [array(column)] * (n_row - 1), [dense] + messages,
+        [pltpu.VMEM((plan.padded, n_col * plan.lanes), BF16)],
+    )
+    shares = exchange_row(shares)
+    result = array(right_sides.shape, F32)
+    upper = call(
+        plan, upper_out_kernel, [result], messages,
+        [pltpu.VMEM((levels,) + column, BF16), pltpu.VMEM((levels,) + right_sides.shape[1:], F32), dma(())],
+        raw_out=True,
+    )[0]
+    args = [diag_inverse, x0] + shares + [upper]
     return call(
-        plan, last_kernel, [array(right_sides.shape, F32)], [place, diag_inverse, x0] + shares + messages,
-        [pltpu.VMEM((levels,) + column, BF16)],
+        plan, last_kernel, [result], args, [pltpu.VMEM(right_sides.shape[1:], F32), dma(())],
+        raw=(len(args) - 1,), raw_out=True, aliases={len(args) - 1: 0},
     )[0]
 
 

time: 89.9 us -> 80.1 us (0.89)
  Pallas kernels: 17.4 us -> 11.5 us
  waiting for transfers between devices: 27.4 us -> 24 us
    pallas_call x15 -> x16, Pallas kernels: 17.4 us -> 11.5 us  [call(): pl.pallas_call(kernel, out_shape=outs, in_specs=specs, out_specs=[pl.Bloc...]
    ppermute x18, waiting for transfers between devices: 18.4 us -> 14 us  [over_row(): return lax.ppermute(value, 'row', [(i, i ^ m) for i in range(n_row)])]
    ppermute x17, waiting for transfers between devices: 9.02 us -> 9.98 us  [over_col(): return lax.ppermute(value, 'col', [(i, i ^ m) for i in range(n_col)])]
  transfers between devices with their start and end apart: 35 -> 35, of which waited for: 19 -> 21; matrix products, arithmetic and copies ran while one was open for 0% -> 0% of each run, Pallas kernels for 6% -> 6%
where the time goes in v4:
time: 80.1 us; the launch traced here: 80 us
  starting transfers between devices  41.1 us (51%)
  waiting for transfers between devices  24 us (30%)
  Pallas kernels  11.5 us (14%)
  local copies, waits for them, and re-layouts  3.14 us (4%)
    ppermute x18, starting transfers between devices, over_row(): return lax.ppermute(value, 'row', [(i, i ^ m) for i in range(n_row)])  28 us
    ppermute x18, waiting for transfers between devices, over_row(): return lax.ppermute(value, 'row', [(i, i ^ m) for i in range(n_row)])  14 us
    ppermute x17, starting transfers between devices, over_col(): return lax.ppermute(value, 'col', [(i, i ^ m) for i in range(n_col)])  13.1 us
    pallas_call x16, Pallas kernels, call(): pl.pallas_call(kernel, out_shape=outs, in_specs=specs, out_specs=[pl.Bloc...  11.5 us
    ppermute x17, waiting for transfers between devices, over_col(): return lax.ppermute(value, 'col', [(i, i ^ m) for i in range(n_col)])  9.98 us
    unnamed x14, local copies, waits for them, and re-layouts  2.93 us
  transfers between devices with their start and end apart: 35, of which 21 were waited for; matrix products, arithmetic and copies ran while one was open for 0% of the time, Pallas kernels for 6%

profile of v4, /device:TPU:0, one launch (start us, length us, event | category | flops | bytes accessed | tf_op | source)
XLA Modules:
  0.0 80.0 jit_solution(1135913881804259097)
XLA Ops:
  2.4 5.1 %collective-permute-start.2 = (bf16[128,128]{1,0:T(8,128)(2,1)S(1)}, bf16[128,128]{1,0:T(8,128)(2,1)S(1)}, u32[]{:S(2)}, u32[]{:S(2)}) collective-permute-start(bf16[128,128]{1,0:T(8,128)(2,1)S(1)} %get-tuple-element.65.refs_1_), channel_id=1, source_target_pairs={{0,24},{8,16},{16,8},{24,0},{1,25},{9,17},{17,9},{25,1},{2,26},{10... | collective-permute-start | bytes 98312 | tf_op jit(solution)/shard_map/ppermute | solution.py:485
  9.5 2.0 %shard_map.56 = (bf16[4,1024,128]{2,1,0:T(8,128)(2,1)S(1)}, bf16[3,128,128]{2,1,0:T(8,128)(2,1)S(1)}, bf16[4,16,128]{2,1,0:T(8,128)(2,1)S(1)}, bf16[1,464,128]{2,1,0:T(8,128)(2,1)S(1)}, bf16[1,464,128]{2,1,0:T(8,128)(2,1)S(1)}) custom-call(s32[3,12,1]{2,1,0:T(8,128)S(1)} %copy.7.refs_0_, s32[3,12,1]{2,1,0:T(8,128)S(1)} %copy.8.refs_1_, ...), custom_call_target="tpu_custom_call" | custom-call | tf_op jit(solution)/shard_map/pallas_call | solution.py:49
  13.0 1.6 %collective-permute-start.10 = (bf16[1,464,128]{2,1,0:T(8,128)(2,1)S(1)}, bf16[1,464,128]{2,1,0:T(8,128)(2,1)S(1)}, u32[]{:S(2)}, u32[]{:S(2)}) collective-permute-start(bf16[1,464,128]{2,1,0:T(8,128)(2,1)S(1)} %get-tuple-element.81.refs_0_), channel_id=1, source_target_pairs={{0,2},{1,3},{2,0},{3,1},{4,6},{5,7},{6,4},{7,5},{8,10},{9,11},{10,... | collective-permute-start | bytes 356360 | tf_op jit(solution)/shard_map/ppermute | solution.py:488
  14.5 1.5 %collective-permute-start.11 = (bf16[1,464,128]{2,1,0:T(8,128)(2,1)S(1)}, bf16[1,464,128]{2,1,0:T(8,128)(2,1)S(1)}, u32[]{:S(2)}, u32[]{:S(2)}) collective-permute-start(bf16[1,464,128]{2,1,0:T(8,128)(2,1)S(1)} %get-tuple-element.83.refs_0_), channel_id=1, source_target_pairs={{0,4},{1,5},{2,6},{3,7},{4,0},{5,1},{6,2},{7,3},{8,12},{9,13},{10,... | collective-permute-start | bytes 356360 | tf_op jit(solution)/shard_map/ppermute | solution.py:488
  18.1 1.5 %collective-permute-start.6 = (bf16[22,16,128]{2,1,0:T(8,128)(2,1)S(1)}, bf16[22,16,128]{2,1,0:T(8,128)(2,1)S(1)}, u32[]{:S(2)}, u32[]{:S(2)}) collective-permute-start(bf16[22,16,128]{2,1,0:T(8,128)(2,1)S(1)} %get-tuple-element.74), channel_id=1, source_target_pairs={{0,2},{1,3},{2,0},{3,1},{4,6},{5,7},{6,4},{7,5},{8,10},{9,11},{10,... | collective-permute-start | bytes 270344 | tf_op jit(solution)/shard_map/ppermute | solution.py:488
  19.7 1.9 %collective-permute-done.11.refs_1_ = bf16[1,464,128]{2,1,0:T(8,128)(2,1)S(1)} collective-permute-done((bf16[1,464,128]{2,1,0:T(8,128)(2,1)S(1)}, bf16[1,464,128]{2,1,0:T(8,128)(2,1)S(1)}, u32[]{:S(2)}, u32[]{:S(2)}) %collective-permute-start.11) | collective-permute-done | bytes 118816 | tf_op jit(solution)/shard_map/ppermute | solution.py:488
  24.3 1.6 %collective-permute-start.12 = (bf16[2,464,128]{2,1,0:T(8,128)(2,1)S(1)}, bf16[2,464,128]{2,1,0:T(8,128)(2,1)S(1)}, u32[]{:S(2)}, u32[]{:S(2)}) collective-permute-start(bf16[2,464,128]{2,1,0:T(8,128)(2,1)S(1)} %shard_map.60.refs_0_), channel_id=1, source_target_pairs={{0,4},{1,5},{2,6},{3,7},{4,0},{5,1},{6,2},{7,3},{8,12},{9,13},{10,... | collective-permute-start | bytes 712712 | tf_op jit(solution)/shard_map/ppermute | solution.py:488
  26.2 3.0 %collective-permute-start.9 = (bf16[8,16,128]{2,1,0:T(8,128)(2,1)S(1)}, bf16[8,16,128]{2,1,0:T(8,128)(2,1)S(1)}, u32[]{:S(2)}, u32[]{:S(2)}) collective-permute-start(bf16[8,16,128]{2,1,0:T(8,128)(2,1)S(1)} %get-tuple-element.87.refs_6_), channel_id=1, source_target_pairs={{0,24},{8,16},{16,8},{24,0},{1,25},{9,17},{17,9},{25,1},{2,26},{10... | collective-permute-start | bytes 98312 | tf_op jit(solution)/shard_map/ppermute | solution.py:485
  29.2 1.5 %collective-permute-start.7 = (bf16[8,16,128]{2,1,0:T(8,128)(2,1)S(1)}, bf16[8,16,128]{2,1,0:T(8,128)(2,1)S(1)}, u32[]{:S(2)}, u32[]{:S(2)}) collective-permute-start(bf16[8,16,128]{2,1,0:T(8,128)(2,1)S(1)} %get-tuple-element.87.refs_6_), channel_id=1, source_target_pairs={{0,8},{8,0},{16,24},{24,16},{1,9},{9,1},{17,25},{25,17},{2,10},{10... | collective-permute-start | bytes 98312 | tf_op jit(solution)/shard_map/ppermute | solution.py:485
  32.0 2.0 %collective-permute-done.8.refs_8_ = bf16[8,16,128]{2,1,0:T(8,128)(2,1)S(1)} collective-permute-done((bf16[8,16,128]{2,1,0:T(8,128)(2,1)S(1)}, bf16[8,16,128]{2,1,0:T(8,128)(2,1)S(1)}, u32[]{:S(2)}, u32[]{:S(2)}) %collective-permute-start.8) | collective-permute-done | bytes 32800 | tf_op jit(solution)/shard_map/ppermute | solution.py:485
  35.9 1.6 %shard_map.63 = (f32[8,16,128]{2,1,0:T(8,128)S(1)}, bf16[8,16,128]{2,1,0:T(8,128)(2,1)S(1)}, s32[8,128]{1,0:T(8,128)S(1)}) custom-call(bf16[22,16,128]{2,1,0:T(8,128)(2,1)S(1)} %get-tuple-element.71.refs_1_.refs_0_, bf16[22,16,128]{2,1,0:T(8,128)(2,1)S(1)} %collective-permute-done.4.refs_2_.refs_1_, ...), custom_call_target="tpu_custom_call" | custom-call | tf_op jit(solution)/shard_map/pallas_call | solution.py:49
  37.5 1.8 %collective-permute-start.18 = (bf16[8,16,128]{2,1,0:T(8,128)(2,1)S(1)}, bf16[8,16,128]{2,1,0:T(8,128)(2,1)S(1)}, u32[]{:S(2)}, u32[]{:S(2)}) collective-permute-start(bf16[8,16,128]{2,1,0:T(8,128)(2,1)S(1)} %get-tuple-element.94.refs_6_), channel_id=1, source_target_pairs={{0,24},{8,16},{16,8},{24,0},{1,25},{9,17},{17,9},{25,1},{2,26},{10... | collective-permute-start | bytes 98312 | tf_op jit(solution)/shard_map/ppermute | solution.py:485
  39.7 2.3 %collective-permute-start.16 = (bf16[8,16,128]{2,1,0:T(8,128)(2,1)S(1)}, bf16[8,16,128]{2,1,0:T(8,128)(2,1)S(1)}, u32[]{:S(2)}, u32[]{:S(2)}) collective-permute-start(bf16[8,16,128]{2,1,0:T(8,128)(2,1)S(1)} %get-tuple-element.94.refs_6_), channel_id=1, source_target_pairs={{0,8},{8,0},{16,24},{24,16},{1,9},{9,1},{17,25},{25,17},{2,10},{10... | collective-permute-start | bytes 98312 | tf_op jit(solution)/shard_map/ppermute | solution.py:485
  42.0 1.8 %collective-permute-done.18.refs_9_ = bf16[8,16,128]{2,1,0:T(8,128)(2,1)S(1)} collective-permute-done((bf16[8,16,128]{2,1,0:T(8,128)(2,1)S(1)}, bf16[8,16,128]{2,1,0:T(8,128)(2,1)S(1)}, u32[]{:S(2)}, u32[]{:S(2)}) %collective-permute-start.18) | collective-permute-done | bytes 32800 | tf_op jit(solution)/shard_map/ppermute | solution.py:485
  44.4 2.5 %shard_map.65 = (bf16[8,16,128]{2,1,0:T(8,128)(2,1)S(1)}, f32[8,16,128]{2,1,0:T(8,128)S(1)}, bf16[8,16,128]{2,1,0:T(8,128)(2,1)S(1)}, bf16[8,16,128]{2,1,0:T(8,128)(2,1)S(1)}, bf16[8,16,128]{2,1,0:T(8,128)(2,1)S(1)}) custom-call(bf16[22,16,128]{2,1,0:T(8,128)(2,1)S(1)} %get-tuple-element.71.refs_1_.refs_0_, ...), custom_call_target="tpu_custom_call" | custom-call | tf_op jit(solution)/shard_map/pallas_call | solution.py:49
  46.9 2.4 %collective-permute-start.19 = (bf16[8,16,128]{2,1,0:T(8,128)(2,1)S(1)}, bf16[8,16,128]{2,1,0:T(8,128)(2,1)S(1)}, u32[]{:S(2)}, u32[]{:S(2)}) collective-permute-start(bf16[8,16,128]{2,1,0:T(8,128)(2,1)S(1)} %get-tuple-element.96), channel_id=1, source_target_pairs={{0,24},{8,16},{16,8},{24,0},{1,25},{9,17},{17,9},{25,1},{2,26},{10... | collective-permute-start | bytes 98312 | tf_op jit(solution)/shard_map/ppermute | solution.py:485
  52.7 1.5 %collective-permute-done.20.refs_9_ = bf16[8,16,128]{2,1,0:T(8,128)(2,1)S(1)} collective-permute-done((bf16[8,16,128]{2,1,0:T(8,128)(2,1)S(1)}, bf16[8,16,128]{2,1,0:T(8,128)(2,1)S(1)}, u32[]{:S(2)}, u32[]{:S(2)}) %collective-permute-start.20) | collective-permute-done | bytes 32800 | tf_op jit(solution)/shard_map/ppermute | solution.py:485
  55.8 1.7 %collective-permute-start.22 = (bf16[8,16,128]{2,1,0:T(8,128)(2,1)S(1)}, bf16[8,16,128]{2,1,0:T(8,128)(2,1)S(1)}, u32[]{:S(2)}, u32[]{:S(2)}) collective-permute-start(bf16[8,16,128]{2,1,0:T(8,128)(2,1)S(1)} %get-tuple-element.101), channel_id=1, source_target_pairs={{0,24},{8,16},{16,8},{24,0},{1,25},{9,17},{17,9},{25,1},{2,26},{10... | collective-permute-start | bytes 98312 | tf_op jit(solution)/shard_map/ppermute | solution.py:485
  58.2 2.0 %collective-permute-start.24 = (bf16[8,16,128]{2,1,0:T(8,128)(2,1)S(1)}, bf16[8,16,128]{2,1,0:T(8,128)(2,1)S(1)}, u32[]{:S(2)}, u32[]{:S(2)}) collective-permute-start(bf16[8,16,128]{2,1,0:T(8,128)(2,1)S(1)} %get-tuple-element.103), channel_id=1, source_target_pairs={{0,8},{8,0},{16,24},{24,16},{1,9},{9,1},{17,25},{25,17},{2,10},{10... | collective-permute-start | bytes 98312 | tf_op jit(solution)/shard_map/ppermute | solution.py:485
  62.9 1.6 %collective-permute-start.25 = (bf16[12,16,128]{2,1,0:T(8,128)(2,1)S(1)}, bf16[12,16,128]{2,1,0:T(8,128)(2,1)S(1)}, u32[]{:S(2)}, u32[]{:S(2)}) collective-permute-start(bf16[12,16,128]{2,1,0:T(8,128)(2,1)S(1)} %get-tuple-element.108), channel_id=1, source_target_pairs={{0,2},{1,3},{2,0},{3,1},{4,6},{5,7},{6,4},{7,5},{8,10},{9,11},{10,... | collective-permute-start | bytes 147464 | tf_op jit(solution)/shard_map/ppermute | solution.py:488
  65.0 1.5 %collective-permute-start.27 = (bf16[12,16,128]{2,1,0:T(8,128)(2,1)S(1)}, bf16[12,16,128]{2,1,0:T(8,128)(2,1)S(1)}, u32[]{:S(2)}, u32[]{:S(2)}) collective-permute-start(bf16[12,16,128]{2,1,0:T(8,128)(2,1)S(1)} %get-tuple-element.110), channel_id=1, source_target_pairs={{0,6},{1,7},{2,4},{3,5},{4,2},{5,3},{6,0},{7,1},{8,14},{9,15},{10,... | collective-permute-start | bytes 147464 | tf_op jit(solution)/shard_map/ppermute | solution.py:488
  67.1 1.6 %collective-permute-done.26.refs_3_.refs_2_ = bf16[12,16,128]{2,1,0:T(8,128)(2,1)S(1)} collective-permute-done((bf16[12,16,128]{2,1,0:T(8,128)(2,1)S(1)}, bf16[12,16,128]{2,1,0:T(8,128)(2,1)S(1)}, u32[]{:S(2)}, u32[]{:S(2)}) %collective-permute-start.26) | collective-permute-done | bytes 49184 | tf_op jit(solution)/shard_map/ppermute | solution.py:488
  71.6 2.2 %collective-permute-start.32 = (bf16[128,128]{1,0:T(8,128)(2,1)S(1)}, bf16[128,128]{1,0:T(8,128)(2,1)S(1)}, u32[]{:S(2)}, u32[]{:S(2)}) collective-permute-start(bf16[128,128]{1,0:T(8,128)(2,1)S(1)} %get-tuple-element.112), channel_id=1, source_target_pairs={{0,24},{8,16},{16,8},{24,0},{1,25},{9,17},{17,9},{25,1},{2,26},{10... | collective-permute-start | bytes 98312 | tf_op jit(solution)/shard_map/ppermute | solution.py:485
  74.6 1.5 %collective-permute-start.34 = (bf16[128,128]{1,0:T(8,128)(2,1)S(1)}, bf16[128,128]{1,0:T(8,128)(2,1)S(1)}, u32[]{:S(2)}, u32[]{:S(2)}) collective-permute-start(bf16[128,128]{1,0:T(8,128)(2,1)S(1)} %get-tuple-element.114), channel_id=1, source_target_pairs={{0,8},{8,0},{16,24},{24,16},{1,9},{9,1},{17,25},{25,17},{2,10},{10... | collective-permute-start | bytes 98312 | tf_op jit(solution)/shard_map/ppermute | solution.py:485
  (78 shorter events, 32.0 us)
Async XLA Ops:
  2.4 9.1 %collective-permute-start.2 = (bf16[128,128]{1,0:T(8,128)(2,1)S(1)}, bf16[128,128]{1,0:T(8,128)(2,1)S(1)}, u32[]{:S(2)}, u32[]{:S(2)}) collective-permute-start(bf16[128,128]{1,0:T(8,128)(2,1)S(1)} %get-tuple-element.65.refs_1_), channel_id=1, source_target_pairs={{0,24},{8,16},{16,8},{24,0},{1,25},{9,17},{17,9},{25,1},{2,26},{10... | collective-permute-start | bytes 98312 | tf_op jit(solution)/shard_map/ppermute | solution.py:485
  7.5 4.8 %collective-permute-start.1 = (bf16[128,128]{1,0:T(8,128)(2,1)S(1)}, bf16[128,128]{1,0:T(8,128)(2,1)S(1)}, u32[]{:S(2)}, u32[]{:S(2)}) collective-permute-start(bf16[128,128]{1,0:T(8,128)(2,1)S(1)} %get-tuple-element.65.refs_1_), channel_id=1, source_target_pairs={{0,16},{8,24},{16,0},{24,8},{1,17},{9,25},{17,1},{25,9},{2,18},{10... | collective-permute-start | bytes 98312 | tf_op jit(solution)/shard_map/ppermute | solution.py:485
  7.5 4.8 %collective-permute-start = (bf16[128,128]{1,0:T(8,128)(2,1)S(1)}, bf16[128,128]{1,0:T(8,128)(2,1)S(1)}, u32[]{:S(2)}, u32[]{:S(2)}) collective-permute-start(bf16[128,128]{1,0:T(8,128)(2,1)S(1)} %get-tuple-element.65.refs_1_), channel_id=1, source_target_pairs={{0,8},{8,0},{16,24},{24,16},{1,9},{9,1},{17,25},{25,17},{2,10},{10... | collective-permute-start | bytes 98312 | tf_op jit(solution)/shard_map/ppermute | solution.py:485
  13.0 6.7 %collective-permute-start.10 = (bf16[1,464,128]{2,1,0:T(8,128)(2,1)S(1)}, bf16[1,464,128]{2,1,0:T(8,128)(2,1)S(1)}, u32[]{:S(2)}, u32[]{:S(2)}) collective-permute-start(bf16[1,464,128]{2,1,0:T(8,128)(2,1)S(1)} %get-tuple-element.81.refs_0_), channel_id=1, source_target_pairs={{0,2},{1,3},{2,0},{3,1},{4,6},{5,7},{6,4},{7,5},{8,10},{9,11},{10,... | collective-permute-start | bytes 356360 | tf_op jit(solution)/shard_map/ppermute | solution.py:488
  14.5 7.1 %collective-permute-start.11 = (bf16[1,464,128]{2,1,0:T(8,128)(2,1)S(1)}, bf16[1,464,128]{2,1,0:T(8,128)(2,1)S(1)}, u32[]{:S(2)}, u32[]{:S(2)}) collective-permute-start(bf16[1,464,128]{2,1,0:T(8,128)(2,1)S(1)} %get-tuple-element.83.refs_0_), channel_id=1, source_target_pairs={{0,4},{1,5},{2,6},{3,7},{4,0},{5,1},{6,2},{7,3},{8,12},{9,13},{10,... | collective-permute-start | bytes 356360 | tf_op jit(solution)/shard_map/ppermute | solution.py:488
  16.1 6.4 %collective-permute-start.4 = (bf16[22,16,128]{2,1,0:T(8,128)(2,1)S(1)}, bf16[22,16,128]{2,1,0:T(8,128)(2,1)S(1)}, u32[]{:S(2)}, u32[]{:S(2)}) collective-permute-start(bf16[22,16,128]{2,1,0:T(8,128)(2,1)S(1)} %get-tuple-element.72), channel_id=1, source_target_pairs={{0,6},{1,7},{2,4},{3,5},{4,2},{5,3},{6,0},{7,1},{8,14},{9,15},{10,... | collective-permute-start | bytes 270344 | tf_op jit(solution)/shard_map/ppermute | solution.py:488
  17.0 6.7 %collective-permute-start.5 = (bf16[22,16,128]{2,1,0:T(8,128)(2,1)S(1)}, bf16[22,16,128]{2,1,0:T(8,128)(2,1)S(1)}, u32[]{:S(2)}, u32[]{:S(2)}) collective-permute-start(bf16[22,16,128]{2,1,0:T(8,128)(2,1)S(1)} %get-tuple-element.73), channel_id=1, source_target_pairs={{0,4},{1,5},{2,6},{3,7},{4,0},{5,1},{6,2},{7,3},{8,12},{9,13},{10,... | collective-permute-start | bytes 270344 | tf_op jit(solution)/shard_map/ppermute | solution.py:488
  18.1 5.5 %collective-permute-start.6 = (bf16[22,16,128]{2,1,0:T(8,128)(2,1)S(1)}, bf16[22,16,128]{2,1,0:T(8,128)(2,1)S(1)}, u32[]{:S(2)}, u32[]{:S(2)}) collective-permute-start(bf16[22,16,128]{2,1,0:T(8,128)(2,1)S(1)} %get-tuple-element.74), channel_id=1, source_target_pairs={{0,2},{1,3},{2,0},{3,1},{4,6},{5,7},{6,4},{7,5},{8,10},{9,11},{10,... | collective-permute-start | bytes 270344 | tf_op jit(solution)/shard_map/ppermute | solution.py:488
  23.7 10.3 %collective-permute-start.13 = (bf16[2,464,128]{2,1,0:T(8,128)(2,1)S(1)}, bf16[2,464,128]{2,1,0:T(8,128)(2,1)S(1)}, u32[]{:S(2)}, u32[]{:S(2)}) collective-permute-start(bf16[2,464,128]{2,1,0:T(8,128)(2,1)S(1)} %shard_map.61.refs_0_), channel_id=1, source_target_pairs={{0,2},{1,3},{2,0},{3,1},{4,6},{5,7},{6,4},{7,5},{8,10},{9,11},{10,... | collective-permute-start | bytes 712712 | tf_op jit(solution)/shard_map/ppermute | solution.py:488
  24.3 9.6 %collective-permute-start.12 = (bf16[2,464,128]{2,1,0:T(8,128)(2,1)S(1)}, bf16[2,464,128]{2,1,0:T(8,128)(2,1)S(1)}, u32[]{:S(2)}, u32[]{:S(2)}) collective-permute-start(bf16[2,464,128]{2,1,0:T(8,128)(2,1)S(1)} %shard_map.60.refs_0_), channel_id=1, source_target_pairs={{0,4},{1,5},{2,6},{3,7},{4,0},{5,1},{6,2},{7,3},{8,12},{9,13},{10,... | collective-permute-start | bytes 712712 | tf_op jit(solution)/shard_map/ppermute | solution.py:488
  26.2 5.8 %collective-permute-start.9 = (bf16[8,16,128]{2,1,0:T(8,128)(2,1)S(1)}, bf16[8,16,128]{2,1,0:T(8,128)(2,1)S(1)}, u32[]{:S(2)}, u32[]{:S(2)}) collective-permute-start(bf16[8,16,128]{2,1,0:T(8,128)(2,1)S(1)} %get-tuple-element.87.refs_6_), channel_id=1, source_target_pairs={{0,24},{8,16},{16,8},{24,0},{1,25},{9,17},{17,9},{25,1},{2,26},{10... | collective-permute-start | bytes 98312 | tf_op jit(solution)/shard_map/ppermute | solution.py:485
  29.2 4.8 %collective-permute-start.8 = (bf16[8,16,128]{2,1,0:T(8,128)(2,1)S(1)}, bf16[8,16,128]{2,1,0:T(8,128)(2,1)S(1)}, u32[]{:S(2)}, u32[]{:S(2)}) collective-permute-start(bf16[8,16,128]{2,1,0:T(8,128)(2,1)S(1)} %get-tuple-element.87.refs_6_), channel_id=1, source_target_pairs={{0,16},{8,24},{16,0},{24,8},{1,17},{9,25},{17,1},{25,9},{2,18},{10... | collective-permute-start | bytes 98312 | tf_op jit(solution)/shard_map/ppermute | solution.py:485
  29.2 4.8 %collective-permute-start.7 = (bf16[8,16,128]{2,1,0:T(8,128)(2,1)S(1)}, bf16[8,16,128]{2,1,0:T(8,128)(2,1)S(1)}, u32[]{:S(2)}, u32[]{:S(2)}) collective-permute-start(bf16[8,16,128]{2,1,0:T(8,128)(2,1)S(1)} %get-tuple-element.87.refs_6_), channel_id=1, source_target_pairs={{0,8},{8,0},{16,24},{24,16},{1,9},{9,1},{17,25},{25,17},{2,10},{10... | collective-permute-start | bytes 98312 | tf_op jit(solution)/shard_map/ppermute | solution.py:485
  34.1 7.9 %collective-permute-start.15 = (bf16[4,464,128]{2,1,0:T(8,128)(2,1)S(1)}, bf16[4,464,128]{2,1,0:T(8,128)(2,1)S(1)}, u32[]{:S(2)}, u32[]{:S(2)}) collective-permute-start(bf16[4,464,128]{2,1,0:T(8,128)(2,1)S(1)} %shard_map.64.refs_4_), channel_id=1, source_target_pairs={{0,1},{1,0},{2,3},{3,2},{4,5},{5,4},{6,7},{7,6},{8,9},{9,8},{10,11... | collective-permute-start | bytes 1425416 | tf_op jit(solution)/shard_map/ppermute | solution.py:488
  37.5 6.2 %collective-permute-start.18 = (bf16[8,16,128]{2,1,0:T(8,128)(2,1)S(1)}, bf16[8,16,128]{2,1,0:T(8,128)(2,1)S(1)}, u32[]{:S(2)}, u32[]{:S(2)}) collective-permute-start(bf16[8,16,128]{2,1,0:T(8,128)(2,1)S(1)} %get-tuple-element.94.refs_6_), channel_id=1, source_target_pairs={{0,24},{8,16},{16,8},{24,0},{1,25},{9,17},{17,9},{25,1},{2,26},{10... | collective-permute-start | bytes 98312 | tf_op jit(solution)/shard_map/ppermute | solution.py:485
  39.4 4.9 %collective-permute-start.17 = (bf16[8,16,128]{2,1,0:T(8,128)(2,1)S(1)}, bf16[8,16,128]{2,1,0:T(8,128)(2,1)S(1)}, u32[]{:S(2)}, u32[]{:S(2)}) collective-permute-start(bf16[8,16,128]{2,1,0:T(8,128)(2,1)S(1)} %get-tuple-element.94.refs_6_), channel_id=1, source_target_pairs={{0,16},{8,24},{16,0},{24,8},{1,17},{9,25},{17,1},{25,9},{2,18},{10... | collective-permute-start | bytes 98312 | tf_op jit(solution)/shard_map/ppermute | solution.py:485
  39.7 4.6 %collective-permute-start.16 = (bf16[8,16,128]{2,1,0:T(8,128)(2,1)S(1)}, bf16[8,16,128]{2,1,0:T(8,128)(2,1)S(1)}, u32[]{:S(2)}, u32[]{:S(2)}) collective-permute-start(bf16[8,16,128]{2,1,0:T(8,128)(2,1)S(1)} %get-tuple-element.94.refs_6_), channel_id=1, source_target_pairs={{0,8},{8,0},{16,24},{24,16},{1,9},{9,1},{17,25},{25,17},{2,10},{10... | collective-permute-start | bytes 98312 | tf_op jit(solution)/shard_map/ppermute | solution.py:485
  46.9 5.8 %collective-permute-start.19 = (bf16[8,16,128]{2,1,0:T(8,128)(2,1)S(1)}, bf16[8,16,128]{2,1,0:T(8,128)(2,1)S(1)}, u32[]{:S(2)}, u32[]{:S(2)}) collective-permute-start(bf16[8,16,128]{2,1,0:T(8,128)(2,1)S(1)} %get-tuple-element.96), channel_id=1, source_target_pairs={{0,24},{8,16},{16,8},{24,0},{1,25},{9,17},{17,9},{25,1},{2,26},{10... | collective-permute-start | bytes 98312 | tf_op jit(solution)/shard_map/ppermute | solution.py:485
  49.3 4.9 %collective-permute-start.20 = (bf16[8,16,128]{2,1,0:T(8,128)(2,1)S(1)}, bf16[8,16,128]{2,1,0:T(8,128)(2,1)S(1)}, u32[]{:S(2)}, u32[]{:S(2)}) collective-permute-start(bf16[8,16,128]{2,1,0:T(8,128)(2,1)S(1)} %get-tuple-element.97), channel_id=1, source_target_pairs={{0,16},{8,24},{16,0},{24,8},{1,17},{9,25},{17,1},{25,9},{2,18},{10... | collective-permute-start | bytes 98312 | tf_op jit(solution)/shard_map/ppermute | solution.py:485
  55.8 5.8 %collective-permute-start.22 = (bf16[8,16,128]{2,1,0:T(8,128)(2,1)S(1)}, bf16[8,16,128]{2,1,0:T(8,128)(2,1)S(1)}, u32[]{:S(2)}, u32[]{:S(2)}) collective-permute-start(bf16[8,16,128]{2,1,0:T(8,128)(2,1)S(1)} %get-tuple-element.101), channel_id=1, source_target_pairs={{0,24},{8,16},{16,8},{24,0},{1,25},{9,17},{17,9},{25,1},{2,26},{10... | collective-permute-start | bytes 98312 | tf_op jit(solution)/shard_map/ppermute | solution.py:485
  57.5 5.2 %collective-permute-start.23 = (bf16[8,16,128]{2,1,0:T(8,128)(2,1)S(1)}, bf16[8,16,128]{2,1,0:T(8,128)(2,1)S(1)}, u32[]{:S(2)}, u32[]{:S(2)}) collective-permute-start(bf16[8,16,128]{2,1,0:T(8,128)(2,1)S(1)} %get-tuple-element.102), channel_id=1, source_target_pairs={{0,16},{8,24},{16,0},{24,8},{1,17},{9,25},{17,1},{25,9},{2,18},{10... | collective-permute-start | bytes 98312 | tf_op jit(solution)/shard_map/ppermute | solution.py:485
  65.0 5.0 %collective-permute-start.27 = (bf16[12,16,128]{2,1,0:T(8,128)(2,1)S(1)}, bf16[12,16,128]{2,1,0:T(8,128)(2,1)S(1)}, u32[]{:S(2)}, u32[]{:S(2)}) collective-permute-start(bf16[12,16,128]{2,1,0:T(8,128)(2,1)S(1)} %get-tuple-element.110), channel_id=1, source_target_pairs={{0,6},{1,7},{2,4},{3,5},{4,2},{5,3},{6,0},{7,1},{8,14},{9,15},{10,... | collective-permute-start | bytes 147464 | tf_op jit(solution)/shard_map/ppermute | solution.py:488
  71.6 5.9 %collective-permute-start.32 = (bf16[128,128]{1,0:T(8,128)(2,1)S(1)}, bf16[128,128]{1,0:T(8,128)(2,1)S(1)}, u32[]{:S(2)}, u32[]{:S(2)}) collective-permute-start(bf16[128,128]{1,0:T(8,128)(2,1)S(1)} %get-tuple-element.112), channel_id=1, source_target_pairs={{0,24},{8,16},{16,8},{24,0},{1,25},{9,17},{17,9},{25,1},{2,26},{10... | collective-permute-start | bytes 98312 | tf_op jit(solution)/shard_map/ppermute | solution.py:485
  73.8 4.9 %collective-permute-start.33 = (bf16[128,128]{1,0:T(8,128)(2,1)S(1)}, bf16[128,128]{1,0:T(8,128)(2,1)S(1)}, u32[]{:S(2)}, u32[]{:S(2)}) collective-permute-start(bf16[128,128]{1,0:T(8,128)(2,1)S(1)} %get-tuple-element.113), channel_id=1, source_target_pairs={{0,16},{8,24},{16,0},{24,8},{1,17},{9,25},{17,1},{25,9},{2,18},{10... | collective-permute-start | bytes 98312 | tf_op jit(solution)/shard_map/ppermute | solution.py:485
  (18 other events, 63.0 us)

commit v5 on v4

--- a/solution.py
+++ b/solution.py
@@ -121,17 +121,9 @@
     return jnp.where(low_lanes(first.shape, half), first, second)
 
 
-def first_kernel(plan, place, sides, inverse, solved, message, sides_here, inverse_here, sems):
-    copies = [
-        pltpu.make_async_copy(sides.at[0], sides_here, sems.at[0]),
-        pltpu.make_async_copy(inverse.at[0], inverse_here, sems.at[1]),
-    ]
-    for copy in copies:
-        copy.start()
-    for copy in copies:
-        copy.wait()
+def first_kernel(plan, place, sides, inverse, solved, message):
     parts = [
-        lax.dot_general(sides_here[b], inverse_here[:, b * plan.block : (b + 1) * plan.block], TN,
+        lax.dot_general(sides[0, b], inverse[0, :, b * plan.block : (b + 1) * plan.block], TN,
                         precision=lax.Precision.HIGHEST, preferred_element_type=F32)
         for b in range(plan.rows_dev)
     ]
@@ -144,43 +136,33 @@
     tiles, sides, inverse = take(refs, 3)
     dense, side_slices, inverse_one = take(refs, 3)
     payloads = take(refs, plan.levels - 1)
-    tiles_here, sides_here, inverse_here, sems = refs
-    copies = [
-        pltpu.make_async_copy(tiles, tiles_here, sems.at[0]),
-        pltpu.make_async_copy(sides, sides_here, sems.at[1]),
-        pltpu.make_async_copy(inverse, inverse_here, sems.at[2]),
-    ]
-    for copy in copies:
-        copy.start()
-    for copy in copies:
-        copy.wait()
     half = plan.block
     lane = lax.broadcasted_iota(jnp.int32, (16, 128), 1)
     for coupling in range(plan.levels):
         if coupling == 0:
             dense[...] = jnp.zeros_like(dense)
             for t in range(plan.tiles):
-                tile = tiles_here[0, t]
-                col = cols[0, t, 0]
+                tile = tiles[0, t]
+                col = cols[0, 0, t]
                 both = jnp.concatenate([tile, tile], axis=1).astype(F32)
                 here = (lax.broadcasted_iota(jnp.int32, both.shape, 1) // half) == col % 2
-                at = pl.ds(pl.multiple_of(rows[0, t, 0] * half, half), half)
+                at = pl.ds(pl.multiple_of(rows[0, 0, t] * half, half), half)
                 dense[col // 2, at, :] += jnp.where(here, both, 0.0).astype(BF16)
             continue
         target = payloads[coupling - 1].at[0]
         for k in range(plan.tiles // 2):
-            pair = jnp.concatenate([tiles_here[coupling, 2 * k], tiles_here[coupling, 2 * k + 1]], axis=1)
+            pair = jnp.concatenate([tiles[coupling, 2 * k], tiles[coupling, 2 * k + 1]], axis=1)
             target[k * half : (k + 1) * half, :] = pair
         index = jnp.zeros((16, 128), F32)
         for t in range(plan.tiles):
-            index = jnp.where(lane == t, rows[coupling, t, 0].astype(F32), index)
-            index = jnp.where(lane == t + 64, cols[coupling, t, 0].astype(F32), index)
+            index = jnp.where(lane == t, rows[coupling, 0, t].astype(F32), index)
+            index = jnp.where(lane == t + 64, cols[coupling, 0, t].astype(F32), index)
         target[plan.tile_rows : plan.inverse_at, :] = index.astype(BF16)
-    inverse_one[...] = inverse_here[1].astype(BF16).reshape(inverse_one.shape)
+    inverse_one[...] = inverse[1].astype(BF16).reshape(inverse_one.shape)
     for level in range(1, plan.levels + 1):
         if level > 1:
-            payloads[level - 2][0, plan.inverse_at :, :] = inverse_here[level].astype(BF16)
-        both = jnp.concatenate([sides_here[level, b] for b in range(plan.rows_dev)], axis=0).T
+            payloads[level - 2][0, plan.inverse_at :, :] = inverse[level].astype(BF16)
+        both = jnp.concatenate([sides[level, b] for b in range(plan.rows_dev)], axis=0).T
         pad_slices(plan, both, side_slices.at[level - 1])
 
 
@@ -345,114 +327,131 @@
     level_forward(plan, place, 1, sums, [None] * plan.n_col, coupled, write)
 
 
-def decode(plan, place, pieces, index):
-    lane = lax.broadcasted_iota(jnp.int32, (1, 128), 1)
-    for p, offset in enumerate(plan.sources()):
-        raw = pieces[p][plan.tile_rows : plan.inverse_at, :].astype(F32).astype(jnp.int32)[0:1]
-        owner = raw // plan.rows_dev * plan.n_col + (place[1] ^ offset)
-        col = owner * plan.rows_dev + raw % plan.rows_dev
-        index[p : p + 1, :] = jnp.where(lane < 64, raw, col)
-
-
-def multiply_forward(plan, place, pieces, received, index, left, right, total, ready):
+def decode(plan, place, core, pieces):
+    def reader(row, col):
+        return lambda tile: (row[0, tile], col[0, tile + 64])
+
+    readers = []
+    for chip, piece in enumerate(pieces):
+        raw = piece[plan.tile_rows : plan.inverse_at, :].astype(F32).astype(jnp.int32)[0:1]
+        owner = raw // plan.rows_dev * plan.n_col + (place[1] ^ (2 * chip + core))
+        readers.append(reader(raw, owner * plan.rows_dev + raw % plan.rows_dev))
+    return readers
+
+
+def multiply_forward(plan, place, core, pieces, left, right, totals):
     half, width = plan.block, plan.slice
-    for m in range(plan.n_row):
-        for u in range(plan.n_col):
-            store_halves(left, right, (place[0] ^ m) * plan.n_col + u, received[m][u].astype(F32), half)
-    total[...] = jnp.zeros_like(total)
-    ready()
-    for p in range(plan.n_col):
-        for k in range(plan.tiles // 2):
-            pair = pieces[p][k * half : (k + 1) * half, :]
-            vectors = jnp.concatenate([left[index[p, 2 * k + 64]], right[index[p, 2 * k + 65]]], axis=0)
-            product = lax.dot_general(vectors, pair, NT, preferred_element_type=F32)
-            total[index[p, 2 * k]] += product[:width]
-            total[index[p, 2 * k + 1]] += product[width:]
-
-
-def multiply_backward(plan, place, pieces, index, upper, left, right, out):
+    for piece, at in zip(pieces, decode(plan, place, core, pieces)):
+        for k in range(plan.tiles // 4):
+            matrix = piece[2 * k * half : (2 * k + 2) * half, :]
+            tiles = [at(4 * k + n) for n in range(4)]
+            vectors = [(right if n % 2 else left)[col] for n, (row, col) in enumerate(tiles)]
+            product = lax.dot_general(jnp.concatenate(vectors, axis=0), matrix, NT, preferred_element_type=F32)
+            for n, total in enumerate(totals):
+                total[tiles[n][0]] += product[n * width : (n + 1) * width]
+
+
+def multiply_backward(plan, place, core, pieces, upper_left, upper_right, left, right):
     half, width = plan.block, plan.slice
-    for p in range(plan.n_col):
-        for k in range(plan.tiles // 2):
-            pair = pieces[p][k * half : (k + 1) * half, :]
-            vectors = jnp.concatenate([upper[index[p, 2 * k]], upper[index[p, 2 * k + 1]]], axis=0)
-            product = jnp.dot(vectors, pair, preferred_element_type=F32)
-            left[index[p, 2 * k + 64]] += product[:width]
-            right[index[p, 2 * k + 65]] += product[width:]
+    for piece, at in zip(pieces, decode(plan, place, core, pieces)):
+        for k in range(plan.tiles // 4):
+            matrix = piece[2 * k * half : (2 * k + 2) * half, :]
+            tiles = [at(4 * k + n) for n in range(4)]
+            vectors = [(upper_right if n > 1 else upper_left)[row] for n, (row, col) in enumerate(tiles)]
+            product = jnp.dot(jnp.concatenate(vectors, axis=0), matrix, preferred_element_type=F32)
+            for n, (row, col) in enumerate(tiles):
+                (right if n % 2 else left)[col] += product[n * width : (n + 1) * width]
+
+
+def put_shares(plan, place, left, right, out):
     for m in range(plan.n_row):
         for u in range(plan.n_col):
             at = (place[0] ^ m) * plan.n_col + u
-            out[m][u] = join_halves(left, right, at, half).astype(out[m].dtype)
-
-
-def put_upper(plan, upper, u, value):
-    upper[2 * u] = value[:, : plan.block].astype(BF16)
-    upper[2 * u + 1] = value[:, plan.block :].astype(BF16)
-
-
-def forward_kernel(coupling, plan, place, *refs):
+            out[m][u] = join_halves(left, right, at, plan.block).astype(out[m].dtype)
+
+
+def clear(refs):
+    for ref in refs:
+        ref[...] = jnp.zeros_like(ref)
+
+
+def forward_near_kernel(coupling, plan, place, *refs):
+    refs = list(refs)
+    pieces, received = views(plan, coupling, take(refs, 1)), take(refs, plan.n_row)
+    left, right = take(refs, 2)
+    totals = refs
+    for m in range(plan.n_row):
+        for u in range(plan.n_col):
+            at = (place[0] ^ m) * plan.n_col + u
+            store_halves(left, right, at, received[m][u].astype(F32), plan.block)
+    clear(totals)
+    multiply_forward(plan, place, 0, pieces, left, right, totals)
+
+
+def forward_far_kernel(coupling, plan, place, *refs):
     refs = list(refs)
     last = coupling == plan.levels - 1
-    sums, pieces = chip_order(take(refs, plan.chips)), views(plan, coupling, take(refs, 2))
-    received = take(refs, plan.n_row)
-    keep = refs.pop(0)
+    sums, stacks = chip_order(take(refs, plan.chips)), take(refs, 2)
+    left, right = take(refs, 2)
+    near_totals, keep = take(refs, 4), refs.pop(0)
+    out = take(refs, plan.n_row if last else 1)
+    totals = take(refs, 4)
+    pieces = views(plan, coupling, stacks)
+    near, far = pieces[: plan.chips], pieces[plan.chips :]
+    clear(totals)
+    multiply_forward(plan, place, 1, far, left, right, totals)
+
     if last:
-        out = take(refs, plan.n_row)
-    else:
-        message, index_out = take(refs, 2)
-    left, right, total, index, sem = take(refs, 5)
-    if last:
-        index_out, upper, back_left, back_right = refs
-    decode(plan, place, pieces, index_out)
-    copy = pltpu.make_async_copy(index_out, index, sem)
-    copy.start()
-    multiply_forward(plan, place, pieces, received, index, left, right, total, copy.wait)
+        upper_left, upper_right, back_left, back_right = refs
+
+    def add(refs, at):
+        return sum((ref[at] for ref in refs[1:]), refs[0][at])
 
     def coupled(u):
-        return jnp.concatenate([total[2 * u], total[2 * u + 1]], axis=1)
-
-    if not last:
-
-        def write(made):
-            for _, u, value in made:
-                keep[u] = value
-                message[u] = value.astype(BF16)
-
-        level_forward(plan, place, coupling + 1, sums, pieces, coupled, write)
-        return
-    back_left[...] = jnp.zeros_like(back_left)
-    back_right[...] = jnp.zeros_like(back_right)
+        all_totals = near_totals + totals
+        low, high = all_totals[0:2] + all_totals[4:6], all_totals[2:4] + all_totals[6:8]
+        first = add(low, 2 * u) + pltpu.roll(add(high, 2 * u), plan.block, 1)
+        second = add(high, 2 * u + 1) + pltpu.roll(add(low, 2 * u + 1), plan.block, 1)
+        return jnp.where(low_lanes(first.shape, plan.block), first, second)
+
+    def write(made):
+        for _, u, value in made:
+            keep[u] = value
+            out[0][u] = value.astype(BF16)
 
     def write_top(made):
         made = [(u, apply_pair_transposed(inverse, value, plan.block)) for inverse, u, value in made]
         for u, value in made:
             keep[u] = value.astype(BF16)
-            put_upper(plan, upper, u, value)
-
-    level_forward(plan, place, plan.levels, sums, pieces, coupled, write_top)
-    multiply_backward(plan, place, pieces, index, upper, back_left, back_right, out)
-
-
-def backward_kernel(level, plan, place, index_here, *refs):
+            store_halves(upper_left, upper_right, u, value, plan.block)
+
+    level_forward(plan, place, coupling + 1, sums, pieces, coupled, write_top if last else write)
+    if last:
+        clear([back_left, back_right])
+        multiply_backward(plan, place, 0, near, upper_left, upper_right, back_left, back_right)
+        multiply_backward(plan, place, 1, far, upper_left, upper_right, back_left, back_right)
+        put_shares(plan, place, back_left, back_right, out)
+
+
+def backward_kernel(level, plan, place, *refs):
     refs = list(refs)
     sums, pieces = chip_order(take(refs, plan.chips)), views(plan, level - 1, take(refs, 2))
     shares = take(refs, plan.n_row)
     solved, keep = take(refs, 2)
     out = take(refs, plan.n_row)
-    upper, left, right, index, sem = refs
-    copy = pltpu.make_async_copy(index_here, index, sem)
-    copy.start()
-    left[...] = jnp.zeros_like(left)
-    right[...] = jnp.zeros_like(right)
+    upper_left, upper_right, left, right = refs
+    clear([left, right])
     back = add_up(shares)
 
     def write(u, value):
         keep[u] = value.astype(BF16)
-        put_upper(plan, upper, u, value)
+        store_halves(upper_left, upper_right, u, value, plan.block)
 
     level_backward(plan, place, level, sums, pieces, lambda u: solved[u] - back(u), write)
-    copy.wait()
-    multiply_backward(plan, place, pieces, index, upper, left, right, out)
+    for core in range(2):
+        here = pieces[core * plan.chips : (core + 1) * plan.chips]
+        multiply_backward(plan, place, core, here, upper_left, upper_right, left, right)
+    put_shares(plan, place, left, right, out)
 
 
 def leave_kernel(plan, place, *refs):
@@ -503,10 +502,9 @@
     slices = (n_col, plan.slice, plan.lanes)
     dma = pltpu.SemaphoreType.DMA
     x0, message = call(
-        plan, first_kernel, [array(column, F32), array(column)], (right_sides, diag_inverse),
-        [pltpu.VMEM(right_sides.shape[1:], F32), pltpu.VMEM(diag_inverse.shape[1:], F32), dma((2,))],
-        raw=(0, 1),
-    )
+        plan, first_kernel, [array(column, F32), array(column)], (right_sides[0:1], diag_inverse[0:1])
+    )
+    tile_row, tile_col = tile_row.transpose(0, 2, 1), tile_col.transpose(0, 2, 1)
     message, tile_row, tile_col = lax.optimization_barrier((message, tile_row, tile_col))
     received = gather_row(message)
     dense, side_slices, inverse_one, *held = call(
@@ -515,9 +513,7 @@
          array((plan.block // plan.slice, plan.slice, plan.lanes))]
         + [array((1, plan.payload_rows(), plan.lanes))] * (levels - 1),
         (tile_row, tile_col, factor_tiles, right_sides, diag_inverse),
-        [pltpu.VMEM(factor_tiles.shape, BF16), pltpu.VMEM(right_sides.shape, F32),
-         pltpu.VMEM(diag_inverse.shape, F32), dma((3,))],
-        scalars=2, raw=(2, 3, 4),
+        scalars=2,
     )
 
     def join(held, other):
@@ -550,21 +546,11 @@
     )
     solved = [None, solved]
 
-    index_shape = (max(8, n_col), 128)
-    forward = [
-        pltpu.VMEM((plan.blocks, plan.slice, plan.lanes), BF16),
-        pltpu.VMEM((plan.blocks, plan.slice, plan.lanes), BF16),
-        pltpu.VMEM((plan.own, plan.slice, plan.block), F32),
-        pltpu.SMEM(index_shape, jnp.int32),
-        dma(()),
-    ]
-    backward = [
-        pltpu.VMEM((plan.own, plan.slice, plan.block), BF16),
-        pltpu.VMEM((plan.blocks, plan.slice, plan.lanes), F32),
-        pltpu.VMEM((plan.blocks, plan.slice, plan.lanes), F32),
-    ]
+    halves = array((plan.blocks, plan.slice, plan.lanes))
+    total = array((plan.own, plan.slice, plan.lanes), F32)
+    totals = [pltpu.VMEM(total.shape, F32)] * 4
+    backward = [pltpu.VMEM(total.shape, BF16)] * 2 + [pltpu.VMEM(halves.shape, F32)] * 2
     partial = [array(slices, F32)] + [array(slices)] * (n_row - 1)
-    index = [None] * levels
     pieces = [None]
     for s in range(1, levels):
         received = gather_row(message)
@@ -574,25 +560,27 @@
             while held[0].shape[0] < chips:
                 held = [join(*step(value, n)) for n, value in enumerate(held, 1)]
         pieces.append([held[s - 1], over_col(held[s - 1], 1)])
-        args = chip_order(sums) + pieces[s] + received
-        if s < levels - 1:
-            value, message, index[s] = call(
-                plan, functools.partial(forward_kernel, s),
-                [array(slices, F32), array(slices), array(index_shape, jnp.int32)], args, forward,
-            )
-            solved.append(value)
-        else:
-            made = call(
-                plan, functools.partial(forward_kernel, s), [array(slices)] + partial, args,
-                forward + [pltpu.VMEM(index_shape, jnp.int32)] + backward,
-            )
+        near = call(
+            plan, functools.partial(forward_near_kernel, s), [halves] * 2 + [total] * 4,
+            pieces[s][:1] + received,
+        )
+        last = s == levels - 1
+        made = call(
+            plan, functools.partial(forward_far_kernel, s),
+            [array(slices, BF16 if last else F32)] + (partial if last else [array(slices)]),
+            chip_order(sums) + pieces[s] + list(near),
+            totals + (backward if last else []),
+        )
+        if not last:
+            solved.append(made[0])
+            message = made[1]
     results = [made[0]]
     shares = exchange_row(made[1:])
     for level in range(levels - 1, 1, -1):
         made = call(
             plan, functools.partial(backward_kernel, level), [array(slices)] + partial,
-            [index[level - 1]] + chip_order(sums) + pieces[level - 1] + shares + [solved[level]],
-            backward + [pltpu.SMEM(index_shape, jnp.int32), dma(())],
+            chip_order(sums) + pieces[level - 1] + shares + [solved[level]],
+            backward,
         )
         results.insert(0, made[0])
         shares = exchange_row(made[1:])

time: 80.1 us -> 77.9 us (0.973)
  Pallas kernels: 11.5 us -> 9.15 us
    pallas_call x16 -> x18, Pallas kernels: 11.5 us -> 9.15 us  [call(): pl.pallas_call(kernel, out_shape=outs, in_specs=specs, out_specs=[pl.Bloc...]
    slice x0 -> x2, local copies, waits for them, and re-layouts: none -> 1.64 us  [the longest x1 0.88 us: on_device(): right_sides[0:1]]
    unnamed x14 -> x10, local copies, waits for them, and re-layouts: 2.93 us -> 2.03 us
  transfers between devices with their start and end apart: 35 -> 35, of which waited for: 21 -> 20; matrix products, arithmetic and copies ran while one was open for 0% -> 0% of each run, Pallas kernels for 6% -> 5%
where the time goes in v5:
time: 77.9 us; the launch traced here: 77.6 us
  starting transfers between devices  41.1 us (53%)
  waiting for transfers between devices  23.5 us (30%)
  Pallas kernels  9.15 us (12%)
  local copies, waits for them, and re-layouts  3.67 us (5%)
    ppermute x18, starting transfers between devices, over_row(): return lax.ppermute(value, 'row', [(i, i ^ m) for i in range(n_row)])  28 us
    ppermute x18, waiting for transfers between devices, over_row(): return lax.ppermute(value, 'row', [(i, i ^ m) for i in range(n_row)])  14 us
    ppermute x17, starting transfers between devices, over_col(): return lax.ppermute(value, 'col', [(i, i ^ m) for i in range(n_col)])  13.1 us
    ppermute x17, waiting for transfers between devices, over_col(): return lax.ppermute(value, 'col', [(i, i ^ m) for i in range(n_col)])  9.5 us
    pallas_call x18, Pallas kernels, call(): pl.pallas_call(kernel, out_shape=outs, in_specs=specs, out_specs=[pl.Bloc...  9.15 us
    unnamed x10, local copies, waits for them, and re-layouts  2.03 us
  transfers between devices with their start and end apart: 35, of which 20 were waited for; matrix products, arithmetic and copies ran while one was open for 0% of the time, Pallas kernels for 5%

profile of v5, /device:TPU:0, one launch (start us, length us, event | category | flops | bytes accessed | tf_op | source)
XLA Modules:
  0.0 77.6 jit_solution(3800065786150815989)
XLA Ops:
  2.1 5.1 %collective-permute-start.2 = (bf16[128,128]{1,0:T(8,128)(2,1)S(1)}, bf16[128,128]{1,0:T(8,128)(2,1)S(1)}, u32[]{:S(2)}, u32[]{:S(2)}) collective-permute-start(bf16[128,128]{1,0:T(8,128)(2,1)S(1)} %get-tuple-element.76.refs_1_), channel_id=1, source_target_pairs={{0,24},{8,16},{16,8},{24,0},{1,25},{9,17},{17,9},{25,1},{2,26},{10... | collective-permute-start | bytes 98312 | tf_op jit(solution)/shard_map/ppermute | solution.py:484
  12.6 1.6 %collective-permute-start.10 = (bf16[1,464,128]{2,1,0:T(8,128)(2,1)S(1)}, bf16[1,464,128]{2,1,0:T(8,128)(2,1)S(1)}, u32[]{:S(2)}, u32[]{:S(2)}) collective-permute-start(bf16[1,464,128]{2,1,0:T(8,128)(2,1)S(1)} %get-tuple-element.92.refs_0_), channel_id=1, source_target_pairs={{0,2},{1,3},{2,0},{3,1},{4,6},{5,7},{6,4},{7,5},{8,10},{9,11},{10,... | collective-permute-start | bytes 356360 | tf_op jit(solution)/shard_map/ppermute | solution.py:487
  14.2 1.5 %collective-permute-start.11 = (bf16[1,464,128]{2,1,0:T(8,128)(2,1)S(1)}, bf16[1,464,128]{2,1,0:T(8,128)(2,1)S(1)}, u32[]{:S(2)}, u32[]{:S(2)}) collective-permute-start(bf16[1,464,128]{2,1,0:T(8,128)(2,1)S(1)} %get-tuple-element.94.refs_0_), channel_id=1, source_target_pairs={{0,4},{1,5},{2,6},{3,7},{4,0},{5,1},{6,2},{7,3},{8,12},{9,13},{10,... | collective-permute-start | bytes 356360 | tf_op jit(solution)/shard_map/ppermute | solution.py:487
  17.8 1.5 %collective-permute-start.6 = (bf16[22,16,128]{2,1,0:T(8,128)(2,1)S(1)}, bf16[22,16,128]{2,1,0:T(8,128)(2,1)S(1)}, u32[]{:S(2)}, u32[]{:S(2)}) collective-permute-start(bf16[22,16,128]{2,1,0:T(8,128)(2,1)S(1)} %get-tuple-element.85), channel_id=1, source_target_pairs={{0,2},{1,3},{2,0},{3,1},{4,6},{5,7},{6,4},{7,5},{8,10},{9,11},{10,... | collective-permute-start | bytes 270344 | tf_op jit(solution)/shard_map/ppermute | solution.py:487
  19.3 2.0 %collective-permute-done.11.refs_1_ = bf16[1,464,128]{2,1,0:T(8,128)(2,1)S(1)} collective-permute-done((bf16[1,464,128]{2,1,0:T(8,128)(2,1)S(1)}, bf16[1,464,128]{2,1,0:T(8,128)(2,1)S(1)}, u32[]{:S(2)}, u32[]{:S(2)}) %collective-permute-start.11) | collective-permute-done | bytes 118816 | tf_op jit(solution)/shard_map/ppermute | solution.py:487
  24.0 1.6 %collective-permute-start.12 = (bf16[2,464,128]{2,1,0:T(8,128)(2,1)S(1)}, bf16[2,464,128]{2,1,0:T(8,128)(2,1)S(1)}, u32[]{:S(2)}, u32[]{:S(2)}) collective-permute-start(bf16[2,464,128]{2,1,0:T(8,128)(2,1)S(1)} %shard_map.60.refs_0_), channel_id=1, source_target_pairs={{0,4},{1,5},{2,6},{3,7},{4,0},{5,1},{6,2},{7,3},{8,12},{9,13},{10,... | collective-permute-start | bytes 712712 | tf_op jit(solution)/shard_map/ppermute | solution.py:487
  25.8 2.6 %collective-permute-start.9 = (bf16[8,16,128]{2,1,0:T(8,128)(2,1)S(1)}, bf16[8,16,128]{2,1,0:T(8,128)(2,1)S(1)}, u32[]{:S(2)}, u32[]{:S(2)}) collective-permute-start(bf16[8,16,128]{2,1,0:T(8,128)(2,1)S(1)} %get-tuple-element.100.refs_1_), channel_id=1, source_target_pairs={{0,24},{8,16},{16,8},{24,0},{1,25},{9,17},{17,9},{25,1},{2,26},{10... | collective-permute-start | bytes 98312 | tf_op jit(solution)/shard_map/ppermute | solution.py:484
  28.4 1.9 %collective-permute-start.7 = (bf16[8,16,128]{2,1,0:T(8,128)(2,1)S(1)}, bf16[8,16,128]{2,1,0:T(8,128)(2,1)S(1)}, u32[]{:S(2)}, u32[]{:S(2)}) collective-permute-start(bf16[8,16,128]{2,1,0:T(8,128)(2,1)S(1)} %get-tuple-element.100.refs_1_), channel_id=1, source_target_pairs={{0,8},{8,0},{16,24},{24,16},{1,9},{9,1},{17,25},{25,17},{2,10},{10... | collective-permute-start | bytes 98312 | tf_op jit(solution)/shard_map/ppermute | solution.py:484
  31.6 1.6 %collective-permute-done.8.refs_3_ = bf16[8,16,128]{2,1,0:T(8,128)(2,1)S(1)} collective-permute-done((bf16[8,16,128]{2,1,0:T(8,128)(2,1)S(1)}, bf16[8,16,128]{2,1,0:T(8,128)(2,1)S(1)}, u32[]{:S(2)}, u32[]{:S(2)}) %collective-permute-start.8) | collective-permute-done | bytes 32800 | tf_op jit(solution)/shard_map/ppermute | solution.py:484
  35.9 1.9 %collective-permute-start.18 = (bf16[8,16,128]{2,1,0:T(8,128)(2,1)S(1)}, bf16[8,16,128]{2,1,0:T(8,128)(2,1)S(1)}, u32[]{:S(2)}, u32[]{:S(2)}) collective-permute-start(bf16[8,16,128]{2,1,0:T(8,128)(2,1)S(1)} %get-tuple-element.110.refs_1_), channel_id=1, source_target_pairs={{0,24},{8,16},{16,8},{24,0},{1,25},{9,17},{17,9},{25,1},{2,26},{10... | collective-permute-start | bytes 98312 | tf_op jit(solution)/shard_map/ppermute | solution.py:484
  38.4 2.0 %collective-permute-start.16 = (bf16[8,16,128]{2,1,0:T(8,128)(2,1)S(1)}, bf16[8,16,128]{2,1,0:T(8,128)(2,1)S(1)}, u32[]{:S(2)}, u32[]{:S(2)}) collective-permute-start(bf16[8,16,128]{2,1,0:T(8,128)(2,1)S(1)} %get-tuple-element.110.refs_1_), channel_id=1, source_target_pairs={{0,8},{8,0},{16,24},{24,16},{1,9},{9,1},{17,25},{25,17},{2,10},{10... | collective-permute-start | bytes 98312 | tf_op jit(solution)/shard_map/ppermute | solution.py:484
  40.4 1.8 %collective-permute-done.18.refs_4_ = bf16[8,16,128]{2,1,0:T(8,128)(2,1)S(1)} collective-permute-done((bf16[8,16,128]{2,1,0:T(8,128)(2,1)S(1)}, bf16[8,16,128]{2,1,0:T(8,128)(2,1)S(1)}, u32[]{:S(2)}, u32[]{:S(2)}) %collective-permute-start.18) | collective-permute-done | bytes 32800 | tf_op jit(solution)/shard_map/ppermute | solution.py:484
  43.4 1.7 %shard_map.67 = (bf16[8,16,128]{2,1,0:T(8,128)(2,1)S(1)}, f32[8,16,128]{2,1,0:T(8,128)S(1)}, bf16[8,16,128]{2,1,0:T(8,128)(2,1)S(1)}, bf16[8,16,128]{2,1,0:T(8,128)(2,1)S(1)}, bf16[8,16,128]{2,1,0:T(8,128)(2,1)S(1)}) custom-call(bf16[22,16,128]{2,1,0:T(8,128)(2,1)S(1)} %get-tuple-element.82.refs_1_.refs_0_, ...), custom_call_target="tpu_custom_call" | custom-call | tf_op jit(solution)/shard_map/pallas_call | solution.py:49
  45.1 2.4 %collective-permute-start.19 = (bf16[8,16,128]{2,1,0:T(8,128)(2,1)S(1)}, bf16[8,16,128]{2,1,0:T(8,128)(2,1)S(1)}, u32[]{:S(2)}, u32[]{:S(2)}) collective-permute-start(bf16[8,16,128]{2,1,0:T(8,128)(2,1)S(1)} %get-tuple-element.118), channel_id=1, source_target_pairs={{0,24},{8,16},{16,8},{24,0},{1,25},{9,17},{17,9},{25,1},{2,26},{10... | collective-permute-start | bytes 98312 | tf_op jit(solution)/shard_map/ppermute | solution.py:484
  48.1 1.5 %collective-permute-start.21 = (bf16[8,16,128]{2,1,0:T(8,128)(2,1)S(1)}, bf16[8,16,128]{2,1,0:T(8,128)(2,1)S(1)}, u32[]{:S(2)}, u32[]{:S(2)}) collective-permute-start(bf16[8,16,128]{2,1,0:T(8,128)(2,1)S(1)} %get-tuple-element.120), channel_id=1, source_target_pairs={{0,8},{8,0},{16,24},{24,16},{1,9},{9,1},{17,25},{25,17},{2,10},{10... | collective-permute-start | bytes 98312 | tf_op jit(solution)/shard_map/ppermute | solution.py:484
  50.9 1.5 %collective-permute-done.20.refs_8_ = bf16[8,16,128]{2,1,0:T(8,128)(2,1)S(1)} collective-permute-done((bf16[8,16,128]{2,1,0:T(8,128)(2,1)S(1)}, bf16[8,16,128]{2,1,0:T(8,128)(2,1)S(1)}, u32[]{:S(2)}, u32[]{:S(2)}) %collective-permute-start.20) | collective-permute-done | bytes 32800 | tf_op jit(solution)/shard_map/ppermute | solution.py:484
  53.4 1.9 %collective-permute-start.22 = (bf16[8,16,128]{2,1,0:T(8,128)(2,1)S(1)}, bf16[8,16,128]{2,1,0:T(8,128)(2,1)S(1)}, u32[]{:S(2)}, u32[]{:S(2)}) collective-permute-start(bf16[8,16,128]{2,1,0:T(8,128)(2,1)S(1)} %get-tuple-element.123), channel_id=1, source_target_pairs={{0,24},{8,16},{16,8},{24,0},{1,25},{9,17},{17,9},{25,1},{2,26},{10... | collective-permute-start | bytes 98312 | tf_op jit(solution)/shard_map/ppermute | solution.py:484
  56.0 1.9 %collective-permute-start.24 = (bf16[8,16,128]{2,1,0:T(8,128)(2,1)S(1)}, bf16[8,16,128]{2,1,0:T(8,128)(2,1)S(1)}, u32[]{:S(2)}, u32[]{:S(2)}) collective-permute-start(bf16[8,16,128]{2,1,0:T(8,128)(2,1)S(1)} %get-tuple-element.125), channel_id=1, source_target_pairs={{0,8},{8,0},{16,24},{24,16},{1,9},{9,1},{17,25},{25,17},{2,10},{10... | collective-permute-start | bytes 98312 | tf_op jit(solution)/shard_map/ppermute | solution.py:484
  60.7 1.6 %collective-permute-start.25 = (bf16[12,16,128]{2,1,0:T(8,128)(2,1)S(1)}, bf16[12,16,128]{2,1,0:T(8,128)(2,1)S(1)}, u32[]{:S(2)}, u32[]{:S(2)}) collective-permute-start(bf16[12,16,128]{2,1,0:T(8,128)(2,1)S(1)} %get-tuple-element.130), channel_id=1, source_target_pairs={{0,2},{1,3},{2,0},{3,1},{4,6},{5,7},{6,4},{7,5},{8,10},{9,11},{10,... | collective-permute-start | bytes 147464 | tf_op jit(solution)/shard_map/ppermute | solution.py:487
  62.8 1.5 %collective-permute-start.27 = (bf16[12,16,128]{2,1,0:T(8,128)(2,1)S(1)}, bf16[12,16,128]{2,1,0:T(8,128)(2,1)S(1)}, u32[]{:S(2)}, u32[]{:S(2)}) collective-permute-start(bf16[12,16,128]{2,1,0:T(8,128)(2,1)S(1)} %get-tuple-element.132), channel_id=1, source_target_pairs={{0,6},{1,7},{2,4},{3,5},{4,2},{5,3},{6,0},{7,1},{8,14},{9,15},{10,... | collective-permute-start | bytes 147464 | tf_op jit(solution)/shard_map/ppermute | solution.py:487
  64.9 1.5 %collective-permute-done.26.refs_3_.refs_2_ = bf16[12,16,128]{2,1,0:T(8,128)(2,1)S(1)} collective-permute-done((bf16[12,16,128]{2,1,0:T(8,128)(2,1)S(1)}, bf16[12,16,128]{2,1,0:T(8,128)(2,1)S(1)}, u32[]{:S(2)}, u32[]{:S(2)}) %collective-permute-start.26) | collective-permute-done | bytes 49184 | tf_op jit(solution)/shard_map/ppermute | solution.py:487
  66.4 1.4 %collective-permute-done.27.refs_4_.refs_3_ = bf16[12,16,128]{2,1,0:T(8,128)(2,1)S(1)} collective-permute-done((bf16[12,16,128]{2,1,0:T(8,128)(2,1)S(1)}, bf16[12,16,128]{2,1,0:T(8,128)(2,1)S(1)}, u32[]{:S(2)}, u32[]{:S(2)}) %collective-permute-start.27) | collective-permute-done | bytes 49184 | tf_op jit(solution)/shard_map/ppermute | solution.py:487
  69.4 2.1 %collective-permute-start.32 = (bf16[128,128]{1,0:T(8,128)(2,1)S(1)}, bf16[128,128]{1,0:T(8,128)(2,1)S(1)}, u32[]{:S(2)}, u32[]{:S(2)}) collective-permute-start(bf16[128,128]{1,0:T(8,128)(2,1)S(1)} %get-tuple-element.134), channel_id=1, source_target_pairs={{0,24},{8,16},{16,8},{24,0},{1,25},{9,17},{17,9},{25,1},{2,26},{10... | collective-permute-start | bytes 98312 | tf_op jit(solution)/shard_map/ppermute | solution.py:484
  72.3 1.6 %collective-permute-start.34 = (bf16[128,128]{1,0:T(8,128)(2,1)S(1)}, bf16[128,128]{1,0:T(8,128)(2,1)S(1)}, u32[]{:S(2)}, u32[]{:S(2)}) collective-permute-start(bf16[128,128]{1,0:T(8,128)(2,1)S(1)} %get-tuple-element.136), channel_id=1, source_target_pairs={{0,8},{8,0},{16,24},{24,16},{1,9},{9,1},{17,25},{25,17},{2,10},{10... | collective-permute-start | bytes 98312 | tf_op jit(solution)/shard_map/ppermute | solution.py:484
  (76 shorter events, 32.0 us)
Async XLA Ops:
  2.1 8.7 %collective-permute-start.2 = (bf16[128,128]{1,0:T(8,128)(2,1)S(1)}, bf16[128,128]{1,0:T(8,128)(2,1)S(1)}, u32[]{:S(2)}, u32[]{:S(2)}) collective-permute-start(bf16[128,128]{1,0:T(8,128)(2,1)S(1)} %get-tuple-element.76.refs_1_), channel_id=1, source_target_pairs={{0,24},{8,16},{16,8},{24,0},{1,25},{9,17},{17,9},{25,1},{2,26},{10... | collective-permute-start | bytes 98312 | tf_op jit(solution)/shard_map/ppermute | solution.py:484
  7.2 4.8 %collective-permute-start.1 = (bf16[128,128]{1,0:T(8,128)(2,1)S(1)}, bf16[128,128]{1,0:T(8,128)(2,1)S(1)}, u32[]{:S(2)}, u32[]{:S(2)}) collective-permute-start(bf16[128,128]{1,0:T(8,128)(2,1)S(1)} %get-tuple-element.76.refs_1_), channel_id=1, source_target_pairs={{0,16},{8,24},{16,0},{24,8},{1,17},{9,25},{17,1},{25,9},{2,18},{10... | collective-permute-start | bytes 98312 | tf_op jit(solution)/shard_map/ppermute | solution.py:484
  7.2 4.8 %collective-permute-start = (bf16[128,128]{1,0:T(8,128)(2,1)S(1)}, bf16[128,128]{1,0:T(8,128)(2,1)S(1)}, u32[]{:S(2)}, u32[]{:S(2)}) collective-permute-start(bf16[128,128]{1,0:T(8,128)(2,1)S(1)} %get-tuple-element.76.refs_1_), channel_id=1, source_target_pairs={{0,8},{8,0},{16,24},{24,16},{1,9},{9,1},{17,25},{25,17},{2,10},{10... | collective-permute-start | bytes 98312 | tf_op jit(solution)/shard_map/ppermute | solution.py:484
  12.6 6.7 %collective-permute-start.10 = (bf16[1,464,128]{2,1,0:T(8,128)(2,1)S(1)}, bf16[1,464,128]{2,1,0:T(8,128)(2,1)S(1)}, u32[]{:S(2)}, u32[]{:S(2)}) collective-permute-start(bf16[1,464,128]{2,1,0:T(8,128)(2,1)S(1)} %get-tuple-element.92.refs_0_), channel_id=1, source_target_pairs={{0,2},{1,3},{2,0},{3,1},{4,6},{5,7},{6,4},{7,5},{8,10},{9,11},{10,... | collective-permute-start | bytes 356360 | tf_op jit(solution)/shard_map/ppermute | solution.py:487
  14.2 7.1 %collective-permute-start.11 = (bf16[1,464,128]{2,1,0:T(8,128)(2,1)S(1)}, bf16[1,464,128]{2,1,0:T(8,128)(2,1)S(1)}, u32[]{:S(2)}, u32[]{:S(2)}) collective-permute-start(bf16[1,464,128]{2,1,0:T(8,128)(2,1)S(1)} %get-tuple-element.94.refs_0_), channel_id=1, source_target_pairs={{0,4},{1,5},{2,6},{3,7},{4,0},{5,1},{6,2},{7,3},{8,12},{9,13},{10,... | collective-permute-start | bytes 356360 | tf_op jit(solution)/shard_map/ppermute | solution.py:487
  15.7 6.4 %collective-permute-start.4 = (bf16[22,16,128]{2,1,0:T(8,128)(2,1)S(1)}, bf16[22,16,128]{2,1,0:T(8,128)(2,1)S(1)}, u32[]{:S(2)}, u32[]{:S(2)}) collective-permute-start(bf16[22,16,128]{2,1,0:T(8,128)(2,1)S(1)} %get-tuple-element.83), channel_id=1, source_target_pairs={{0,6},{1,7},{2,4},{3,5},{4,2},{5,3},{6,0},{7,1},{8,14},{9,15},{10,... | collective-permute-start | bytes 270344 | tf_op jit(solution)/shard_map/ppermute | solution.py:487
  16.7 6.7 %collective-permute-start.5 = (bf16[22,16,128]{2,1,0:T(8,128)(2,1)S(1)}, bf16[22,16,128]{2,1,0:T(8,128)(2,1)S(1)}, u32[]{:S(2)}, u32[]{:S(2)}) collective-permute-start(bf16[22,16,128]{2,1,0:T(8,128)(2,1)S(1)} %get-tuple-element.84), channel_id=1, source_target_pairs={{0,4},{1,5},{2,6},{3,7},{4,0},{5,1},{6,2},{7,3},{8,12},{9,13},{10,... | collective-permute-start | bytes 270344 | tf_op jit(solution)/shard_map/ppermute | solution.py:487
  17.8 5.5 %collective-permute-start.6 = (bf16[22,16,128]{2,1,0:T(8,128)(2,1)S(1)}, bf16[22,16,128]{2,1,0:T(8,128)(2,1)S(1)}, u32[]{:S(2)}, u32[]{:S(2)}) collective-permute-start(bf16[22,16,128]{2,1,0:T(8,128)(2,1)S(1)} %get-tuple-element.85), channel_id=1, source_target_pairs={{0,2},{1,3},{2,0},{3,1},{4,6},{5,7},{6,4},{7,5},{8,10},{9,11},{10,... | collective-permute-start | bytes 270344 | tf_op jit(solution)/shard_map/ppermute | solution.py:487
  23.4 9.8 %collective-permute-start.13 = (bf16[2,464,128]{2,1,0:T(8,128)(2,1)S(1)}, bf16[2,464,128]{2,1,0:T(8,128)(2,1)S(1)}, u32[]{:S(2)}, u32[]{:S(2)}) collective-permute-start(bf16[2,464,128]{2,1,0:T(8,128)(2,1)S(1)} %shard_map.61.refs_0_), channel_id=1, source_target_pairs={{0,2},{1,3},{2,0},{3,1},{4,6},{5,7},{6,4},{7,5},{8,10},{9,11},{10,... | collective-permute-start | bytes 712712 | tf_op jit(solution)/shard_map/ppermute | solution.py:487
  24.0 9.2 %collective-permute-start.12 = (bf16[2,464,128]{2,1,0:T(8,128)(2,1)S(1)}, bf16[2,464,128]{2,1,0:T(8,128)(2,1)S(1)}, u32[]{:S(2)}, u32[]{:S(2)}) collective-permute-start(bf16[2,464,128]{2,1,0:T(8,128)(2,1)S(1)} %shard_map.60.refs_0_), channel_id=1, source_target_pairs={{0,4},{1,5},{2,6},{3,7},{4,0},{5,1},{6,2},{7,3},{8,12},{9,13},{10,... | collective-permute-start | bytes 712712 | tf_op jit(solution)/shard_map/ppermute | solution.py:487
  25.8 5.8 %collective-permute-start.9 = (bf16[8,16,128]{2,1,0:T(8,128)(2,1)S(1)}, bf16[8,16,128]{2,1,0:T(8,128)(2,1)S(1)}, u32[]{:S(2)}, u32[]{:S(2)}) collective-permute-start(bf16[8,16,128]{2,1,0:T(8,128)(2,1)S(1)} %get-tuple-element.100.refs_1_), channel_id=1, source_target_pairs={{0,24},{8,16},{16,8},{24,0},{1,25},{9,17},{17,9},{25,1},{2,26},{10... | collective-permute-start | bytes 98312 | tf_op jit(solution)/shard_map/ppermute | solution.py:484
  28.4 4.8 %collective-permute-start.8 = (bf16[8,16,128]{2,1,0:T(8,128)(2,1)S(1)}, bf16[8,16,128]{2,1,0:T(8,128)(2,1)S(1)}, u32[]{:S(2)}, u32[]{:S(2)}) collective-permute-start(bf16[8,16,128]{2,1,0:T(8,128)(2,1)S(1)} %get-tuple-element.100.refs_1_), channel_id=1, source_target_pairs={{0,16},{8,24},{16,0},{24,8},{1,17},{9,25},{17,1},{25,9},{2,18},{10... | collective-permute-start | bytes 98312 | tf_op jit(solution)/shard_map/ppermute | solution.py:484
  28.4 4.8 %collective-permute-start.7 = (bf16[8,16,128]{2,1,0:T(8,128)(2,1)S(1)}, bf16[8,16,128]{2,1,0:T(8,128)(2,1)S(1)}, u32[]{:S(2)}, u32[]{:S(2)}) collective-permute-start(bf16[8,16,128]{2,1,0:T(8,128)(2,1)S(1)} %get-tuple-element.100.refs_1_), channel_id=1, source_target_pairs={{0,8},{8,0},{16,24},{24,16},{1,9},{9,1},{17,25},{25,17},{2,10},{10... | collective-permute-start | bytes 98312 | tf_op jit(solution)/shard_map/ppermute | solution.py:484
  33.4 10.0 %collective-permute-start.15 = (bf16[4,464,128]{2,1,0:T(8,128)(2,1)S(1)}, bf16[4,464,128]{2,1,0:T(8,128)(2,1)S(1)}, u32[]{:S(2)}, u32[]{:S(2)}) collective-permute-start(bf16[4,464,128]{2,1,0:T(8,128)(2,1)S(1)} %shard_map.63.refs_0_.refs_4_), channel_id=1, source_target_pairs={{0,1},{1,0},{2,3},{3,2},{4,5},{5,4},{6,7},{7,6},{8,9},{9,8},{10,11... | collective-permute-start | bytes 1425416 | tf_op jit(solution)/shard_map/ppermute | solution.py:487
  35.9 6.2 %collective-permute-start.18 = (bf16[8,16,128]{2,1,0:T(8,128)(2,1)S(1)}, bf16[8,16,128]{2,1,0:T(8,128)(2,1)S(1)}, u32[]{:S(2)}, u32[]{:S(2)}) collective-permute-start(bf16[8,16,128]{2,1,0:T(8,128)(2,1)S(1)} %get-tuple-element.110.refs_1_), channel_id=1, source_target_pairs={{0,24},{8,16},{16,8},{24,0},{1,25},{9,17},{17,9},{25,1},{2,26},{10... | collective-permute-start | bytes 98312 | tf_op jit(solution)/shard_map/ppermute | solution.py:484
  37.9 5.0 %collective-permute-start.17 = (bf16[8,16,128]{2,1,0:T(8,128)(2,1)S(1)}, bf16[8,16,128]{2,1,0:T(8,128)(2,1)S(1)}, u32[]{:S(2)}, u32[]{:S(2)}) collective-permute-start(bf16[8,16,128]{2,1,0:T(8,128)(2,1)S(1)} %get-tuple-element.110.refs_1_), channel_id=1, source_target_pairs={{0,16},{8,24},{16,0},{24,8},{1,17},{9,25},{17,1},{25,9},{2,18},{10... | collective-permute-start | bytes 98312 | tf_op jit(solution)/shard_map/ppermute | solution.py:484
  38.4 4.4 %collective-permute-start.16 = (bf16[8,16,128]{2,1,0:T(8,128)(2,1)S(1)}, bf16[8,16,128]{2,1,0:T(8,128)(2,1)S(1)}, u32[]{:S(2)}, u32[]{:S(2)}) collective-permute-start(bf16[8,16,128]{2,1,0:T(8,128)(2,1)S(1)} %get-tuple-element.110.refs_1_), channel_id=1, source_target_pairs={{0,8},{8,0},{16,24},{24,16},{1,9},{9,1},{17,25},{25,17},{2,10},{10... | collective-permute-start | bytes 98312 | tf_op jit(solution)/shard_map/ppermute | solution.py:484
  45.1 5.8 %collective-permute-start.19 = (bf16[8,16,128]{2,1,0:T(8,128)(2,1)S(1)}, bf16[8,16,128]{2,1,0:T(8,128)(2,1)S(1)}, u32[]{:S(2)}, u32[]{:S(2)}) collective-permute-start(bf16[8,16,128]{2,1,0:T(8,128)(2,1)S(1)} %get-tuple-element.118), channel_id=1, source_target_pairs={{0,24},{8,16},{16,8},{24,0},{1,25},{9,17},{17,9},{25,1},{2,26},{10... | collective-permute-start | bytes 98312 | tf_op jit(solution)/shard_map/ppermute | solution.py:484
  47.5 4.9 %collective-permute-start.20 = (bf16[8,16,128]{2,1,0:T(8,128)(2,1)S(1)}, bf16[8,16,128]{2,1,0:T(8,128)(2,1)S(1)}, u32[]{:S(2)}, u32[]{:S(2)}) collective-permute-start(bf16[8,16,128]{2,1,0:T(8,128)(2,1)S(1)} %get-tuple-element.119), channel_id=1, source_target_pairs={{0,16},{8,24},{16,0},{24,8},{1,17},{9,25},{17,1},{25,9},{2,18},{10... | collective-permute-start | bytes 98312 | tf_op jit(solution)/shard_map/ppermute | solution.py:484
  53.4 5.8 %collective-permute-start.22 = (bf16[8,16,128]{2,1,0:T(8,128)(2,1)S(1)}, bf16[8,16,128]{2,1,0:T(8,128)(2,1)S(1)}, u32[]{:S(2)}, u32[]{:S(2)}) collective-permute-start(bf16[8,16,128]{2,1,0:T(8,128)(2,1)S(1)} %get-tuple-element.123), channel_id=1, source_target_pairs={{0,24},{8,16},{16,8},{24,0},{1,25},{9,17},{17,9},{25,1},{2,26},{10... | collective-permute-start | bytes 98312 | tf_op jit(solution)/shard_map/ppermute | solution.py:484
  55.3 5.2 %collective-permute-start.23 = (bf16[8,16,128]{2,1,0:T(8,128)(2,1)S(1)}, bf16[8,16,128]{2,1,0:T(8,128)(2,1)S(1)}, u32[]{:S(2)}, u32[]{:S(2)}) collective-permute-start(bf16[8,16,128]{2,1,0:T(8,128)(2,1)S(1)} %get-tuple-element.124), channel_id=1, source_target_pairs={{0,16},{8,24},{16,0},{24,8},{1,17},{9,25},{17,1},{25,9},{2,18},{10... | collective-permute-start | bytes 98312 | tf_op jit(solution)/shard_map/ppermute | solution.py:484
  62.8 5.0 %collective-permute-start.27 = (bf16[12,16,128]{2,1,0:T(8,128)(2,1)S(1)}, bf16[12,16,128]{2,1,0:T(8,128)(2,1)S(1)}, u32[]{:S(2)}, u32[]{:S(2)}) collective-permute-start(bf16[12,16,128]{2,1,0:T(8,128)(2,1)S(1)} %get-tuple-element.132), channel_id=1, source_target_pairs={{0,6},{1,7},{2,4},{3,5},{4,2},{5,3},{6,0},{7,1},{8,14},{9,15},{10,... | collective-permute-start | bytes 147464 | tf_op jit(solution)/shard_map/ppermute | solution.py:487
  69.4 5.8 %collective-permute-start.32 = (bf16[128,128]{1,0:T(8,128)(2,1)S(1)}, bf16[128,128]{1,0:T(8,128)(2,1)S(1)}, u32[]{:S(2)}, u32[]{:S(2)}) collective-permute-start(bf16[128,128]{1,0:T(8,128)(2,1)S(1)} %get-tuple-element.134), channel_id=1, source_target_pairs={{0,24},{8,16},{16,8},{24,0},{1,25},{9,17},{17,9},{25,1},{2,26},{10... | collective-permute-start | bytes 98312 | tf_op jit(solution)/shard_map/ppermute | solution.py:484
  71.5 4.9 %collective-permute-start.33 = (bf16[128,128]{1,0:T(8,128)(2,1)S(1)}, bf16[128,128]{1,0:T(8,128)(2,1)S(1)}, u32[]{:S(2)}, u32[]{:S(2)}) collective-permute-start(bf16[128,128]{1,0:T(8,128)(2,1)S(1)} %get-tuple-element.135), channel_id=1, source_target_pairs={{0,16},{8,24},{16,0},{24,8},{1,17},{9,25},{17,1},{25,9},{2,18},{10... | collective-permute-start | bytes 98312 | tf_op jit(solution)/shard_map/ppermute | solution.py:484
  (16 other events, 56.0 us)

commit v6 on v5

--- a/solution.py
+++ b/solution.py
@@ -119,16 +119,6 @@
     first = left[2 * at] + pltpu.roll(right[2 * at], half, 1)
     second = right[2 * at + 1] + pltpu.roll(left[2 * at + 1], half, 1)
     return jnp.where(low_lanes(first.shape, half), first, second)
-
-
-def first_kernel(plan, place, sides, inverse, solved, message):
-    parts = [
-        lax.dot_general(sides[0, b], inverse[0, :, b * plan.block : (b + 1) * plan.block], TN,
-                        precision=lax.Precision.HIGHEST, preferred_element_type=F32)
-        for b in range(plan.rows_dev)
-    ]
-    pad_slices(plan, jnp.concatenate(parts, axis=1), solved)
-    message[...] = solved[...].astype(BF16)
 
 
 def pack_kernel(plan, place, rows, cols, *refs):
@@ -501,9 +491,12 @@
     column = (plan.padded, plan.lanes)
     slices = (n_col, plan.slice, plan.lanes)
     dma = pltpu.SemaphoreType.DMA
-    x0, message = call(
-        plan, first_kernel, [array(column, F32), array(column)], (right_sides[0:1], diag_inverse[0:1])
-    )
+    x0 = lax.dot_general(right_sides[0], diag_inverse[0], (((1,), (0,)), ((), ())), precision=lax.Precision.HIGHEST)
+    owner = jnp.arange(plan.lanes) // plan.block
+    x0 = sum(jnp.where(owner == b, x0[b], 0.0) for b in range(plan.rows_dev))
+    x0 = x0.reshape(n_col, plan.real, plan.lanes)
+    x0 = jnp.pad(x0, ((0, 0), (0, plan.slice - plan.real), (0, 0))).reshape(column)
+    message = x0.astype(BF16)
     tile_row, tile_col = tile_row.transpose(0, 2, 1), tile_col.transpose(0, 2, 1)
     message, tile_row, tile_col = lax.optimization_barrier((message, tile_row, tile_col))
     received = gather_row(message)

time: 77.9 us -> 76.5 us (0.982)
  local copies, waits for them, and re-layouts: 3.67 us -> 1.08 us
  matrix products: 0 us -> 1.29 us
    slice x2 -> x0, local copies, waits for them, and re-layouts: 1.64 us -> none  [the longest x1 0.88 us: on_device(): right_sides[0:1]]
    dot_general x0 -> x1, matrix products: none -> 1.29 us  [on_device(): lax.dot_general(right_sides[0], diag_inverse[0], (((1,), (0,)), ((), ()))...]
    unnamed x10, local copies, waits for them, and re-layouts: 2.03 us -> 1.08 us
    pallas_call x18 -> x17, Pallas kernels: 9.15 us -> 8.76 us  [call(): pl.pallas_call(kernel, out_shape=outs, in_specs=specs, out_specs=[pl.Bloc...]
  transfers between devices with their start and end apart: 35 -> 35, of which waited for: 20 -> 22; matrix products, arithmetic and copies ran while one was open for 0% -> 0% of each run, Pallas kernels for 5% -> 5%
where the time goes in v6:
time: 76.5 us; the launch traced here: 76.3 us
  starting transfers between devices  41.1 us (54%)
  waiting for transfers between devices  23.9 us (31%)
  Pallas kernels  8.76 us (11%)
  matrix products  1.29 us (2%)
  local copies, waits for them, and re-layouts  1.08 us (1%)
    ppermute x18, starting transfers between devices, over_row(): return lax.ppermute(value, 'row', [(i, i ^ m) for i in range(n_row)])  28 us
    ppermute x18, waiting for transfers between devices, over_row(): return lax.ppermute(value, 'row', [(i, i ^ m) for i in range(n_row)])  14.4 us
    ppermute x17, starting transfers between devices, over_col(): return lax.ppermute(value, 'col', [(i, i ^ m) for i in range(n_col)])  13.1 us
    ppermute x17, waiting for transfers between devices, over_col(): return lax.ppermute(value, 'col', [(i, i ^ m) for i in range(n_col)])  9.5 us
    pallas_call x17, Pallas kernels, call(): pl.pallas_call(kernel, out_shape=outs, in_specs=specs, out_specs=[pl.Bloc...  8.76 us
  transfers between devices with their start and end apart: 35, of which 22 were waited for; matrix products, arithmetic and copies ran while one was open for 0% of the time, Pallas kernels for 5%

profile of v6, /device:TPU:0, one launch (start us, length us, event | category | flops | bytes accessed | tf_op | source)
XLA Modules:
  0.0 76.3 jit_solution(4249045065834792096)
XLA Ops:
  1.4 5.1 %collective-permute-start.2 = (bf16[128,128]{1,0:T(8,128)(2,1)S(1)}, bf16[128,128]{1,0:T(8,128)(2,1)S(1)}, u32[]{:S(2)}, u32[]{:S(2)}) collective-permute-start(bf16[128,128]{1,0:T(8,128)(2,1)S(1)} %get-tuple-element.72.refs_1_), channel_id=1, source_target_pairs={{0,24},{8,16},{16,8},{24,0},{1,25},{9,17},{17,9},{25,1},{2,26},{10... | collective-permute-start | bytes 98312 | tf_op jit(solution)/shard_map/ppermute | solution.py:474
  9.1 2.2 %collective-permute-done.1.refs_3_ = bf16[128,128]{1,0:T(8,128)(2,1)S(1)} collective-permute-done((bf16[128,128]{1,0:T(8,128)(2,1)S(1)}, bf16[128,128]{1,0:T(8,128)(2,1)S(1)}, u32[]{:S(2)}, u32[]{:S(2)}) %collective-permute-start.1) | collective-permute-done | bytes 32800 | tf_op jit(solution)/shard_map/ppermute | solution.py:474
  11.9 1.6 %collective-permute-start.10 = (bf16[1,464,128]{2,1,0:T(8,128)(2,1)S(1)}, bf16[1,464,128]{2,1,0:T(8,128)(2,1)S(1)}, u32[]{:S(2)}, u32[]{:S(2)}) collective-permute-start(bf16[1,464,128]{2,1,0:T(8,128)(2,1)S(1)} %get-tuple-element.88.refs_0_), channel_id=1, source_target_pairs={{0,2},{1,3},{2,0},{3,1},{4,6},{5,7},{6,4},{7,5},{8,10},{9,11},{10,... | collective-permute-start | bytes 356360 | tf_op jit(solution)/shard_map/ppermute | solution.py:477
  13.5 1.5 %collective-permute-start.11 = (bf16[1,464,128]{2,1,0:T(8,128)(2,1)S(1)}, bf16[1,464,128]{2,1,0:T(8,128)(2,1)S(1)}, u32[]{:S(2)}, u32[]{:S(2)}) collective-permute-start(bf16[1,464,128]{2,1,0:T(8,128)(2,1)S(1)} %get-tuple-element.90.refs_0_), channel_id=1, source_target_pairs={{0,4},{1,5},{2,6},{3,7},{4,0},{5,1},{6,2},{7,3},{8,12},{9,13},{10,... | collective-permute-start | bytes 356360 | tf_op jit(solution)/shard_map/ppermute | solution.py:477
  17.1 1.5 %collective-permute-start.6 = (bf16[22,16,128]{2,1,0:T(8,128)(2,1)S(1)}, bf16[22,16,128]{2,1,0:T(8,128)(2,1)S(1)}, u32[]{:S(2)}, u32[]{:S(2)}) collective-permute-start(bf16[22,16,128]{2,1,0:T(8,128)(2,1)S(1)} %get-tuple-element.81), channel_id=1, source_target_pairs={{0,2},{1,3},{2,0},{3,1},{4,6},{5,7},{6,4},{7,5},{8,10},{9,11},{10,... | collective-permute-start | bytes 270344 | tf_op jit(solution)/shard_map/ppermute | solution.py:477
  18.6 1.9 %collective-permute-done.11.refs_1_ = bf16[1,464,128]{2,1,0:T(8,128)(2,1)S(1)} collective-permute-done((bf16[1,464,128]{2,1,0:T(8,128)(2,1)S(1)}, bf16[1,464,128]{2,1,0:T(8,128)(2,1)S(1)}, u32[]{:S(2)}, u32[]{:S(2)}) %collective-permute-start.11) | collective-permute-done | bytes 118816 | tf_op jit(solution)/shard_map/ppermute | solution.py:477
  23.3 1.6 %collective-permute-start.12 = (bf16[2,464,128]{2,1,0:T(8,128)(2,1)S(1)}, bf16[2,464,128]{2,1,0:T(8,128)(2,1)S(1)}, u32[]{:S(2)}, u32[]{:S(2)}) collective-permute-start(bf16[2,464,128]{2,1,0:T(8,128)(2,1)S(1)} %shard_map.59.refs_0_), channel_id=1, source_target_pairs={{0,4},{1,5},{2,6},{3,7},{4,0},{5,1},{6,2},{7,3},{8,12},{9,13},{10,... | collective-permute-start | bytes 712712 | tf_op jit(solution)/shard_map/ppermute | solution.py:477
  25.1 1.6 %collective-permute-start.9 = (bf16[8,16,128]{2,1,0:T(8,128)(2,1)S(1)}, bf16[8,16,128]{2,1,0:T(8,128)(2,1)S(1)}, u32[]{:S(2)}, u32[]{:S(2)}) collective-permute-start(bf16[8,16,128]{2,1,0:T(8,128)(2,1)S(1)} %get-tuple-element.96.refs_1_), channel_id=1, source_target_pairs={{0,24},{8,16},{16,8},{24,0},{1,25},{9,17},{17,9},{25,1},{2,26},{10... | collective-permute-start | bytes 98312 | tf_op jit(solution)/shard_map/ppermute | solution.py:474
  27.3 2.3 %collective-permute-start.7 = (bf16[8,16,128]{2,1,0:T(8,128)(2,1)S(1)}, bf16[8,16,128]{2,1,0:T(8,128)(2,1)S(1)}, u32[]{:S(2)}, u32[]{:S(2)}) collective-permute-start(bf16[8,16,128]{2,1,0:T(8,128)(2,1)S(1)} %get-tuple-element.96.refs_1_), channel_id=1, source_target_pairs={{0,8},{8,0},{16,24},{24,16},{1,9},{9,1},{17,25},{25,17},{2,10},{10... | collective-permute-start | bytes 98312 | tf_op jit(solution)/shard_map/ppermute | solution.py:474
  29.6 1.6 %collective-permute-done.9.refs_4_ = bf16[8,16,128]{2,1,0:T(8,128)(2,1)S(1)} collective-permute-done((bf16[8,16,128]{2,1,0:T(8,128)(2,1)S(1)}, bf16[8,16,128]{2,1,0:T(8,128)(2,1)S(1)}, u32[]{:S(2)}, u32[]{:S(2)}) %collective-permute-start.9) | collective-permute-done | bytes 32800 | tf_op jit(solution)/shard_map/ppermute | solution.py:474
  34.6 2.4 %collective-permute-start.18 = (bf16[8,16,128]{2,1,0:T(8,128)(2,1)S(1)}, bf16[8,16,128]{2,1,0:T(8,128)(2,1)S(1)}, u32[]{:S(2)}, u32[]{:S(2)}) collective-permute-start(bf16[8,16,128]{2,1,0:T(8,128)(2,1)S(1)} %get-tuple-element.106.refs_1_), channel_id=1, source_target_pairs={{0,24},{8,16},{16,8},{24,0},{1,25},{9,17},{17,9},{25,1},{2,26},{10... | collective-permute-start | bytes 98312 | tf_op jit(solution)/shard_map/ppermute | solution.py:474
  39.0 1.5 %collective-permute-done.18.refs_4_ = bf16[8,16,128]{2,1,0:T(8,128)(2,1)S(1)} collective-permute-done((bf16[8,16,128]{2,1,0:T(8,128)(2,1)S(1)}, bf16[8,16,128]{2,1,0:T(8,128)(2,1)S(1)}, u32[]{:S(2)}, u32[]{:S(2)}) %collective-permute-start.18) | collective-permute-done | bytes 32800 | tf_op jit(solution)/shard_map/ppermute | solution.py:474
  42.5 1.7 %shard_map.66 = (bf16[8,16,128]{2,1,0:T(8,128)(2,1)S(1)}, f32[8,16,128]{2,1,0:T(8,128)S(1)}, bf16[8,16,128]{2,1,0:T(8,128)(2,1)S(1)}, bf16[8,16,128]{2,1,0:T(8,128)(2,1)S(1)}, bf16[8,16,128]{2,1,0:T(8,128)(2,1)S(1)}) custom-call(bf16[22,16,128]{2,1,0:T(8,128)(2,1)S(1)} %get-tuple-element.78.refs_1_.refs_0_, ...), custom_call_target="tpu_custom_call" | custom-call | tf_op jit(solution)/shard_map/pallas_call | solution.py:49
  44.2 1.7 %collective-permute-start.19 = (bf16[8,16,128]{2,1,0:T(8,128)(2,1)S(1)}, bf16[8,16,128]{2,1,0:T(8,128)(2,1)S(1)}, u32[]{:S(2)}, u32[]{:S(2)}) collective-permute-start(bf16[8,16,128]{2,1,0:T(8,128)(2,1)S(1)} %get-tuple-element.114), channel_id=1, source_target_pairs={{0,24},{8,16},{16,8},{24,0},{1,25},{9,17},{17,9},{25,1},{2,26},{10... | collective-permute-start | bytes 98312 | tf_op jit(solution)/shard_map/ppermute | solution.py:474
  46.7 2.0 %collective-permute-start.21 = (bf16[8,16,128]{2,1,0:T(8,128)(2,1)S(1)}, bf16[8,16,128]{2,1,0:T(8,128)(2,1)S(1)}, u32[]{:S(2)}, u32[]{:S(2)}) collective-permute-start(bf16[8,16,128]{2,1,0:T(8,128)(2,1)S(1)} %get-tuple-element.116), channel_id=1, source_target_pairs={{0,8},{8,0},{16,24},{24,16},{1,9},{9,1},{17,25},{25,17},{2,10},{10... | collective-permute-start | bytes 98312 | tf_op jit(solution)/shard_map/ppermute | solution.py:474
  48.7 1.5 %collective-permute-done.19.refs_7_ = bf16[8,16,128]{2,1,0:T(8,128)(2,1)S(1)} collective-permute-done((bf16[8,16,128]{2,1,0:T(8,128)(2,1)S(1)}, bf16[8,16,128]{2,1,0:T(8,128)(2,1)S(1)}, u32[]{:S(2)}, u32[]{:S(2)}) %collective-permute-start.19) | collective-permute-done | bytes 32800 | tf_op jit(solution)/shard_map/ppermute | solution.py:474
  52.1 2.3 %collective-permute-start.22 = (bf16[8,16,128]{2,1,0:T(8,128)(2,1)S(1)}, bf16[8,16,128]{2,1,0:T(8,128)(2,1)S(1)}, u32[]{:S(2)}, u32[]{:S(2)}) collective-permute-start(bf16[8,16,128]{2,1,0:T(8,128)(2,1)S(1)} %get-tuple-element.119), channel_id=1, source_target_pairs={{0,24},{8,16},{16,8},{24,0},{1,25},{9,17},{17,9},{25,1},{2,26},{10... | collective-permute-start | bytes 98312 | tf_op jit(solution)/shard_map/ppermute | solution.py:474
  57.9 1.4 %collective-permute-done.23.refs_6_ = bf16[8,16,128]{2,1,0:T(8,128)(2,1)S(1)} collective-permute-done((bf16[8,16,128]{2,1,0:T(8,128)(2,1)S(1)}, bf16[8,16,128]{2,1,0:T(8,128)(2,1)S(1)}, u32[]{:S(2)}, u32[]{:S(2)}) %collective-permute-start.23) | collective-permute-done | bytes 32800 | tf_op jit(solution)/shard_map/ppermute | solution.py:474
  59.7 1.5 %collective-permute-start.25 = (bf16[12,16,128]{2,1,0:T(8,128)(2,1)S(1)}, bf16[12,16,128]{2,1,0:T(8,128)(2,1)S(1)}, u32[]{:S(2)}, u32[]{:S(2)}) collective-permute-start(bf16[12,16,128]{2,1,0:T(8,128)(2,1)S(1)} %get-tuple-element.126), channel_id=1, source_target_pairs={{0,2},{1,3},{2,0},{3,1},{4,6},{5,7},{6,4},{7,5},{8,10},{9,11},{10,... | collective-permute-start | bytes 147464 | tf_op jit(solution)/shard_map/ppermute | solution.py:477
  61.8 1.5 %collective-permute-start.27 = (bf16[12,16,128]{2,1,0:T(8,128)(2,1)S(1)}, bf16[12,16,128]{2,1,0:T(8,128)(2,1)S(1)}, u32[]{:S(2)}, u32[]{:S(2)}) collective-permute-start(bf16[12,16,128]{2,1,0:T(8,128)(2,1)S(1)} %get-tuple-element.128), channel_id=1, source_target_pairs={{0,6},{1,7},{2,4},{3,5},{4,2},{5,3},{6,0},{7,1},{8,14},{9,15},{10,... | collective-permute-start | bytes 147464 | tf_op jit(solution)/shard_map/ppermute | solution.py:477
  63.9 1.5 %collective-permute-done.26.refs_3_.refs_2_ = bf16[12,16,128]{2,1,0:T(8,128)(2,1)S(1)} collective-permute-done((bf16[12,16,128]{2,1,0:T(8,128)(2,1)S(1)}, bf16[12,16,128]{2,1,0:T(8,128)(2,1)S(1)}, u32[]{:S(2)}, u32[]{:S(2)}) %collective-permute-start.26) | collective-permute-done | bytes 49184 | tf_op jit(solution)/shard_map/ppermute | solution.py:477
  65.4 1.4 %collective-permute-done.27.refs_4_.refs_3_ = bf16[12,16,128]{2,1,0:T(8,128)(2,1)S(1)} collective-permute-done((bf16[12,16,128]{2,1,0:T(8,128)(2,1)S(1)}, bf16[12,16,128]{2,1,0:T(8,128)(2,1)S(1)}, u32[]{:S(2)}, u32[]{:S(2)}) %collective-permute-start.27) | collective-permute-done | bytes 49184 | tf_op jit(solution)/shard_map/ppermute | solution.py:477
  68.3 1.8 %collective-permute-start.32 = (bf16[128,128]{1,0:T(8,128)(2,1)S(1)}, bf16[128,128]{1,0:T(8,128)(2,1)S(1)}, u32[]{:S(2)}, u32[]{:S(2)}) collective-permute-start(bf16[128,128]{1,0:T(8,128)(2,1)S(1)} %get-tuple-element.130), channel_id=1, source_target_pairs={{0,24},{8,16},{16,8},{24,0},{1,25},{9,17},{17,9},{25,1},{2,26},{10... | collective-permute-start | bytes 98312 | tf_op jit(solution)/shard_map/ppermute | solution.py:474
  70.9 1.9 %collective-permute-start.34 = (bf16[128,128]{1,0:T(8,128)(2,1)S(1)}, bf16[128,128]{1,0:T(8,128)(2,1)S(1)}, u32[]{:S(2)}, u32[]{:S(2)}) collective-permute-start(bf16[128,128]{1,0:T(8,128)(2,1)S(1)} %get-tuple-element.132), channel_id=1, source_target_pairs={{0,8},{8,0},{16,24},{24,16},{1,9},{9,1},{17,25},{25,17},{2,10},{10... | collective-permute-start | bytes 98312 | tf_op jit(solution)/shard_map/ppermute | solution.py:474
  (76 shorter events, 31.0 us)
Async XLA Ops:
  1.4 7.7 %collective-permute-start.2 = (bf16[128,128]{1,0:T(8,128)(2,1)S(1)}, bf16[128,128]{1,0:T(8,128)(2,1)S(1)}, u32[]{:S(2)}, u32[]{:S(2)}) collective-permute-start(bf16[128,128]{1,0:T(8,128)(2,1)S(1)} %get-tuple-element.72.refs_1_), channel_id=1, source_target_pairs={{0,24},{8,16},{16,8},{24,0},{1,25},{9,17},{17,9},{25,1},{2,26},{10... | collective-permute-start | bytes 98312 | tf_op jit(solution)/shard_map/ppermute | solution.py:474
  6.5 4.8 %collective-permute-start.1 = (bf16[128,128]{1,0:T(8,128)(2,1)S(1)}, bf16[128,128]{1,0:T(8,128)(2,1)S(1)}, u32[]{:S(2)}, u32[]{:S(2)}) collective-permute-start(bf16[128,128]{1,0:T(8,128)(2,1)S(1)} %get-tuple-element.72.refs_1_), channel_id=1, source_target_pairs={{0,16},{8,24},{16,0},{24,8},{1,17},{9,25},{17,1},{25,9},{2,18},{10... | collective-permute-start | bytes 98312 | tf_op jit(solution)/shard_map/ppermute | solution.py:474
  6.5 4.8 %collective-permute-start = (bf16[128,128]{1,0:T(8,128)(2,1)S(1)}, bf16[128,128]{1,0:T(8,128)(2,1)S(1)}, u32[]{:S(2)}, u32[]{:S(2)}) collective-permute-start(bf16[128,128]{1,0:T(8,128)(2,1)S(1)} %get-tuple-element.72.refs_1_), channel_id=1, source_target_pairs={{0,8},{8,0},{16,24},{24,16},{1,9},{9,1},{17,25},{25,17},{2,10},{10... | collective-permute-start | bytes 98312 | tf_op jit(solution)/shard_map/ppermute | solution.py:474
  11.9 6.7 %collective-permute-start.10 = (bf16[1,464,128]{2,1,0:T(8,128)(2,1)S(1)}, bf16[1,464,128]{2,1,0:T(8,128)(2,1)S(1)}, u32[]{:S(2)}, u32[]{:S(2)}) collective-permute-start(bf16[1,464,128]{2,1,0:T(8,128)(2,1)S(1)} %get-tuple-element.88.refs_0_), channel_id=1, source_target_pairs={{0,2},{1,3},{2,0},{3,1},{4,6},{5,7},{6,4},{7,5},{8,10},{9,11},{10,... | collective-permute-start | bytes 356360 | tf_op jit(solution)/shard_map/ppermute | solution.py:477
  13.5 7.1 %collective-permute-start.11 = (bf16[1,464,128]{2,1,0:T(8,128)(2,1)S(1)}, bf16[1,464,128]{2,1,0:T(8,128)(2,1)S(1)}, u32[]{:S(2)}, u32[]{:S(2)}) collective-permute-start(bf16[1,464,128]{2,1,0:T(8,128)(2,1)S(1)} %get-tuple-element.90.refs_0_), channel_id=1, source_target_pairs={{0,4},{1,5},{2,6},{3,7},{4,0},{5,1},{6,2},{7,3},{8,12},{9,13},{10,... | collective-permute-start | bytes 356360 | tf_op jit(solution)/shard_map/ppermute | solution.py:477
  15.0 6.4 %collective-permute-start.4 = (bf16[22,16,128]{2,1,0:T(8,128)(2,1)S(1)}, bf16[22,16,128]{2,1,0:T(8,128)(2,1)S(1)}, u32[]{:S(2)}, u32[]{:S(2)}) collective-permute-start(bf16[22,16,128]{2,1,0:T(8,128)(2,1)S(1)} %get-tuple-element.79), channel_id=1, source_target_pairs={{0,6},{1,7},{2,4},{3,5},{4,2},{5,3},{6,0},{7,1},{8,14},{9,15},{10,... | collective-permute-start | bytes 270344 | tf_op jit(solution)/shard_map/ppermute | solution.py:477
  16.0 6.7 %collective-permute-start.5 = (bf16[22,16,128]{2,1,0:T(8,128)(2,1)S(1)}, bf16[22,16,128]{2,1,0:T(8,128)(2,1)S(1)}, u32[]{:S(2)}, u32[]{:S(2)}) collective-permute-start(bf16[22,16,128]{2,1,0:T(8,128)(2,1)S(1)} %get-tuple-element.80), channel_id=1, source_target_pairs={{0,4},{1,5},{2,6},{3,7},{4,0},{5,1},{6,2},{7,3},{8,12},{9,13},{10,... | collective-permute-start | bytes 270344 | tf_op jit(solution)/shard_map/ppermute | solution.py:477
  17.1 5.5 %collective-permute-start.6 = (bf16[22,16,128]{2,1,0:T(8,128)(2,1)S(1)}, bf16[22,16,128]{2,1,0:T(8,128)(2,1)S(1)}, u32[]{:S(2)}, u32[]{:S(2)}) collective-permute-start(bf16[22,16,128]{2,1,0:T(8,128)(2,1)S(1)} %get-tuple-element.81), channel_id=1, source_target_pairs={{0,2},{1,3},{2,0},{3,1},{4,6},{5,7},{6,4},{7,5},{8,10},{9,11},{10,... | collective-permute-start | bytes 270344 | tf_op jit(solution)/shard_map/ppermute | solution.py:477
  22.7 9.2 %collective-permute-start.13 = (bf16[2,464,128]{2,1,0:T(8,128)(2,1)S(1)}, bf16[2,464,128]{2,1,0:T(8,128)(2,1)S(1)}, u32[]{:S(2)}, u32[]{:S(2)}) collective-permute-start(bf16[2,464,128]{2,1,0:T(8,128)(2,1)S(1)} %shard_map.60.refs_0_), channel_id=1, source_target_pairs={{0,2},{1,3},{2,0},{3,1},{4,6},{5,7},{6,4},{7,5},{8,10},{9,11},{10,... | collective-permute-start | bytes 712712 | tf_op jit(solution)/shard_map/ppermute | solution.py:477
  23.3 8.6 %collective-permute-start.12 = (bf16[2,464,128]{2,1,0:T(8,128)(2,1)S(1)}, bf16[2,464,128]{2,1,0:T(8,128)(2,1)S(1)}, u32[]{:S(2)}, u32[]{:S(2)}) collective-permute-start(bf16[2,464,128]{2,1,0:T(8,128)(2,1)S(1)} %shard_map.59.refs_0_), channel_id=1, source_target_pairs={{0,4},{1,5},{2,6},{3,7},{4,0},{5,1},{6,2},{7,3},{8,12},{9,13},{10,... | collective-permute-start | bytes 712712 | tf_op jit(solution)/shard_map/ppermute | solution.py:477
  25.1 6.0 %collective-permute-start.9 = (bf16[8,16,128]{2,1,0:T(8,128)(2,1)S(1)}, bf16[8,16,128]{2,1,0:T(8,128)(2,1)S(1)}, u32[]{:S(2)}, u32[]{:S(2)}) collective-permute-start(bf16[8,16,128]{2,1,0:T(8,128)(2,1)S(1)} %get-tuple-element.96.refs_1_), channel_id=1, source_target_pairs={{0,24},{8,16},{16,8},{24,0},{1,25},{9,17},{17,9},{25,1},{2,26},{10... | collective-permute-start | bytes 98312 | tf_op jit(solution)/shard_map/ppermute | solution.py:474
  26.8 4.9 %collective-permute-start.8 = (bf16[8,16,128]{2,1,0:T(8,128)(2,1)S(1)}, bf16[8,16,128]{2,1,0:T(8,128)(2,1)S(1)}, u32[]{:S(2)}, u32[]{:S(2)}) collective-permute-start(bf16[8,16,128]{2,1,0:T(8,128)(2,1)S(1)} %get-tuple-element.96.refs_1_), channel_id=1, source_target_pairs={{0,16},{8,24},{16,0},{24,8},{1,17},{9,25},{17,1},{25,9},{2,18},{10... | collective-permute-start | bytes 98312 | tf_op jit(solution)/shard_map/ppermute | solution.py:474
  27.3 4.6 %collective-permute-start.7 = (bf16[8,16,128]{2,1,0:T(8,128)(2,1)S(1)}, bf16[8,16,128]{2,1,0:T(8,128)(2,1)S(1)}, u32[]{:S(2)}, u32[]{:S(2)}) collective-permute-start(bf16[8,16,128]{2,1,0:T(8,128)(2,1)S(1)} %get-tuple-element.96.refs_1_), channel_id=1, source_target_pairs={{0,8},{8,0},{16,24},{24,16},{1,9},{9,1},{17,25},{25,17},{2,10},{10... | collective-permute-start | bytes 98312 | tf_op jit(solution)/shard_map/ppermute | solution.py:474
  32.0 10.5 %collective-permute-start.15 = (bf16[4,464,128]{2,1,0:T(8,128)(2,1)S(1)}, bf16[4,464,128]{2,1,0:T(8,128)(2,1)S(1)}, u32[]{:S(2)}, u32[]{:S(2)}) collective-permute-start(bf16[4,464,128]{2,1,0:T(8,128)(2,1)S(1)} %shard_map.62.refs_0_.refs_4_), channel_id=1, source_target_pairs={{0,1},{1,0},{2,3},{3,2},{4,5},{5,4},{6,7},{7,6},{8,9},{9,8},{10,11... | collective-permute-start | bytes 1425416 | tf_op jit(solution)/shard_map/ppermute | solution.py:477
  34.6 6.0 %collective-permute-start.18 = (bf16[8,16,128]{2,1,0:T(8,128)(2,1)S(1)}, bf16[8,16,128]{2,1,0:T(8,128)(2,1)S(1)}, u32[]{:S(2)}, u32[]{:S(2)}) collective-permute-start(bf16[8,16,128]{2,1,0:T(8,128)(2,1)S(1)} %get-tuple-element.106.refs_1_), channel_id=1, source_target_pairs={{0,24},{8,16},{16,8},{24,0},{1,25},{9,17},{17,9},{25,1},{2,26},{10... | collective-permute-start | bytes 98312 | tf_op jit(solution)/shard_map/ppermute | solution.py:474
  37.0 4.9 %collective-permute-start.17 = (bf16[8,16,128]{2,1,0:T(8,128)(2,1)S(1)}, bf16[8,16,128]{2,1,0:T(8,128)(2,1)S(1)}, u32[]{:S(2)}, u32[]{:S(2)}) collective-permute-start(bf16[8,16,128]{2,1,0:T(8,128)(2,1)S(1)} %get-tuple-element.106.refs_1_), channel_id=1, source_target_pairs={{0,16},{8,24},{16,0},{24,8},{1,17},{9,25},{17,1},{25,9},{2,18},{10... | collective-permute-start | bytes 98312 | tf_op jit(solution)/shard_map/ppermute | solution.py:474
  44.2 6.0 %collective-permute-start.19 = (bf16[8,16,128]{2,1,0:T(8,128)(2,1)S(1)}, bf16[8,16,128]{2,1,0:T(8,128)(2,1)S(1)}, u32[]{:S(2)}, u32[]{:S(2)}) collective-permute-start(bf16[8,16,128]{2,1,0:T(8,128)(2,1)S(1)} %get-tuple-element.114), channel_id=1, source_target_pairs={{0,24},{8,16},{16,8},{24,0},{1,25},{9,17},{17,9},{25,1},{2,26},{10... | collective-permute-start | bytes 98312 | tf_op jit(solution)/shard_map/ppermute | solution.py:474
  45.9 5.2 %collective-permute-start.20 = (bf16[8,16,128]{2,1,0:T(8,128)(2,1)S(1)}, bf16[8,16,128]{2,1,0:T(8,128)(2,1)S(1)}, u32[]{:S(2)}, u32[]{:S(2)}) collective-permute-start(bf16[8,16,128]{2,1,0:T(8,128)(2,1)S(1)} %get-tuple-element.115), channel_id=1, source_target_pairs={{0,16},{8,24},{16,0},{24,8},{1,17},{9,25},{17,1},{25,9},{2,18},{10... | collective-permute-start | bytes 98312 | tf_op jit(solution)/shard_map/ppermute | solution.py:474
  46.7 4.4 %collective-permute-start.21 = (bf16[8,16,128]{2,1,0:T(8,128)(2,1)S(1)}, bf16[8,16,128]{2,1,0:T(8,128)(2,1)S(1)}, u32[]{:S(2)}, u32[]{:S(2)}) collective-permute-start(bf16[8,16,128]{2,1,0:T(8,128)(2,1)S(1)} %get-tuple-element.116), channel_id=1, source_target_pairs={{0,8},{8,0},{16,24},{24,16},{1,9},{9,1},{17,25},{25,17},{2,10},{10... | collective-permute-start | bytes 98312 | tf_op jit(solution)/shard_map/ppermute | solution.py:474
  52.1 5.8 %collective-permute-start.22 = (bf16[8,16,128]{2,1,0:T(8,128)(2,1)S(1)}, bf16[8,16,128]{2,1,0:T(8,128)(2,1)S(1)}, u32[]{:S(2)}, u32[]{:S(2)}) collective-permute-start(bf16[8,16,128]{2,1,0:T(8,128)(2,1)S(1)} %get-tuple-element.119), channel_id=1, source_target_pairs={{0,24},{8,16},{16,8},{24,0},{1,25},{9,17},{17,9},{25,1},{2,26},{10... | collective-permute-start | bytes 98312 | tf_op jit(solution)/shard_map/ppermute | solution.py:474
  54.4 4.9 %collective-permute-start.23 = (bf16[8,16,128]{2,1,0:T(8,128)(2,1)S(1)}, bf16[8,16,128]{2,1,0:T(8,128)(2,1)S(1)}, u32[]{:S(2)}, u32[]{:S(2)}) collective-permute-start(bf16[8,16,128]{2,1,0:T(8,128)(2,1)S(1)} %get-tuple-element.120), channel_id=1, source_target_pairs={{0,16},{8,24},{16,0},{24,8},{1,17},{9,25},{17,1},{25,9},{2,18},{10... | collective-permute-start | bytes 98312 | tf_op jit(solution)/shard_map/ppermute | solution.py:474
  61.8 5.0 %collective-permute-start.27 = (bf16[12,16,128]{2,1,0:T(8,128)(2,1)S(1)}, bf16[12,16,128]{2,1,0:T(8,128)(2,1)S(1)}, u32[]{:S(2)}, u32[]{:S(2)}) collective-permute-start(bf16[12,16,128]{2,1,0:T(8,128)(2,1)S(1)} %get-tuple-element.128), channel_id=1, source_target_pairs={{0,6},{1,7},{2,4},{3,5},{4,2},{5,3},{6,0},{7,1},{8,14},{9,15},{10,... | collective-permute-start | bytes 147464 | tf_op jit(solution)/shard_map/ppermute | solution.py:477
  68.3 6.0 %collective-permute-start.32 = (bf16[128,128]{1,0:T(8,128)(2,1)S(1)}, bf16[128,128]{1,0:T(8,128)(2,1)S(1)}, u32[]{:S(2)}, u32[]{:S(2)}) collective-permute-start(bf16[128,128]{1,0:T(8,128)(2,1)S(1)} %get-tuple-element.130), channel_id=1, source_target_pairs={{0,24},{8,16},{16,8},{24,0},{1,25},{9,17},{17,9},{25,1},{2,26},{10... | collective-permute-start | bytes 98312 | tf_op jit(solution)/shard_map/ppermute | solution.py:474
  70.1 5.1 %collective-permute-start.33 = (bf16[128,128]{1,0:T(8,128)(2,1)S(1)}, bf16[128,128]{1,0:T(8,128)(2,1)S(1)}, u32[]{:S(2)}, u32[]{:S(2)}) collective-permute-start(bf16[128,128]{1,0:T(8,128)(2,1)S(1)} %get-tuple-element.131), channel_id=1, source_target_pairs={{0,16},{8,24},{16,0},{24,8},{1,17},{9,25},{17,1},{25,9},{2,18},{10... | collective-permute-start | bytes 98312 | tf_op jit(solution)/shard_map/ppermute | solution.py:474
  (16 other events, 60.9 us)

commit v7 on v6

--- a/solution.py
+++ b/solution.py
@@ -34,7 +34,7 @@
         return self.inverse_at + self.block
 
     def extra(self):
-        return self.levels + self.block // self.slice
+        return self.levels - 1 + self.block // self.slice
 
     def sources(self):
         return [2 * chip + core for core in range(2) for chip in range(self.chips)]
@@ -175,9 +175,11 @@
             here = pl.ds(pl.multiple_of(number * width, 16), width)
             for u in range(plan.n_col):
                 out[chip, u] = total[u, here, :].astype(out.dtype)
-            for level in range(plan.levels):
-                extra[chip, at + level] = side_slices[level, here, :]
-            extra[chip, at + plan.levels : at + plan.extra()] = inverse_one[...]
+            mine = total[place[1], here, :] - side_slices[0, here, :].astype(F32)
+            out[chip, place[1]] = mine.astype(out.dtype)
+            for level in range(1, plan.levels):
+                extra[chip, at + level - 1] = side_slices[level, here, :]
+            extra[chip, at + plan.levels - 1 : at + plan.extra()] = inverse_one[...]
 
 
 def add_kernel(plan, place, keep, keep_extra, received, own, *out):
@@ -194,7 +196,7 @@
 
 def near_backward_kernel(plan, place, dense, *refs):
     refs = list(refs)
-    received = take(refs, plan.n_col)
+    received = chip_order(take(refs, plan.chips)) + chip_order(take(refs, plan.chips))
     out = take(refs, plan.n_row)
     (upper,) = refs
     width, lanes = plan.slice, plan.lanes
@@ -212,7 +214,7 @@
 
 def upper_out_kernel(plan, place, *refs):
     refs = list(refs)
-    pieces = take(refs, plan.n_col)
+    pieces = chip_order(take(refs, plan.chips)) + chip_order(take(refs, plan.chips))
     out, all_slices, result, sem = refs
     half, width = plan.block, plan.slice
     core = place[1] & 1
@@ -256,7 +258,7 @@
 def inverse_of(plan, level, extra, piece):
     if level == 1:
         ref, at = extra
-        return ref[pl.ds(at + plan.levels, plan.block // plan.slice)].reshape(plan.block, plan.lanes)
+        return ref[pl.ds(at + plan.levels - 1, plan.block // plan.slice)].reshape(plan.block, plan.lanes)
     return piece[plan.inverse_at :, :]
 
 
@@ -264,9 +266,11 @@
     made = []
     for extra, piece, offset in zip(extras(plan, place, sums), pieces, plan.sources()):
         u = place[1] ^ offset
-        side = extra[0][extra[1] + level - 1].astype(F32)
+        value = -coupled(u)
+        if level > 1:
+            value = extra[0][extra[1] + level - 2].astype(F32) + value
         inverse = inverse_of(plan, level, extra, piece)
-        made.append((inverse, u, apply_pair(inverse, side - coupled(u), plan.block)))
+        made.append((inverse, u, apply_pair(inverse, value, plan.block)))
     write(made)
 
 
@@ -531,7 +535,7 @@
         [keep, keep_extra, swapped],
     )
     own, sums = made[0], exchange_chips(made[1:])
-    held = [join(*value) for value in after(held, sums)]
+    held = [join(*held[0])] + [join(*value) for value in after(held[1:], sums)]
     if chips > 2:
         held = [step(value, s) for s, value in enumerate(held, 1)]
     solved, message = call(
@@ -582,7 +586,7 @@
         chip_order(sums) + shares + [solved[1]] + results,
     )
     messages = exchange_chips(messages)
-    messages = messages + [over_col(value, 1) for value in messages]
+    messages = chip_order(messages) + chip_order([over_col(value, 1) for value in messages])
     shares = call(
         plan, near_backward_kernel, [array(column, F32)] + [array(column)] * (n_row - 1), [dense] + messages,
         [pltpu.VMEM((plan.padded, n_col * plan.lanes), BF16)],

time: 76.5 us -> 75.2 us (0.983)
  waiting for transfers between devices: 23.9 us -> 22.6 us
    ppermute x17, waiting for transfers between devices: 9.5 us -> 8.08 us  [over_col(): return lax.ppermute(value, 'col', [(i, i ^ m) for i in range(n_col)])]
  transfers between devices with their start and end apart: 35 -> 35, of which waited for: 22 -> 23; matrix products, arithmetic and copies ran while one was open for 0% -> 0% of each run, Pallas kernels for 5% -> 5%
where the time goes in v7:
time: 75.2 us; the launch traced here: 75 us
  starting transfers between devices  41.1 us (55%)
  waiting for transfers between devices  22.6 us (30%)
  Pallas kernels  8.74 us (12%)
  matrix products  1.29 us (2%)
  local copies, waits for them, and re-layouts  1.08 us (1%)
    ppermute x18, starting transfers between devices, over_row(): return lax.ppermute(value, 'row', [(i, i ^ m) for i in range(n_row)])  28 us
    ppermute x18, waiting for transfers between devices, over_row(): return lax.ppermute(value, 'row', [(i, i ^ m) for i in range(n_row)])  14.5 us
    ppermute x17, starting transfers between devices, over_col(): return lax.ppermute(value, 'col', [(i, i ^ m) for i in range(n_col)])  13 us
    pallas_call x17, Pallas kernels, call(): pl.pallas_call(kernel, out_shape=outs, in_specs=specs, out_specs=[pl.Bloc...  8.74 us
    ppermute x17, waiting for transfers between devices, over_col(): return lax.ppermute(value, 'col', [(i, i ^ m) for i in range(n_col)])  8.08 us
  transfers between devices with their start and end apart: 35, of which 23 were waited for; matrix products, arithmetic and copies ran while one was open for 0% of the time, Pallas kernels for 5%

profile of v7, /device:TPU:0, one launch (start us, length us, event | category | flops | bytes accessed | tf_op | source)
XLA Modules:
  0.0 75.0 jit_solution(17024838930911780844)
XLA Ops:
  1.4 5.1 %collective-permute-start.2 = (bf16[128,128]{1,0:T(8,128)(2,1)S(1)}, bf16[128,128]{1,0:T(8,128)(2,1)S(1)}, u32[]{:S(2)}, u32[]{:S(2)}) collective-permute-start(bf16[128,128]{1,0:T(8,128)(2,1)S(1)} %get-tuple-element.70.refs_1_), channel_id=1, source_target_pairs={{0,24},{8,16},{16,8},{24,0},{1,25},{9,17},{17,9},{25,1},{2,26},{10... | collective-permute-start | bytes 98312 | tf_op jit(solution)/shard_map/ppermute | solution.py:478
  9.1 2.2 %collective-permute-done.1.refs_3_ = bf16[128,128]{1,0:T(8,128)(2,1)S(1)} collective-permute-done((bf16[128,128]{1,0:T(8,128)(2,1)S(1)}, bf16[128,128]{1,0:T(8,128)(2,1)S(1)}, u32[]{:S(2)}, u32[]{:S(2)}) %collective-permute-start.1) | collective-permute-done | bytes 32800 | tf_op jit(solution)/shard_map/ppermute | solution.py:478
  11.9 1.6 %collective-permute-start.10 = (bf16[1,464,128]{2,1,0:T(8,128)(2,1)S(1)}, bf16[1,464,128]{2,1,0:T(8,128)(2,1)S(1)}, u32[]{:S(2)}, u32[]{:S(2)}) collective-permute-start(bf16[1,464,128]{2,1,0:T(8,128)(2,1)S(1)} %get-tuple-element.84.refs_0_), channel_id=1, source_target_pairs={{0,2},{1,3},{2,0},{3,1},{4,6},{5,7},{6,4},{7,5},{8,10},{9,11},{10,... | collective-permute-start | bytes 356360 | tf_op jit(solution)/shard_map/ppermute | solution.py:481
  13.5 1.5 %collective-permute-start.12 = (bf16[1,464,128]{2,1,0:T(8,128)(2,1)S(1)}, bf16[1,464,128]{2,1,0:T(8,128)(2,1)S(1)}, u32[]{:S(2)}, u32[]{:S(2)}) collective-permute-start(bf16[1,464,128]{2,1,0:T(8,128)(2,1)S(1)} %get-tuple-element.86.refs_0_), channel_id=1, source_target_pairs={{0,4},{1,5},{2,6},{3,7},{4,0},{5,1},{6,2},{7,3},{8,12},{9,13},{10,... | collective-permute-start | bytes 356360 | tf_op jit(solution)/shard_map/ppermute | solution.py:481
  17.1 1.5 %collective-permute-start.6 = (bf16[20,16,128]{2,1,0:T(8,128)(2,1)S(1)}, bf16[20,16,128]{2,1,0:T(8,128)(2,1)S(1)}, u32[]{:S(2)}, u32[]{:S(2)}) collective-permute-start(bf16[20,16,128]{2,1,0:T(8,128)(2,1)S(1)} %get-tuple-element.79), channel_id=1, source_target_pairs={{0,2},{1,3},{2,0},{3,1},{4,6},{5,7},{6,4},{7,5},{8,10},{9,11},{10,... | collective-permute-start | bytes 245768 | tf_op jit(solution)/shard_map/ppermute | solution.py:481
  21.3 1.3 %collective-permute-done.5.refs_3_.refs_2_ = bf16[20,16,128]{2,1,0:T(8,128)(2,1)S(1)} collective-permute-done((bf16[20,16,128]{2,1,0:T(8,128)(2,1)S(1)}, bf16[20,16,128]{2,1,0:T(8,128)(2,1)S(1)}, u32[]{:S(2)}, u32[]{:S(2)}) %collective-permute-start.5) | collective-permute-done | bytes 81952 | tf_op jit(solution)/shard_map/ppermute | solution.py:481
  24.0 1.6 %collective-permute-start.9 = (bf16[8,16,128]{2,1,0:T(8,128)(2,1)S(1)}, bf16[8,16,128]{2,1,0:T(8,128)(2,1)S(1)}, u32[]{:S(2)}, u32[]{:S(2)}) collective-permute-start(bf16[8,16,128]{2,1,0:T(8,128)(2,1)S(1)} %get-tuple-element.92.refs_1_), channel_id=1, source_target_pairs={{0,24},{8,16},{16,8},{24,0},{1,25},{9,17},{17,9},{25,1},{2,26},{10... | collective-permute-start | bytes 98312 | tf_op jit(solution)/shard_map/ppermute | solution.py:478
  26.2 2.3 %collective-permute-start.7 = (bf16[8,16,128]{2,1,0:T(8,128)(2,1)S(1)}, bf16[8,16,128]{2,1,0:T(8,128)(2,1)S(1)}, u32[]{:S(2)}, u32[]{:S(2)}) collective-permute-start(bf16[8,16,128]{2,1,0:T(8,128)(2,1)S(1)} %get-tuple-element.92.refs_1_), channel_id=1, source_target_pairs={{0,8},{8,0},{16,24},{24,16},{1,9},{9,1},{17,25},{25,17},{2,10},{10... | collective-permute-start | bytes 98312 | tf_op jit(solution)/shard_map/ppermute | solution.py:478
  28.5 1.3 %collective-permute-done.9.refs_4_ = bf16[8,16,128]{2,1,0:T(8,128)(2,1)S(1)} collective-permute-done((bf16[8,16,128]{2,1,0:T(8,128)(2,1)S(1)}, bf16[8,16,128]{2,1,0:T(8,128)(2,1)S(1)}, u32[]{:S(2)}, u32[]{:S(2)}) %collective-permute-start.9) | collective-permute-done | bytes 32800 | tf_op jit(solution)/shard_map/ppermute | solution.py:478
  33.4 2.4 %collective-permute-start.18 = (bf16[8,16,128]{2,1,0:T(8,128)(2,1)S(1)}, bf16[8,16,128]{2,1,0:T(8,128)(2,1)S(1)}, u32[]{:S(2)}, u32[]{:S(2)}) collective-permute-start(bf16[8,16,128]{2,1,0:T(8,128)(2,1)S(1)} %get-tuple-element.102.refs_1_), channel_id=1, source_target_pairs={{0,24},{8,16},{16,8},{24,0},{1,25},{9,17},{17,9},{25,1},{2,26},{10... | collective-permute-start | bytes 98312 | tf_op jit(solution)/shard_map/ppermute | solution.py:478
  37.9 1.6 %collective-permute-done.18.refs_4_ = bf16[8,16,128]{2,1,0:T(8,128)(2,1)S(1)} collective-permute-done((bf16[8,16,128]{2,1,0:T(8,128)(2,1)S(1)}, bf16[8,16,128]{2,1,0:T(8,128)(2,1)S(1)}, u32[]{:S(2)}, u32[]{:S(2)}) %collective-permute-start.18) | collective-permute-done | bytes 32800 | tf_op jit(solution)/shard_map/ppermute | solution.py:478
  41.4 1.7 %shard_map.66 = (bf16[8,16,128]{2,1,0:T(8,128)(2,1)S(1)}, f32[8,16,128]{2,1,0:T(8,128)S(1)}, bf16[8,16,128]{2,1,0:T(8,128)(2,1)S(1)}, bf16[8,16,128]{2,1,0:T(8,128)(2,1)S(1)}, bf16[8,16,128]{2,1,0:T(8,128)(2,1)S(1)}) custom-call(bf16[20,16,128]{2,1,0:T(8,128)(2,1)S(1)} %get-tuple-element.76.refs_1_.refs_0_, ...), custom_call_target="tpu_custom_call" | custom-call | tf_op jit(solution)/shard_map/pallas_call | solution.py:49
  43.1 1.7 %collective-permute-start.19 = (bf16[8,16,128]{2,1,0:T(8,128)(2,1)S(1)}, bf16[8,16,128]{2,1,0:T(8,128)(2,1)S(1)}, u32[]{:S(2)}, u32[]{:S(2)}) collective-permute-start(bf16[8,16,128]{2,1,0:T(8,128)(2,1)S(1)} %get-tuple-element.110), channel_id=1, source_target_pairs={{0,24},{8,16},{16,8},{24,0},{1,25},{9,17},{17,9},{25,1},{2,26},{10... | collective-permute-start | bytes 98312 | tf_op jit(solution)/shard_map/ppermute | solution.py:478
  45.6 2.0 %collective-permute-start.21 = (bf16[8,16,128]{2,1,0:T(8,128)(2,1)S(1)}, bf16[8,16,128]{2,1,0:T(8,128)(2,1)S(1)}, u32[]{:S(2)}, u32[]{:S(2)}) collective-permute-start(bf16[8,16,128]{2,1,0:T(8,128)(2,1)S(1)} %get-tuple-element.112), channel_id=1, source_target_pairs={{0,8},{8,0},{16,24},{24,16},{1,9},{9,1},{17,25},{25,17},{2,10},{10... | collective-permute-start | bytes 98312 | tf_op jit(solution)/shard_map/ppermute | solution.py:478
  47.6 1.5 %collective-permute-done.19.refs_7_ = bf16[8,16,128]{2,1,0:T(8,128)(2,1)S(1)} collective-permute-done((bf16[8,16,128]{2,1,0:T(8,128)(2,1)S(1)}, bf16[8,16,128]{2,1,0:T(8,128)(2,1)S(1)}, u32[]{:S(2)}, u32[]{:S(2)}) %collective-permute-start.19) | collective-permute-done | bytes 32800 | tf_op jit(solution)/shard_map/ppermute | solution.py:478
  51.0 2.3 %collective-permute-start.22 = (bf16[8,16,128]{2,1,0:T(8,128)(2,1)S(1)}, bf16[8,16,128]{2,1,0:T(8,128)(2,1)S(1)}, u32[]{:S(2)}, u32[]{:S(2)}) collective-permute-start(bf16[8,16,128]{2,1,0:T(8,128)(2,1)S(1)} %get-tuple-element.115), channel_id=1, source_target_pairs={{0,24},{8,16},{16,8},{24,0},{1,25},{9,17},{17,9},{25,1},{2,26},{10... | collective-permute-start | bytes 98312 | tf_op jit(solution)/shard_map/ppermute | solution.py:478
  54.1 1.4 %collective-permute-start.24 = (bf16[8,16,128]{2,1,0:T(8,128)(2,1)S(1)}, bf16[8,16,128]{2,1,0:T(8,128)(2,1)S(1)}, u32[]{:S(2)}, u32[]{:S(2)}) collective-permute-start(bf16[8,16,128]{2,1,0:T(8,128)(2,1)S(1)} %get-tuple-element.117), channel_id=1, source_target_pairs={{0,8},{8,0},{16,24},{24,16},{1,9},{9,1},{17,25},{25,17},{2,10},{10... | collective-permute-start | bytes 98312 | tf_op jit(solution)/shard_map/ppermute | solution.py:478
  55.4 1.3 %collective-permute-done.22.refs_5_ = bf16[8,16,128]{2,1,0:T(8,128)(2,1)S(1)} collective-permute-done((bf16[8,16,128]{2,1,0:T(8,128)(2,1)S(1)}, bf16[8,16,128]{2,1,0:T(8,128)(2,1)S(1)}, u32[]{:S(2)}, u32[]{:S(2)}) %collective-permute-start.22) | collective-permute-done | bytes 32800 | tf_op jit(solution)/shard_map/ppermute | solution.py:478
  56.8 1.4 %collective-permute-done.23.refs_6_ = bf16[8,16,128]{2,1,0:T(8,128)(2,1)S(1)} collective-permute-done((bf16[8,16,128]{2,1,0:T(8,128)(2,1)S(1)}, bf16[8,16,128]{2,1,0:T(8,128)(2,1)S(1)}, u32[]{:S(2)}, u32[]{:S(2)}) %collective-permute-start.23) | collective-permute-done | bytes 32800 | tf_op jit(solution)/shard_map/ppermute | solution.py:478
  58.6 2.4 %collective-permute-start.25 = (bf16[12,16,128]{2,1,0:T(8,128)(2,1)S(1)}, bf16[12,16,128]{2,1,0:T(8,128)(2,1)S(1)}, u32[]{:S(2)}, u32[]{:S(2)}) collective-permute-start(bf16[12,16,128]{2,1,0:T(8,128)(2,1)S(1)} %get-tuple-element.122), channel_id=1, source_target_pairs={{0,6},{1,7},{2,4},{3,5},{4,2},{5,3},{6,0},{7,1},{8,14},{9,15},{10,... | collective-permute-start | bytes 147464 | tf_op jit(solution)/shard_map/ppermute | solution.py:481
  62.2 1.5 %collective-permute-done.25.refs_2_.refs_1_ = bf16[12,16,128]{2,1,0:T(8,128)(2,1)S(1)} collective-permute-done((bf16[12,16,128]{2,1,0:T(8,128)(2,1)S(1)}, bf16[12,16,128]{2,1,0:T(8,128)(2,1)S(1)}, u32[]{:S(2)}, u32[]{:S(2)}) %collective-permute-start.25) | collective-permute-done | bytes 49184 | tf_op jit(solution)/shard_map/ppermute | solution.py:481
  63.7 1.5 %collective-permute-done.26.refs_3_.refs_2_ = bf16[12,16,128]{2,1,0:T(8,128)(2,1)S(1)} collective-permute-done((bf16[12,16,128]{2,1,0:T(8,128)(2,1)S(1)}, bf16[12,16,128]{2,1,0:T(8,128)(2,1)S(1)}, u32[]{:S(2)}, u32[]{:S(2)}) %collective-permute-start.26) | collective-permute-done | bytes 49184 | tf_op jit(solution)/shard_map/ppermute | solution.py:481
  66.9 1.8 %collective-permute-start.32 = (bf16[128,128]{1,0:T(8,128)(2,1)S(1)}, bf16[128,128]{1,0:T(8,128)(2,1)S(1)}, u32[]{:S(2)}, u32[]{:S(2)}) collective-permute-start(bf16[128,128]{1,0:T(8,128)(2,1)S(1)} %get-tuple-element.126), channel_id=1, source_target_pairs={{0,24},{8,16},{16,8},{24,0},{1,25},{9,17},{17,9},{25,1},{2,26},{10... | collective-permute-start | bytes 98312 | tf_op jit(solution)/shard_map/ppermute | solution.py:478
  69.4 1.9 %collective-permute-start.34 = (bf16[128,128]{1,0:T(8,128)(2,1)S(1)}, bf16[128,128]{1,0:T(8,128)(2,1)S(1)}, u32[]{:S(2)}, u32[]{:S(2)}) collective-permute-start(bf16[128,128]{1,0:T(8,128)(2,1)S(1)} %get-tuple-element.128), channel_id=1, source_target_pairs={{0,8},{8,0},{16,24},{24,16},{1,9},{9,1},{17,25},{25,17},{2,10},{10... | collective-permute-start | bytes 98312 | tf_op jit(solution)/shard_map/ppermute | solution.py:478
  (76 shorter events, 29.9 us)
Async XLA Ops:
  1.4 7.7 %collective-permute-start.2 = (bf16[128,128]{1,0:T(8,128)(2,1)S(1)}, bf16[128,128]{1,0:T(8,128)(2,1)S(1)}, u32[]{:S(2)}, u32[]{:S(2)}) collective-permute-start(bf16[128,128]{1,0:T(8,128)(2,1)S(1)} %get-tuple-element.70.refs_1_), channel_id=1, source_target_pairs={{0,24},{8,16},{16,8},{24,0},{1,25},{9,17},{17,9},{25,1},{2,26},{10... | collective-permute-start | bytes 98312 | tf_op jit(solution)/shard_map/ppermute | solution.py:478
  6.5 4.8 %collective-permute-start.1 = (bf16[128,128]{1,0:T(8,128)(2,1)S(1)}, bf16[128,128]{1,0:T(8,128)(2,1)S(1)}, u32[]{:S(2)}, u32[]{:S(2)}) collective-permute-start(bf16[128,128]{1,0:T(8,128)(2,1)S(1)} %get-tuple-element.70.refs_1_), channel_id=1, source_target_pairs={{0,16},{8,24},{16,0},{24,8},{1,17},{9,25},{17,1},{25,9},{2,18},{10... | collective-permute-start | bytes 98312 | tf_op jit(solution)/shard_map/ppermute | solution.py:478
  6.5 4.8 %collective-permute-start = (bf16[128,128]{1,0:T(8,128)(2,1)S(1)}, bf16[128,128]{1,0:T(8,128)(2,1)S(1)}, u32[]{:S(2)}, u32[]{:S(2)}) collective-permute-start(bf16[128,128]{1,0:T(8,128)(2,1)S(1)} %get-tuple-element.70.refs_1_), channel_id=1, source_target_pairs={{0,8},{8,0},{16,24},{24,16},{1,9},{9,1},{17,25},{25,17},{2,10},{10... | collective-permute-start | bytes 98312 | tf_op jit(solution)/shard_map/ppermute | solution.py:478
  11.9 6.7 %collective-permute-start.10 = (bf16[1,464,128]{2,1,0:T(8,128)(2,1)S(1)}, bf16[1,464,128]{2,1,0:T(8,128)(2,1)S(1)}, u32[]{:S(2)}, u32[]{:S(2)}) collective-permute-start(bf16[1,464,128]{2,1,0:T(8,128)(2,1)S(1)} %get-tuple-element.84.refs_0_), channel_id=1, source_target_pairs={{0,2},{1,3},{2,0},{3,1},{4,6},{5,7},{6,4},{7,5},{8,10},{9,11},{10,... | collective-permute-start | bytes 356360 | tf_op jit(solution)/shard_map/ppermute | solution.py:481
  13.5 6.9 %collective-permute-start.12 = (bf16[1,464,128]{2,1,0:T(8,128)(2,1)S(1)}, bf16[1,464,128]{2,1,0:T(8,128)(2,1)S(1)}, u32[]{:S(2)}, u32[]{:S(2)}) collective-permute-start(bf16[1,464,128]{2,1,0:T(8,128)(2,1)S(1)} %get-tuple-element.86.refs_0_), channel_id=1, source_target_pairs={{0,4},{1,5},{2,6},{3,7},{4,0},{5,1},{6,2},{7,3},{8,12},{9,13},{10,... | collective-permute-start | bytes 356360 | tf_op jit(solution)/shard_map/ppermute | solution.py:481
  15.0 6.3 %collective-permute-start.4 = (bf16[20,16,128]{2,1,0:T(8,128)(2,1)S(1)}, bf16[20,16,128]{2,1,0:T(8,128)(2,1)S(1)}, u32[]{:S(2)}, u32[]{:S(2)}) collective-permute-start(bf16[20,16,128]{2,1,0:T(8,128)(2,1)S(1)} %get-tuple-element.77), channel_id=1, source_target_pairs={{0,6},{1,7},{2,4},{3,5},{4,2},{5,3},{6,0},{7,1},{8,14},{9,15},{10,... | collective-permute-start | bytes 245768 | tf_op jit(solution)/shard_map/ppermute | solution.py:481
  15.9 6.7 %collective-permute-start.5 = (bf16[20,16,128]{2,1,0:T(8,128)(2,1)S(1)}, bf16[20,16,128]{2,1,0:T(8,128)(2,1)S(1)}, u32[]{:S(2)}, u32[]{:S(2)}) collective-permute-start(bf16[20,16,128]{2,1,0:T(8,128)(2,1)S(1)} %get-tuple-element.78), channel_id=1, source_target_pairs={{0,4},{1,5},{2,6},{3,7},{4,0},{5,1},{6,2},{7,3},{8,12},{9,13},{10,... | collective-permute-start | bytes 245768 | tf_op jit(solution)/shard_map/ppermute | solution.py:481
  17.1 5.5 %collective-permute-start.6 = (bf16[20,16,128]{2,1,0:T(8,128)(2,1)S(1)}, bf16[20,16,128]{2,1,0:T(8,128)(2,1)S(1)}, u32[]{:S(2)}, u32[]{:S(2)}) collective-permute-start(bf16[20,16,128]{2,1,0:T(8,128)(2,1)S(1)} %get-tuple-element.79), channel_id=1, source_target_pairs={{0,2},{1,3},{2,0},{3,1},{4,6},{5,7},{6,4},{7,5},{8,10},{9,11},{10,... | collective-permute-start | bytes 245768 | tf_op jit(solution)/shard_map/ppermute | solution.py:481
  18.6 12.1 %collective-permute-start.11 = (bf16[2,464,128]{2,1,0:T(8,128)(2,1)S(1)}, bf16[2,464,128]{2,1,0:T(8,128)(2,1)S(1)}, u32[]{:S(2)}, u32[]{:S(2)}) collective-permute-start(bf16[2,464,128]{2,1,0:T(8,128)(2,1)S(1)} %shard_map.59.refs_0_), channel_id=1, source_target_pairs={{0,4},{1,5},{2,6},{3,7},{4,0},{5,1},{6,2},{7,3},{8,12},{9,13},{10,... | collective-permute-start | bytes 712712 | tf_op jit(solution)/shard_map/ppermute | solution.py:481
  22.6 8.1 %collective-permute-start.13 = (bf16[2,464,128]{2,1,0:T(8,128)(2,1)S(1)}, bf16[2,464,128]{2,1,0:T(8,128)(2,1)S(1)}, u32[]{:S(2)}, u32[]{:S(2)}) collective-permute-start(bf16[2,464,128]{2,1,0:T(8,128)(2,1)S(1)} %shard_map.60.refs_0_), channel_id=1, source_target_pairs={{0,2},{1,3},{2,0},{3,1},{4,6},{5,7},{6,4},{7,5},{8,10},{9,11},{10,... | collective-permute-start | bytes 712712 | tf_op jit(solution)/shard_map/ppermute | solution.py:481
  24.0 5.8 %collective-permute-start.9 = (bf16[8,16,128]{2,1,0:T(8,128)(2,1)S(1)}, bf16[8,16,128]{2,1,0:T(8,128)(2,1)S(1)}, u32[]{:S(2)}, u32[]{:S(2)}) collective-permute-start(bf16[8,16,128]{2,1,0:T(8,128)(2,1)S(1)} %get-tuple-element.92.refs_1_), channel_id=1, source_target_pairs={{0,24},{8,16},{16,8},{24,0},{1,25},{9,17},{17,9},{25,1},{2,26},{10... | collective-permute-start | bytes 98312 | tf_op jit(solution)/shard_map/ppermute | solution.py:478
  25.6 4.9 %collective-permute-start.8 = (bf16[8,16,128]{2,1,0:T(8,128)(2,1)S(1)}, bf16[8,16,128]{2,1,0:T(8,128)(2,1)S(1)}, u32[]{:S(2)}, u32[]{:S(2)}) collective-permute-start(bf16[8,16,128]{2,1,0:T(8,128)(2,1)S(1)} %get-tuple-element.92.refs_1_), channel_id=1, source_target_pairs={{0,16},{8,24},{16,0},{24,8},{1,17},{9,25},{17,1},{25,9},{2,18},{10... | collective-permute-start | bytes 98312 | tf_op jit(solution)/shard_map/ppermute | solution.py:478
  26.2 4.5 %collective-permute-start.7 = (bf16[8,16,128]{2,1,0:T(8,128)(2,1)S(1)}, bf16[8,16,128]{2,1,0:T(8,128)(2,1)S(1)}, u32[]{:S(2)}, u32[]{:S(2)}) collective-permute-start(bf16[8,16,128]{2,1,0:T(8,128)(2,1)S(1)} %get-tuple-element.92.refs_1_), channel_id=1, source_target_pairs={{0,8},{8,0},{16,24},{24,16},{1,9},{9,1},{17,25},{25,17},{2,10},{10... | collective-permute-start | bytes 98312 | tf_op jit(solution)/shard_map/ppermute | solution.py:478
  30.9 10.5 %collective-permute-start.15 = (bf16[4,464,128]{2,1,0:T(8,128)(2,1)S(1)}, bf16[4,464,128]{2,1,0:T(8,128)(2,1)S(1)}, u32[]{:S(2)}, u32[]{:S(2)}) collective-permute-start(bf16[4,464,128]{2,1,0:T(8,128)(2,1)S(1)} %shard_map.62.refs_0_.refs_4_), channel_id=1, source_target_pairs={{0,1},{1,0},{2,3},{3,2},{4,5},{5,4},{6,7},{7,6},{8,9},{9,8},{10,11... | collective-permute-start | bytes 1425416 | tf_op jit(solution)/shard_map/ppermute | solution.py:481
  33.4 6.0 %collective-permute-start.18 = (bf16[8,16,128]{2,1,0:T(8,128)(2,1)S(1)}, bf16[8,16,128]{2,1,0:T(8,128)(2,1)S(1)}, u32[]{:S(2)}, u32[]{:S(2)}) collective-permute-start(bf16[8,16,128]{2,1,0:T(8,128)(2,1)S(1)} %get-tuple-element.102.refs_1_), channel_id=1, source_target_pairs={{0,24},{8,16},{16,8},{24,0},{1,25},{9,17},{17,9},{25,1},{2,26},{10... | collective-permute-start | bytes 98312 | tf_op jit(solution)/shard_map/ppermute | solution.py:478
  35.8 4.9 %collective-permute-start.17 = (bf16[8,16,128]{2,1,0:T(8,128)(2,1)S(1)}, bf16[8,16,128]{2,1,0:T(8,128)(2,1)S(1)}, u32[]{:S(2)}, u32[]{:S(2)}) collective-permute-start(bf16[8,16,128]{2,1,0:T(8,128)(2,1)S(1)} %get-tuple-element.102.refs_1_), channel_id=1, source_target_pairs={{0,16},{8,24},{16,0},{24,8},{1,17},{9,25},{17,1},{25,9},{2,18},{10... | collective-permute-start | bytes 98312 | tf_op jit(solution)/shard_map/ppermute | solution.py:478
  43.1 6.0 %collective-permute-start.19 = (bf16[8,16,128]{2,1,0:T(8,128)(2,1)S(1)}, bf16[8,16,128]{2,1,0:T(8,128)(2,1)S(1)}, u32[]{:S(2)}, u32[]{:S(2)}) collective-permute-start(bf16[8,16,128]{2,1,0:T(8,128)(2,1)S(1)} %get-tuple-element.110), channel_id=1, source_target_pairs={{0,24},{8,16},{16,8},{24,0},{1,25},{9,17},{17,9},{25,1},{2,26},{10... | collective-permute-start | bytes 98312 | tf_op jit(solution)/shard_map/ppermute | solution.py:478
  44.8 5.2 %collective-permute-start.20 = (bf16[8,16,128]{2,1,0:T(8,128)(2,1)S(1)}, bf16[8,16,128]{2,1,0:T(8,128)(2,1)S(1)}, u32[]{:S(2)}, u32[]{:S(2)}) collective-permute-start(bf16[8,16,128]{2,1,0:T(8,128)(2,1)S(1)} %get-tuple-element.111), channel_id=1, source_target_pairs={{0,16},{8,24},{16,0},{24,8},{1,17},{9,25},{17,1},{25,9},{2,18},{10... | collective-permute-start | bytes 98312 | tf_op jit(solution)/shard_map/ppermute | solution.py:478
  51.0 5.8 %collective-permute-start.22 = (bf16[8,16,128]{2,1,0:T(8,128)(2,1)S(1)}, bf16[8,16,128]{2,1,0:T(8,128)(2,1)S(1)}, u32[]{:S(2)}, u32[]{:S(2)}) collective-permute-start(bf16[8,16,128]{2,1,0:T(8,128)(2,1)S(1)} %get-tuple-element.115), channel_id=1, source_target_pairs={{0,24},{8,16},{16,8},{24,0},{1,25},{9,17},{17,9},{25,1},{2,26},{10... | collective-permute-start | bytes 98312 | tf_op jit(solution)/shard_map/ppermute | solution.py:478
  53.3 4.9 %collective-permute-start.23 = (bf16[8,16,128]{2,1,0:T(8,128)(2,1)S(1)}, bf16[8,16,128]{2,1,0:T(8,128)(2,1)S(1)}, u32[]{:S(2)}, u32[]{:S(2)}) collective-permute-start(bf16[8,16,128]{2,1,0:T(8,128)(2,1)S(1)} %get-tuple-element.116), channel_id=1, source_target_pairs={{0,16},{8,24},{16,0},{24,8},{1,17},{9,25},{17,1},{25,9},{2,18},{10... | collective-permute-start | bytes 98312 | tf_op jit(solution)/shard_map/ppermute | solution.py:478
  58.6 5.1 %collective-permute-start.25 = (bf16[12,16,128]{2,1,0:T(8,128)(2,1)S(1)}, bf16[12,16,128]{2,1,0:T(8,128)(2,1)S(1)}, u32[]{:S(2)}, u32[]{:S(2)}) collective-permute-start(bf16[12,16,128]{2,1,0:T(8,128)(2,1)S(1)} %get-tuple-element.122), channel_id=1, source_target_pairs={{0,6},{1,7},{2,4},{3,5},{4,2},{5,3},{6,0},{7,1},{8,14},{9,15},{10,... | collective-permute-start | bytes 147464 | tf_op jit(solution)/shard_map/ppermute | solution.py:481
  66.9 6.2 %collective-permute-start.32 = (bf16[128,128]{1,0:T(8,128)(2,1)S(1)}, bf16[128,128]{1,0:T(8,128)(2,1)S(1)}, u32[]{:S(2)}, u32[]{:S(2)}) collective-permute-start(bf16[128,128]{1,0:T(8,128)(2,1)S(1)} %get-tuple-element.126), channel_id=1, source_target_pairs={{0,24},{8,16},{16,8},{24,0},{1,25},{9,17},{17,9},{25,1},{2,26},{10... | collective-permute-start | bytes 98312 | tf_op jit(solution)/shard_map/ppermute | solution.py:478
  68.7 5.3 %collective-permute-start.33 = (bf16[128,128]{1,0:T(8,128)(2,1)S(1)}, bf16[128,128]{1,0:T(8,128)(2,1)S(1)}, u32[]{:S(2)}, u32[]{:S(2)}) collective-permute-start(bf16[128,128]{1,0:T(8,128)(2,1)S(1)} %get-tuple-element.127), channel_id=1, source_target_pairs={{0,16},{8,24},{16,0},{24,8},{1,17},{9,25},{17,1},{25,9},{2,18},{10... | collective-permute-start | bytes 98312 | tf_op jit(solution)/shard_map/ppermute | solution.py:478
  69.4 4.5 %collective-permute-start.34 = (bf16[128,128]{1,0:T(8,128)(2,1)S(1)}, bf16[128,128]{1,0:T(8,128)(2,1)S(1)}, u32[]{:S(2)}, u32[]{:S(2)}) collective-permute-start(bf16[128,128]{1,0:T(8,128)(2,1)S(1)} %get-tuple-element.128), channel_id=1, source_target_pairs={{0,8},{8,0},{16,24},{24,16},{1,9},{9,1},{17,25},{25,17},{2,10},{10... | collective-permute-start | bytes 98312 | tf_op jit(solution)/shard_map/ppermute | solution.py:478
  (16 other events, 59.8 us)
